TPU v7x, 512 devices: a whole 4x8x8 slice. The times are simulated.
512 devices in a mesh: replica: 32 (over z_hi, x, core), fsdp: 16 (over y, z_lo).
Axes of the slice: x: 4, y: 8, z: 8 (z_hi: 4, z_lo: 2; z = z_hi * 2 + z_lo), core: 2. Of those that a mesh axis runs over, the one named last changes fastest.
Arguments:
- tokens: bfloat16 [65536, 4096], P(('replica', 'fsdp')), may hold values from -6 to 6
- cotangent: bfloat16 [65536, 512], P(('replica', 'fsdp')), may hold values from -6 to 6
- weight: float32 [32, 4096, 512], P('replica', 'fsdp'), may hold values from -3 to 3
- moment: bfloat16 [32, 4096, 512], P('replica', 'fsdp'), may hold values from -1.5 to 1.5
- second: bfloat16 [32, 4096, 512], P('replica', 'fsdp'), may hold values from 0.25 to 1
- outer_params: bfloat16 [4096, 512], P('fsdp'), may hold values from -6 to 6
- momentum: bfloat16 [4096, 512], P('fsdp'), may hold values from -3 to 3
Outputs:
- projected: bfloat16 [65536, 512], P(('replica', 'fsdp'))
- input_grad: bfloat16 [65536, 4096], P(('replica', 'fsdp'))
- new_weight: float32 [32, 4096, 512], P('replica', 'fsdp')
- new_moment: bfloat16 [32, 4096, 512], P('replica', 'fsdp')
- new_second: bfloat16 [32, 4096, 512], P('replica', 'fsdp')
All inputs are finite; a program needn't handle non-finite values.
Results may differ from a plain program's by a relative error of at most 0.0049.
Values may be sent and summed in bfloat16 or wider, within the bound.
No kernel may reach another device: no remote copies, remote signals or barrier semaphores. Data moves between devices by JAX's collectives and lax.ppermute only.
A program may use at most 64 MiB of HBM per device.

v0:
```python
import math

import jax
import jax.numpy as jnp
from jax import lax
from jax.sharding import PartitionSpec as P


def body(tokens, cotangent, weight, moment, second, outer_params, momentum):
    model_width = tokens.shape[1]
    factor = 1.0 / math.sqrt(model_width)
    local_rows = weight[0]
    outer_wide = outer_params.astype(jnp.float32)
    pseudo_grad = outer_wide - local_rows
    replicas = lax.axis_size("replica")
    average = lax.psum(pseudo_grad, "replica") / replicas
    velocity = 0.9 * momentum.astype(jnp.float32) + average
    outer_new = outer_wide - 0.7 * (average + 0.9 * velocity)
    compute_rows = local_rows.astype(jnp.bfloat16)
    forward_sum = jnp.dot(
        tokens,
        lax.all_gather(compute_rows, "fsdp", axis=0, tiled=True),
        preferred_element_type=jnp.float32,
    )
    backward_sum = lax.dot_general(
        cotangent,
        lax.all_gather(compute_rows, "fsdp", axis=0, tiled=True),
        (((1,), (1,)), ((), ())),
        preferred_element_type=jnp.float32,
    )
    projected = (forward_sum * factor).astype(jnp.bfloat16)
    input_grad = (backward_sum * factor).astype(jnp.bfloat16)
    token_slab = lax.all_to_all(tokens, "fsdp", split_axis=1, concat_axis=0, tiled=True)
    grad_sum = lax.dot_general(
        token_slab,
        lax.all_gather(cotangent, "fsdp", axis=0, tiled=True),
        (((0,), (0,)), ((), ())),
        preferred_element_type=jnp.float32,
    )
    grad = grad_sum * factor
    first_new = 0.8 * moment[0].astype(jnp.float32) + 0.2 * grad
    second_new = 0.95 * second[0].astype(jnp.float32) + 0.05 * grad * grad
    inner = local_rows - 0.05 * (first_new / (jnp.sqrt(second_new) + 1e-08) + 0.1 * local_rows)
    merged = 0.5 * inner + 0.5 * outer_new
    return (
        projected,
        input_grad,
        merged[None],
        first_new.astype(jnp.bfloat16)[None],
        second_new.astype(jnp.bfloat16)[None],
    )


def solution(mesh):
    return jax.shard_map(
        body,
        mesh=mesh,
        in_specs=(
            P(("replica", "fsdp"), None),
            P(("replica", "fsdp"), None),
            P("replica", "fsdp", None),
            P("replica", "fsdp", None),
            P("replica", "fsdp", None),
            P("fsdp", None),
            P("fsdp", None),
        ),
        out_specs=(
            P(("replica", "fsdp"), None),
            P(("replica", "fsdp"), None),
            P("replica", "fsdp", None),
            P("replica", "fsdp", None),
            P("replica", "fsdp", None),
        ),
        check_vma=False,
    )
```

profile of v0, /device:TPU:1, one launch (start us, length us, event | category | flops | bytes accessed | tf_op | source)
XLA Modules:
  0.0 370.6 jit_solution(15986693048845438323)
XLA Ops:
  8.0 0.0 all-reduce.2.cloned.1.call-start
  8.0 2.0 convert_subtract_fusion.1
  10.0 0.0 all-reduce.2.cloned.1.call-update
  10.1 0.0 all-gather.5.cloned.1.call-start
  10.1 0.5 all-gather.5.cloned.1.call-update
  10.7 0.0 all-gather.3.cloned.1.call-start
  10.7 1.8 bitcast_convert_fusion
  12.5 0.0 all-gather.3.cloned.1.call-update
  12.5 1.6 copy.12
  14.1 41.1 %all_to_all.19 = bf16[128,16,256]{0,2,1:T(8,128)(2,1)S(1)} all-to-all(bf16[128,16,256]{0,2,1:T(8,128)(2,1)S(1)} %bitcast.43), channel_id=1, replica_groups=mesh['replica'=32,'fsdp'=16] {'fsdp'}, dimensions={1} | all-to-all | bytes 2097152 | tf_op jit(solution)/shard_map/all_to_all | solution.py:33
  55.3 0.5 copy.13
  55.8 0.0 copy-start.1
  55.8 297.1 %all-reduce.2.cloned.1.call-done = f32[256,512]{1,0:T(8,128)} async-done(((f32[256,512]{1,0:T(8,128)}), f32[256,512]{1,0:T(8,128)}) %all-reduce.2.cloned.1.call-update) | async-done | bytes 524304 | tf_op jit(solution)/shard_map/psum | solution.py:16
  353.0 0.0 copy-done.2
  353.0 0.0 copy-done.4
  353.0 0.0 copy-done.5
  353.0 0.0 copy-done.6
  353.0 4.0 %convert_bitcast_fusion = (bf16[1,256,512]{2,1,0:T(8,128)(2,1)}, f32[1,256,512]{2,1,0:T(8,128)}, bf16[1,256,512]{2,1,0:T(8,128)(2,1)}) fusion(bf16[1,256,512]{2,1,0:T(8,128)(2,1)S(1)} %copy-done.5, bf16[256,512]{1,0:T(8,128)(2,1)S(1)} %copy-done.6, f32[256,512]{1,0:T(8,128)} %all-reduce.2.cloned.1.call-done, bf16[256,512]{1,0:T(8,128)(2,1)S(1)} %copy-done.4, ...), kind=kOutput, calls=%fused_computation.18 | convolution fusion | flops 540672000 | bytes 6291456 | tf_op jit(solution)/shard_map/dot_general | solution.py:34
  357.0 0.0 copy-done.1
  357.0 0.0 copy-start
  357.0 3.7 %fusion.1 = bf16[128,512]{1,0:T(8,128)(2,1)} fusion(bf16[128,4096]{1,0:T(8,128)(2,1)S(1)} %copy-done.1, bf16[4096,512]{1,0:T(8,128)(2,1)} %all-gather.3.cloned.1.call-done), kind=kOutput, calls=%fused_computation.3 | convolution fusion | flops 537001984 | bytes 5373952 | tf_op jit(solution)/shard_map/dot_general | solution.py:20
  360.7 0.0 copy-done.3
  360.7 0.0 copy-done
  360.7 2.5 fusion
  (7 shorter events, 0.0 us)
Async XLA Ops:
  8.0 345.0 %all-reduce.2.cloned.1.call-start = ((), (), s32[]{:S(2)}) async-start(), calls=%async_computation.3 | async-start | bytes 1048576 | tf_op jit(solution)/shard_map/psum | solution.py:16
  10.0 342.9 %copy-start.2 = (f32[1,256,512]{2,1,0:T(8,128)S(1)}, f32[1,256,512]{2,1,0:T(8,128)}, u32[]{:S(2)}) copy-start(f32[1,256,512]{2,1,0:T(8,128)} %param.9) | copy-start | bytes 1572868
  10.0 342.9 %copy-start.4 = (bf16[256,512]{1,0:T(8,128)(2,1)S(1)}, bf16[256,512]{1,0:T(8,128)(2,1)}, u32[]{:S(2)}) copy-start(bf16[256,512]{1,0:T(8,128)(2,1)} %param.12) | copy-start | bytes 786436
  10.0 342.9 %copy-start.5 = (bf16[1,256,512]{2,1,0:T(8,128)(2,1)S(1)}, bf16[1,256,512]{2,1,0:T(8,128)(2,1)}, u32[]{:S(2)}) copy-start(bf16[1,256,512]{2,1,0:T(8,128)(2,1)} %param.11) | copy-start | bytes 786436
  10.0 342.9 %copy-start.6 = (bf16[256,512]{1,0:T(8,128)(2,1)S(1)}, bf16[256,512]{1,0:T(8,128)(2,1)}, u32[]{:S(2)}) copy-start(bf16[256,512]{1,0:T(8,128)(2,1)} %param.13) | copy-start | bytes 786436
  10.1 342.9 %all-gather.5.cloned.1.call-start = ((), (), s32[]{:S(2)}) async-start(), calls=%async_computation.2 | async-start | bytes 2228224 | tf_op jit(solution)/shard_map/all_gather | solution.py:36
  10.7 346.3 %all-gather.3.cloned.1.call-start = ((), (), s32[]{:S(2)}) async-start(), calls=%async_computation.1 | async-start | bytes 4456448 | tf_op jit(solution)/shard_map/all_gather | solution.py:22
  55.8 301.2 %copy-start.1 = (bf16[128,4096]{1,0:T(8,128)(2,1)S(1)}, bf16[128,4096]{1,0:T(8,128)(2,1)}, u32[]{:S(2)}) copy-start(bf16[128,4096]{1,0:T(8,128)(2,1)} %param.7) | copy-start | bytes 3145732
  356.9 3.7 %copy-start.3 = (bf16[128,512]{1,0:T(8,128)(2,1)S(1)}, bf16[128,512]{1,0:T(8,128)(2,1)}, u32[]{:S(2)}) copy-start(bf16[128,512]{1,0:T(8,128)(2,1)} %param.8) | copy-start | bytes 393220
  357.0 3.7 %copy-start = (bf16[4096,512]{1,0:T(8,128)(2,1)S(1)}, bf16[4096,512]{1,0:T(8,128)(2,1)}, u32[]{:S(2)}) copy-start(bf16[4096,512]{1,0:T(8,128)(2,1)} %all-gather.3.cloned.1.call-done) | copy-start | bytes 12582916
Sparse Core Ops, SparseCore 0:
  12.3 340.6 all-reduce.1
Sparse Core Ops, SparseCore 1:
  12.6 81.6 all-gather.4
  96.8 108.1 all-gather.2
where the time goes:
time: 371 us
  waiting for transfers between devices  298 us (80%)
  blocking collectives  41.1 us (11%)
  between operations  15.5 us (4%)
  matrix products  10.1 us (3%)
  other arithmetic  3.77 us (1%)
    psum x1, waiting for transfers between devices, body(): average = lax.psum(pseudo_grad, 'replica') / replicas  297 us
    all_to_all x1, blocking collectives, body(): lax.all_to_all(tokens, 'fsdp', split_axis=1, concat_axis=0, tiled=True)  41.1 us
  transfers between devices with their start and end apart: 3, of which 1 were waited for; matrix products, arithmetic and copies ran while one was open for 2% of the time, Pallas kernels for 0%

commit v1 on v0

v1 whole, which is shorter than its diff:
```python
import math

import jax
import jax.numpy as jnp
from jax import lax
from jax.sharding import Mesh, PartitionSpec as P

SIZES = (4, 4, 2, 8, 2)
NAMES = ("zh", "x", "core", "y", "zl")
REPLICA = ("zh", "x", "core")
FSDP = ("y", "zl")
PAIR = [(0, 1), (1, 0)]
BF16 = jnp.bfloat16
F32 = jnp.float32


def replica_mean(rows):
    replicas = lax.axis_size(REPLICA)
    parts = rows.reshape(replicas, -1, rows.shape[-1])
    mine = lax.all_to_all(parts, REPLICA, 0, 0, tiled=True)
    mean = (jnp.sum(mine.astype(F32), axis=0) / replicas).astype(BF16)
    out = lax.all_to_all(jnp.broadcast_to(mean[None], parts.shape), REPLICA, 0, 0, tiled=True)
    return out.reshape(rows.shape).astype(F32)


def body(tokens, cotangent, weight, moment, second, outer_params, momentum):
    n_tok, model_width = tokens.shape
    kv = cotangent.shape[1]
    factor = 1.0 / math.sqrt(model_width)
    ys = lax.axis_size("y")
    zl = lax.axis_index("zl")
    local_rows = weight[0]
    rows = local_rows.shape[0]
    half = ys * rows
    compute_rows = local_rows.astype(BF16)

    both = lax.all_gather(jnp.concatenate([compute_rows, cotangent], 0), "y", axis=0, tiled=False)
    w_half = both[:, :rows].reshape(half, kv)
    cot_y = both[:, rows:].reshape(ys * n_tok, kv)

    blocks = tokens.reshape(n_tok, ys, 2, rows)
    own = jnp.where(zl == 0, blocks[:, :, 0], blocks[:, :, 1]).reshape(n_tok, half)
    other = jnp.where(zl == 0, blocks[:, :, 1], blocks[:, :, 0]).reshape(n_tok, half)
    got = lax.ppermute(jnp.concatenate([other, cotangent], 1), "zl", PAIR)

    slab = lax.all_to_all(tokens, "y", split_axis=1, concat_axis=0, tiled=True)
    mean_rows = replica_mean(compute_rows)

    forward = jnp.dot(got[:, :half], w_half, preferred_element_type=F32)
    back = lax.dot_general(got[:, half:], w_half, (((1,), (1,)), ((), ())), preferred_element_type=F32)
    returned = lax.ppermute(
        jnp.concatenate([(back * factor).astype(BF16), (forward * factor).astype(BF16)], 1), "zl", PAIR
    )
    forward_own = jnp.dot(own, w_half, preferred_element_type=F32)
    back_own = lax.dot_general(cotangent, w_half, (((1,), (1,)), ((), ())), preferred_element_type=F32)

    partial = lax.dot_general(slab, cot_y, (((0,), (0,)), ((), ())), preferred_element_type=F32) * factor
    partial_own = jnp.where(zl == 0, partial[:rows], partial[rows:])
    partial_other = jnp.where(zl == 0, partial[rows:], partial[:rows]).astype(BF16)
    grad = partial_own + lax.ppermute(partial_other, "zl", PAIR).astype(F32)

    outer_wide = outer_params.astype(F32)
    average = outer_wide - mean_rows
    velocity = 0.9 * momentum.astype(F32) + average
    outer_new = outer_wide - 0.7 * (average + 0.9 * velocity)
    first_new = 0.8 * moment[0].astype(F32) + 0.2 * grad
    second_new = 0.95 * second[0].astype(F32) + 0.05 * grad * grad
    inner = local_rows - 0.05 * (first_new / (jnp.sqrt(second_new) + 1e-08) + 0.1 * local_rows)
    merged = 0.5 * inner + 0.5 * outer_new

    projected = (forward_own * factor + returned[:, half:].astype(F32)).astype(BF16)
    mine = (back_own * factor).astype(BF16).reshape(n_tok, ys, rows)
    theirs = returned[:, :half].reshape(n_tok, ys, rows)
    input_grad = jnp.where(
        zl == 0, jnp.stack([mine, theirs], 2), jnp.stack([theirs, mine], 2)
    ).reshape(n_tok, model_width)
    return (
        projected,
        input_grad,
        merged[None],
        first_new.astype(BF16)[None],
        second_new.astype(BF16)[None],
    )


def solution(mesh):
    fine = Mesh(mesh.devices.reshape(SIZES), NAMES)
    tok = P(NAMES, None)
    par = P(REPLICA, FSDP, None)
    outer = P(FSDP, None)
    return jax.shard_map(
        body,
        mesh=fine,
        in_specs=(tok, tok, par, par, par, outer, outer),
        out_specs=(tok, tok, par, par, par),
        check_vma=False,
    )
```

time: 371 us -> 135 us (0.36)
  waiting for transfers between devices: 298 us -> 29.5 us
  local copies, waits for them, and re-layouts: 2.17 us -> 25.7 us
  starting transfers between devices: 0.12 us -> 18.4 us
  blocking collectives: 41.1 us -> 27.9 us
  other arithmetic: 3.77 us -> 8.34 us
    psum x1 -> x0, waiting for transfers between devices: 297 us -> none  [body(): average = lax.psum(pseudo_grad, 'replica') / replicas]
    ppermute x0 -> x3, waiting for transfers between devices: none -> 15.4 us  [the longest x1 9.47 us: body(): grad = partial_own + lax.ppermute(partial_other, 'zl', PAIR).astype(F32)]
    all_to_all x0 -> x2, waiting for transfers between devices: none -> 14.1 us  [the longest x1 11.1 us: replica_mean(): lax.all_to_all(jnp.broadcast_to(mean[None], parts.shape), REPLICA, 0, 0,...]
    all_to_all x1, blocking collectives: 41.1 us -> 27.9 us  [replica_mean(): mine = lax.all_to_all(parts, REPLICA, 0, 0, tiled=True)]
    all_to_all x0 -> x2, starting transfers between devices: none -> 10.5 us  [the longest x1 6.82 us: body(): slab = lax.all_to_all(tokens, 'y', split_axis=1, concat_axis=0, tiled=True)]
    unnamed x15 -> x33, local copies, waits for them, and re-layouts: 1.65 us -> 10.4 us
    ppermute x0 -> x3, starting transfers between devices: none -> 7.89 us  [the longest x1 2.74 us: body(): got = lax.ppermute(jnp.concatenate([other, cotangent], 1), 'zl', PAIR)]
    all_gather x0 -> x1, local copies, waits for them, and re-layouts: none -> 4.65 us  [body(): lax.all_gather(jnp.concatenate([compute_rows, cotangent], 0), 'y', axis=0...]
  transfers between devices with their start and end apart: 3 -> 6, of which waited for: 1 -> 4; matrix products, arithmetic and copies ran while one was open for 2% -> 25% of each run, Pallas kernels for 0% -> 0%
where the time goes in v1:
time: 135 us; the launch traced here: 134 us
  waiting for transfers between devices  29.5 us (22%)
  blocking collectives  27.9 us (21%)
  local copies, waits for them, and re-layouts  25.7 us (19%)
  starting transfers between devices  18.4 us (14%)
  between operations  14.3 us (11%)
  matrix products  9.75 us (7%)
  other arithmetic  8.34 us (6%)
    all_to_all x1, blocking collectives, replica_mean(): mine = lax.all_to_all(parts, REPLICA, 0, 0, tiled=True)  27.9 us
    all_to_all x1, waiting for transfers between devices, replica_mean(): lax.all_to_all(jnp.broadcast_to(mean[None], parts.shape), REPLICA, 0, 0,...  11.1 us
    unnamed x33, local copies, waits for them, and re-layouts  10.4 us
    ppermute x1, waiting for transfers between devices, body(): grad = partial_own + lax.ppermute(partial_other, 'zl', PAIR).astype(F32)  9.47 us
    all_to_all x1, starting transfers between devices, body(): slab = lax.all_to_all(tokens, 'y', split_axis=1, concat_axis=0, tiled=True)  6.82 us
    ppermute x1, waiting for transfers between devices, body(): got = lax.ppermute(jnp.concatenate([other, cotangent], 1), 'zl', PAIR)  5.94 us
    all_gather x1, local copies, waits for them, and re-layouts, body(): lax.all_gather(jnp.concatenate([compute_rows, cotangent], 0), 'y', axis=0...  4.65 us
    all_to_all x1, starting transfers between devices, replica_mean(): lax.all_to_all(jnp.broadcast_to(mean[None], parts.shape), REPLICA, 0, 0,...  3.66 us
  transfers between devices with their start and end apart: 6, of which 4 were waited for; matrix products, arithmetic and copies ran while one was open for 25% of the time, Pallas kernels for 0%

profile of v1, /device:TPU:1, one launch (start us, length us, event | category | flops | bytes accessed | tf_op | source)
XLA Modules:
  0.0 133.9 jit_solution(6454438115814124410)
XLA Ops:
  10.5 27.9 %all_to_all.26 = bf16[32,8,512]{2,1,0:T(8,128)(2,1)S(1)} all-to-all(bf16[32,8,512]{2,1,0:T(8,128)(2,1)S(1)} %convert_bitcast_fusion), channel_id=1, replica_groups=mesh['zh'=4,'x'=4,'core'=2,'y'=8,'zl'=2] {'zh','x','core'}, dimensions={0} | all-to-all | bytes 524288 | tf_op jit(solution)/shard_map/all_to_all | solution.py:20
  39.2 3.7 %all-to-all-start.2 = ((bf16[32,8,512]{2,1,0:T(8,128)(2,1)}), bf16[32,8,512]{2,1,0:T(8,128)(2,1)S(1)}, u32[]{:S(2)}, u32[]{:S(2)}) async-start(bf16[32,8,512]{2,1,0:T(8,128)(2,1)} %broadcast_in_dim.15), calls=%async_computation.2 | async-start | bytes 524288 | tf_op jit(solution)/shard_map/all_to_all | solution.py:22
  44.9 11.1 %all-to-all-done.2 = bf16[32,8,512]{2,1,0:T(8,128)(2,1)S(1)} async-done(((bf16[32,8,512]{2,1,0:T(8,128)(2,1)}), bf16[32,8,512]{2,1,0:T(8,128)(2,1)S(1)}, u32[]{:S(2)}, u32[]{:S(2)}) %all-to-all-start.2) | async-done | bytes 262176 | tf_op jit(solution)/shard_map/all_to_all | solution.py:22
  56.0 6.8 %all-to-all-start = ((bf16[128,8,512]{2,0,1:T(8,128)(2,1)}), bf16[128,8,512]{2,0,1:T(8,128)(2,1)}, u32[]{:S(2)}, u32[]{:S(2)}) async-start(bf16[128,8,512]{2,0,1:T(8,128)(2,1)} %copy.58), calls=%async_computation | async-start | bytes 2097152 | tf_op jit(solution)/shard_map/all_to_all | solution.py:46
  63.7 2.7 %collective-permute-start = (bf16[128,2560]{0,1:T(8,128)(2,1)}, bf16[128,2560]{0,1:T(8,128)(2,1)}, u32[]{:S(2)}, u32[]{:S(2)}) collective-permute-start(bf16[128,2560]{0,1:T(8,128)(2,1)} %pad_maximum_fusion), channel_id=1, source_target_pairs={{0,1},{1,0},{2,3},{3,2},{4,5},{5,4},{6,7},{7,6},{8,9},{9,8},{10,11... | collective-permute-start | bytes 1966088 | tf_op jit(solution)/shard_map/ppermute | solution.py:44
  70.2 4.7 %copy.50 = bf16[3072,512]{1,0:T(8,128)(2,1)} copy(bf16[3072,512]{0,1:T(8,128)(2,1)} %all-gather.3.cloned.1.call-done) | data formatting | bytes 6291456 | tf_op jit(solution)/shard_map/all_gather | solution.py:37
  74.9 1.8 %slice.46 = bf16[8,256,512]{2,1,0:T(8,128)(2,1)S(1)} slice(bf16[8,384,512]{2,1,0:T(8,128)(2,1)} %bitcast.83), slice={[0:8], [0:256], [0:512]} | slice | bytes 4194304 | tf_op jit(solution)/shard_map/slice | solution.py:38
  76.7 5.9 %collective-permute-done = bf16[128,2560]{0,1:T(8,128)(2,1)} collective-permute-done((bf16[128,2560]{0,1:T(8,128)(2,1)}, bf16[128,2560]{0,1:T(8,128)(2,1)}, u32[]{:S(2)}, u32[]{:S(2)}) %collective-permute-start) | collective-permute-done | bytes 655392 | tf_op jit(solution)/shard_map/ppermute | solution.py:44
  82.6 1.5 %fusion.5 = bf16[128,512]{1,0:T(8,128)(2,1)S(1)} fusion(bf16[2048,512]{1,0:T(8,128)(2,1)S(1)} %bitcast.77, bf16[128,2560]{0,1:T(8,128)(2,1)} %collective-permute-done), kind=kOutput, calls=%fused_computation.10 | convolution fusion | flops 268566528 | bytes 2752512 | tf_op jit(solution)/shard_map/dot_general | solution.py:49
  84.2 1.7 %fusion = bf16[128,2048]{1,0:T(8,128)(2,1)S(1)} fusion(bf16[2048,512]{1,0:T(8,128)(2,1)S(1)} %bitcast.78, bf16[128,2560]{0,1:T(8,128)(2,1)} %collective-permute-done), kind=kOutput, calls=%fused_computation.2 | convolution fusion | flops 268959744 | bytes 2752512 | tf_op jit(solution)/shard_map/dot_general | solution.py:50
  86.8 2.5 %collective-permute-start.1 = (bf16[128,2560]{1,0:T(8,128)(2,1)}, bf16[128,2560]{1,0:T(8,128)(2,1)}, u32[]{:S(2)}, u32[]{:S(2)}) collective-permute-start(bf16[128,2560]{1,0:T(8,128)(2,1)} %pad_maximum_fusion.1), channel_id=1, source_target_pairs={{0,1},{1,0},{2,3},{3,2},{4,5},{5,4},{6,7},{7,6},{8,9},{9,8},{10,11... | collective-permute-start | bytes 1966088 | tf_op jit(solution)/shard_map/ppermute | solution.py:51
  89.3 3.0 %all-to-all-done = bf16[128,8,512]{2,0,1:T(8,128)(2,1)} async-done(((bf16[128,8,512]{2,0,1:T(8,128)(2,1)}), bf16[128,8,512]{2,0,1:T(8,128)(2,1)}, u32[]{:S(2)}, u32[]{:S(2)}) %all-to-all-start) | async-done | bytes 1048608 | tf_op jit(solution)/shard_map/all_to_all | solution.py:46
  92.4 2.3 %fusion.3 = f32[512,512]{0,1:T(8,128)S(1)} fusion(bf16[8,384,512]{2,1,0:T(8,128)(2,1)} %bitcast.84, bf16[128,8,512]{2,0,1:T(8,128)(2,1)} %all-to-all-done), kind=kOutput, calls=%fused_computation.6 | convolution fusion | flops 537133056 | bytes 3145728 | tf_op jit(solution)/shard_map/dot_general | solution.py:57
  95.5 2.6 %collective-permute-start.2 = (bf16[256,512]{0,1:T(8,128)(2,1)}, bf16[256,512]{0,1:T(8,128)(2,1)}, u32[]{:S(2)}, u32[]{:S(2)}) collective-permute-start(bf16[256,512]{0,1:T(8,128)(2,1)} %select_convert_fusion), channel_id=1, source_target_pairs={{0,1},{1,0},{2,3},{3,2},{4,5},{5,4},{6,7},{7,6},{8,9},{9,8},{10,11... | collective-permute-start | bytes 786440 | tf_op jit(solution)/shard_map/ppermute | solution.py:60
  98.1 1.5 %fusion.1 = bf16[2048,128]{1,0:T(8,128)(2,1)} fusion(bf16[2048,512]{1,0:T(8,128)(2,1)S(1)} %bitcast.79, bf16[128,512]{1,0:T(8,128)(2,1)S(1)} %copy-done.6), kind=kOutput, calls=%fused_computation.3 | convolution fusion | flops 268959744 | bytes 2752512 | tf_op jit(solution)/shard_map/dot_general | solution.py:55
  99.6 1.5 %copy.53 = bf16[128,8,1,256]{3,1,0,2:T(8,128)(2,1)S(1)} copy(bf16[128,8,1,256]{0,3,1,2:T(8,128)(2,1)} %bitcast.89) | data formatting | bytes 1048576 | tf_op jit(solution)/shard_map/stack;reshape | solution.py:75
  101.1 9.5 %collective-permute-done.2 = bf16[256,512]{0,1:T(8,128)(2,1)} collective-permute-done((bf16[256,512]{0,1:T(8,128)(2,1)}, bf16[256,512]{0,1:T(8,128)(2,1)}, u32[]{:S(2)}, u32[]{:S(2)}) %collective-permute-start.2) | collective-permute-done | bytes 262176 | tf_op jit(solution)/shard_map/ppermute | solution.py:60
  110.6 2.1 %fusion.22 = (bf16[1,256,512]{1,2,0:T(8,128)(2,1)}, f32[256,512]{0,1:T(8,128)S(1)}) fusion(bf16[1,256,512]{1,2,0:T(8,128)(2,1)S(1)} %copy.60, bf16[256,512]{0,1:T(8,128)(2,1)} %collective-permute-done.2, f32[512,512]{0,1:T(8,128)} %copy-done.2, pred[]{:T(512)S(6)} %eq.2), kind=kLoop, calls=%fused_computation.42 | loop fusion | flops 1179648 | bytes 2359297 | tf_op jit(solution)/shard_map/broadcast_in_dim | solution.py:82
  112.7 2.4 %fusion.23 = (bf16[1,256,512]{1,2,0:T(8,128)(2,1)}, f32[1,256,512]{1,2,0:T(8,128)S(1)}) fusion(f32[256,512]{0,1:T(8,128)S(1)} %get-tuple-element.21, bf16[1,256,512]{1,2,0:T(8,128)(2,1)} %copy.56, bf16[256,512]{0,1:T(8,128)(2,1)} %copy.63, f32[256,512]{0,1:T(8,128)S(1)} %copy-done.4, bf16[256,512]{0,1:T(8,128)(2,1)} %copy.61, ...), kind=kLoop, calls=%fused_computation.43 | loop fusion | flops 3538944 | bytes 3407872 | tf_op jit(solution)/shard_map/broadcast_in_dim | solution.py:81
  116.1 1.8 %copy.65 = bf16[1,256,512]{2,1,0:T(8,128)(2,1)} copy(bf16[1,256,512]{1,2,0:T(8,128)(2,1)} %get-tuple-element.22) | data formatting | bytes 524288
  117.9 1.8 %copy.66 = bf16[1,256,512]{2,1,0:T(8,128)(2,1)} copy(bf16[1,256,512]{1,2,0:T(8,128)(2,1)} %get-tuple-element.20) | data formatting | bytes 524288
  121.1 1.6 %copy.55 = bf16[128,8,2,256]{3,2,1,0:T(2,128)(2,1)S(1)} copy(bf16[128,8,2,256]{3,1,0,2:T(8,128)(2,1)S(1)} %maximum_select_fusion) | data formatting | bytes 2097152 | tf_op jit(solution)/shard_map/jit(_where)/select_n | solution.py:74
  122.7 1.6 %select_n.50 = bf16[128,4096]{1,0:T(8,128)(2,1)} reshape(bf16[128,8,2,256]{3,2,1,0:T(2,128)(2,1)S(1)} %copy.55) | data formatting | bytes 2097152 | tf_op jit(solution)/shard_map/jit(_where)/select_n | solution.py:74
  124.3 2.7 %add_convert_fusion = bf16[128,512]{1,0:T(8,128)(2,1)} fusion(bf16[128,2560]{1,0:T(8,128)(2,1)} %collective-permute-done.1, pred[]{:T(512)S(6)} %eq.2, bf16[128,8,2,256]{0,3,2,1:T(8,128)(2,1)S(1)} %bitcast.82, bf16[8,384,512]{2,1,0:T(8,128)(2,1)} %bitcast.85), kind=kOutput, calls=%fused_computation.46 | convolution fusion | flops 268959744 | bytes 3407873 | tf_op jit(solution)/shard_map/dot_general | solution.py:54
  (50 shorter events, 14.7 us)
Async XLA Ops:
  7.2 3.3 %copy-start.3 = (f32[1,256,512]{2,1,0:T(8,128)S(1)}, f32[1,256,512]{2,1,0:T(8,128)}, u32[]{:S(2)}) copy-start(f32[1,256,512]{2,1,0:T(8,128)} %param.9) | copy-start | bytes 1572868
  7.2 63.1 %all-gather.3.cloned.1.call-start = ((), (), s32[]{:S(2)}) async-start(), calls=%async_computation.3 | async-start | bytes 3538944 | tf_op jit(solution)/shard_map/all_gather | solution.py:37
  9.5 29.6 %copy-start = (f32[1,256,512]{1,2,0:T(8,128)}, f32[1,256,512]{1,2,0:T(8,128)S(1)}, u32[]{:S(2)}) copy-start(f32[1,256,512]{1,2,0:T(8,128)S(1)} %copy.48) | copy-start | bytes 1572868
  9.6 33.3 %copy-start.5 = (bf16[128,4096]{1,0:T(8,128)(2,1)S(1)}, bf16[128,4096]{1,0:T(8,128)(2,1)}, u32[]{:S(2)}) copy-start(bf16[128,4096]{1,0:T(8,128)(2,1)} %param.7) | copy-start | bytes 3145732
  39.2 16.8 %all-to-all-start.2 = ((bf16[32,8,512]{2,1,0:T(8,128)(2,1)}), bf16[32,8,512]{2,1,0:T(8,128)(2,1)S(1)}, u32[]{:S(2)}, u32[]{:S(2)}) async-start(bf16[32,8,512]{2,1,0:T(8,128)(2,1)} %broadcast_in_dim.15), calls=%async_computation.2 | async-start | bytes 524288 | tf_op jit(solution)/shard_map/all_to_all | solution.py:22
  44.9 21.6 %copy-start.7 = (bf16[1,256,512]{2,1,0:T(8,128)(2,1)S(1)}, bf16[1,256,512]{2,1,0:T(8,128)(2,1)}, u32[]{:S(2)}) copy-start(bf16[1,256,512]{2,1,0:T(8,128)(2,1)} %param.11) | copy-start | bytes 786436
  44.9 21.7 %copy-start.8 = (bf16[1,256,512]{2,1,0:T(8,128)(2,1)S(1)}, bf16[1,256,512]{2,1,0:T(8,128)(2,1)}, u32[]{:S(2)}) copy-start(bf16[1,256,512]{2,1,0:T(8,128)(2,1)} %param.10) | copy-start | bytes 786436
  44.9 22.6 %copy-start.9 = (bf16[256,512]{1,0:T(8,128)(2,1)S(1)}, bf16[256,512]{1,0:T(8,128)(2,1)}, u32[]{:S(2)}) copy-start(bf16[256,512]{1,0:T(8,128)(2,1)} %param.13) | copy-start | bytes 786436
  44.9 23.4 %copy-start.10 = (bf16[256,512]{1,0:T(8,128)(2,1)S(1)}, bf16[256,512]{1,0:T(8,128)(2,1)}, u32[]{:S(2)}) copy-start(bf16[256,512]{1,0:T(8,128)(2,1)} %param.12) | copy-start | bytes 786436
  56.0 36.3 %all-to-all-start = ((bf16[128,8,512]{2,0,1:T(8,128)(2,1)}), bf16[128,8,512]{2,0,1:T(8,128)(2,1)}, u32[]{:S(2)}, u32[]{:S(2)}) async-start(bf16[128,8,512]{2,0,1:T(8,128)(2,1)} %copy.58), calls=%async_computation | async-start | bytes 2097152 | tf_op jit(solution)/shard_map/all_to_all | solution.py:46
  63.7 18.9 %collective-permute-start = (bf16[128,2560]{0,1:T(8,128)(2,1)}, bf16[128,2560]{0,1:T(8,128)(2,1)}, u32[]{:S(2)}, u32[]{:S(2)}) collective-permute-start(bf16[128,2560]{0,1:T(8,128)(2,1)} %pad_maximum_fusion), channel_id=1, source_target_pairs={{0,1},{1,0},{2,3},{3,2},{4,5},{5,4},{6,7},{7,6},{8,9},{9,8},{10,11... | collective-permute-start | bytes 1966088 | tf_op jit(solution)/shard_map/ppermute | solution.py:44
  86.8 11.3 %copy-start.6 = (bf16[128,512]{1,0:T(8,128)(2,1)S(1)}, bf16[128,512]{1,0:T(8,128)(2,1)}, u32[]{:S(2)}) copy-start(bf16[128,512]{1,0:T(8,128)(2,1)} %param.8) | copy-start | bytes 393220
  86.8 32.9 %collective-permute-start.1 = (bf16[128,2560]{1,0:T(8,128)(2,1)}, bf16[128,2560]{1,0:T(8,128)(2,1)}, u32[]{:S(2)}, u32[]{:S(2)}) collective-permute-start(bf16[128,2560]{1,0:T(8,128)(2,1)} %pad_maximum_fusion.1), channel_id=1, source_target_pairs={{0,1},{1,0},{2,3},{3,2},{4,5},{5,4},{6,7},{7,6},{8,9},{9,8},{10,11... | collective-permute-start | bytes 1966088 | tf_op jit(solution)/shard_map/ppermute | solution.py:51
  94.6 5.0 %copy-start.2 = (f32[512,512]{0,1:T(8,128)}, f32[512,512]{0,1:T(8,128)S(1)}, u32[]{:S(2)}) copy-start(f32[512,512]{0,1:T(8,128)S(1)} %fusion.3) | copy-start | bytes 3145732
  95.5 15.1 %collective-permute-start.2 = (bf16[256,512]{0,1:T(8,128)(2,1)}, bf16[256,512]{0,1:T(8,128)(2,1)}, u32[]{:S(2)}, u32[]{:S(2)}) collective-permute-start(bf16[256,512]{0,1:T(8,128)(2,1)} %select_convert_fusion), channel_id=1, source_target_pairs={{0,1},{1,0},{2,3},{3,2},{4,5},{5,4},{6,7},{7,6},{8,9},{9,8},{10,11... | collective-permute-start | bytes 786440 | tf_op jit(solution)/shard_map/ppermute | solution.py:60
  99.6 13.1 %copy-start.1 = (f32[1,256,512]{1,2,0:T(8,128)S(1)}, f32[1,256,512]{1,2,0:T(8,128)}, u32[]{:S(2)}) copy-start(f32[1,256,512]{1,2,0:T(8,128)} %copy-done) | copy-start | bytes 1572868
  99.6 13.1 %copy-start.4 = (f32[256,512]{0,1:T(8,128)S(1)}, f32[256,512]{0,1:T(8,128)}, u32[]{:S(2)}) copy-start(f32[256,512]{0,1:T(8,128)} %copy.62) | copy-start | bytes 1572868
Sparse Core Ops, SparseCore 0:
  10.7 51.9 all-gather.2

commit v2 on v1

v2 whole, which is shorter than its diff:
```python
import functools
import math

import jax
import jax.numpy as jnp
from jax import lax
from jax.experimental import pallas as pl
from jax.experimental.pallas import tpu as pltpu
from jax.sharding import Mesh, PartitionSpec as P

SIZES = (4, 4, 2, 8, 2)
NAMES = ("zh", "x", "core", "y", "zl")
REPLICA = ("zh", "x", "core")
FSDP = ("y", "zl")
PAIR = [(0, 1), (1, 0)]
BF16 = jnp.bfloat16
F32 = jnp.float32
YS = 8
ROWS = 256
TOK = 128
KV = 512
MIB = 1 << 20


def shift(k):
    return [(i, (i + k) % YS) for i in range(YS)]


def whole(shape):
    return pl.BlockSpec(shape, lambda i, s: (0,) * len(shape))


TOP = pl.BlockSpec((ROWS, KV), lambda i, s: (0, 0))
LOW = pl.BlockSpec((ROWS, KV), lambda i, s: (1, 0))


def call(kernel, place, args, in_specs, outs, flops, scratch=()):
    size = sum(math.prod(a.shape) * a.dtype.itemsize for a in args)
    size += sum(math.prod(o.shape) * o.dtype.itemsize for o in outs)
    return pl.pallas_call(
        kernel,
        out_shape=outs,
        grid_spec=pltpu.PrefetchScalarGridSpec(
            num_scalar_prefetch=1,
            grid=(1,),
            in_specs=in_specs,
            out_specs=[whole(o.shape) for o in outs],
            scratch_shapes=scratch,
        ),
        compiler_params=pltpu.CompilerParams(vmem_limit_bytes=40 * MIB),
        cost_estimate=pl.CostEstimate(flops=flops, bytes_accessed=size, transcendentals=0),
    )(place, *args)


def lanes(index):
    return pl.ds(pl.multiple_of(index * ROWS, ROWS), ROWS)


def split_kernel(place, tok, blocks, other):
    zl = place[1]
    for f in range(2 * YS):
        blocks[f] = tok[:, f * ROWS : (f + 1) * ROWS]
    for f in range(YS):
        other[:, f * ROWS : (f + 1) * ROWS] = tok[:, lanes(2 * f + 1 - zl)]


def block_products(place, k, factor, tok, got, cots, w):
    f = lax.rem(place[0] + k + YS, YS)
    x = jnp.concatenate([tok[:, lanes(2 * f + place[1])], got[:, lanes(f)]], 0)
    ahead = jnp.dot(x, w, preferred_element_type=F32)
    back = lax.dot_general(cots, w, (((1,), (1,)), ((), ())), preferred_element_type=F32)
    return ahead, (back * factor).astype(BF16)


def near_kernel(ks, factor, place, tok, got, cot, cot_got, *refs):
    w_refs, (back_own, back_got, ahead) = refs[: len(ks)], refs[len(ks) :]
    cots = jnp.concatenate([cot[...], cot_got[...]], 0)
    for i, k in enumerate(ks):
        a, b = block_products(place, k, factor, tok, got, cots, w_refs[i][...])
        back_own[:, i * ROWS : (i + 1) * ROWS] = b[:TOK]
        back_got[:, i * ROWS : (i + 1) * ROWS] = b[TOK:]
        ahead[...] = a if i == 0 else ahead[...] + a


def far_kernel(k, factor, place, tok, got, cot, cot_got, w, ahead, ahead_own, back_own, back):
    cots = jnp.concatenate([cot[...], cot_got[...]], 0)
    a, b = block_products(place, k, factor, tok, got, cots, w[...])
    total = (ahead[...] + a) * factor
    ahead_own[...] = total[:TOK]
    back_own[...] = b[:TOK]
    back[:, :ROWS] = b[TOK:]
    back[:, ROWS:] = total[TOK:].astype(BF16)


def join_kernel(ks, place, own_near, got_near, own_far, far, ahead_own, projected, input_grad):
    zl = place[1]
    for i, k in enumerate(ks):
        f = lax.rem(place[0] + k + YS, YS)
        near = i < len(ks) - 1
        cols = slice(i * ROWS, (i + 1) * ROWS)
        input_grad[:, lanes(2 * f + zl)] = own_near[:, cols] if near else own_far[...]
        input_grad[:, lanes(2 * f + 1 - zl)] = got_near[:, cols] if near else far[:, :ROWS]
    projected[...] = (ahead_own[...] + far[:, ROWS:].astype(F32)).astype(BF16)


def step_kernel(ks, factor, place, slab, weight, moment, second, outer, momentum, mean, *refs):
    c_refs, (new_weight, new_moment, new_second) = refs[: len(ks)], refs[len(ks) :]
    total = None
    for i, k in enumerate(ks):
        f = lax.rem(place[0] + k + YS, YS)
        x = slab[pl.ds(2 * f, 2)].reshape(2 * TOK, ROWS)
        part = lax.dot_general(x, c_refs[i][...], (((0,), (0,)), ((), ())), preferred_element_type=F32)
        total = part if i == 0 else total + part
    grad = total * factor
    local = weight[...]
    outer_wide = outer[...].astype(F32)
    average = outer_wide - mean[...].astype(F32)
    velocity = 0.9 * momentum[...].astype(F32) + average
    outer_new = outer_wide - 0.7 * (average + 0.9 * velocity)
    first_new = 0.8 * moment[...].astype(F32) + 0.2 * grad
    second_new = 0.95 * second[...].astype(F32) + 0.05 * grad * grad
    inner = local - 0.05 * (first_new / (jnp.sqrt(second_new) + 1e-08) + 0.1 * local)
    new_weight[...] = 0.5 * inner + 0.5 * outer_new
    new_moment[...] = first_new.astype(BF16)
    new_second[...] = second_new.astype(BF16)


def replica_mean(rows):
    replicas = lax.axis_size(REPLICA)
    parts = rows.reshape(replicas, -1, rows.shape[-1])
    mine = lax.all_to_all(parts, REPLICA, 0, 0, tiled=True)
    mean = (jnp.sum(mine.astype(F32), axis=0) / replicas).astype(BF16)
    out = lax.all_to_all(jnp.broadcast_to(mean[None], parts.shape), REPLICA, 0, 0, tiled=True)
    return out.reshape(rows.shape)


def body(tokens, cotangent, weight, moment, second, outer_params, momentum):
    factor = 1.0 / math.sqrt(tokens.shape[1])
    zl = lax.axis_index("zl")
    place = jnp.stack([lax.axis_index("y"), zl]).astype(jnp.int32)
    sds = jax.ShapeDtypeStruct
    compute_rows = weight[0].astype(BF16)

    cot_got = lax.ppermute(cotangent, "zl", PAIR)
    blocks, other = call(
        split_kernel, place, [tokens], [whole(tokens.shape)],
        [sds((2 * YS, TOK, ROWS), BF16), sds((TOK, YS * ROWS), BF16)], 0,
    )
    first = jnp.where(zl == 0, cotangent, cot_got)
    last = jnp.where(zl == 0, cot_got, cotangent)
    home = jnp.concatenate([compute_rows, first, last], 0)

    up, down = [home], [home]
    for _ in range(3):
        up.append(lax.ppermute(up[-1], "y", shift(1)))
        down.append(lax.ppermute(down[-1], "y", shift(-1)))
    far_w = lax.ppermute(up[3][:ROWS], "y", shift(1))
    far_c = lax.ppermute(down[3][ROWS:], "y", shift(-1))

    got = lax.ppermute(other, "zl", PAIR)
    blocks, _ = lax.optimization_barrier((blocks, up[1]))
    slab = lax.all_to_all(blocks, FSDP, 0, 0, tiled=True)
    mean_rows = replica_mean(compute_rows)

    ks = (0, -1, 1, -2, 2, -3, 3)
    near = [home, up[1], down[1], up[2], down[2], up[3], down[3]]
    flops = 4 * 2 * TOK * ROWS * KV
    common = [tokens, got, cotangent, cot_got]
    common_specs = [whole(a.shape) for a in common]
    back_own, back_got, ahead = call(
        functools.partial(near_kernel, ks, factor), place, common + near, common_specs + [TOP] * 7,
        [sds((TOK, 7 * ROWS), BF16), sds((TOK, 7 * ROWS), BF16), sds((2 * TOK, KV), F32)], 7 * flops,
    )
    near_back = lax.ppermute(back_got, "zl", PAIR)
    ahead_own, far_own, far_got = call(
        functools.partial(far_kernel, 4, factor), place, common + [far_w, ahead],
        common_specs + [whole(far_w.shape), whole(ahead.shape)],
        [sds((TOK, KV), F32), sds((TOK, ROWS), BF16), sds((TOK, ROWS + KV), BF16)], flops,
    )
    far_back = lax.ppermute(far_got, "zl", PAIR)

    states = [slab, weight[0], moment[0], second[0], outer_params, momentum, mean_rows]
    new_weight, new_moment, new_second = call(
        functools.partial(step_kernel, ks + (4,), factor), place, states + near + [far_c],
        [whole(a.shape) for a in states] + [LOW] * 7 + [whole(far_c.shape)],
        [sds((ROWS, KV), F32), sds((ROWS, KV), BF16), sds((ROWS, KV), BF16)], 8 * flops // 2,
    )
    parts = [back_own, near_back, far_own, far_back, ahead_own]
    projected, input_grad = call(
        functools.partial(join_kernel, ks + (4,)), place, parts, [whole(a.shape) for a in parts],
        [sds((TOK, KV), BF16), sds(tokens.shape, BF16)], 0,
    )
    return projected, input_grad, new_weight[None], new_moment[None], new_second[None]


def solution(mesh):
    fine = Mesh(mesh.devices.reshape(SIZES), NAMES)
    tok = P(NAMES, None)
    par = P(REPLICA, FSDP, None)
    outer = P(FSDP, None)
    return jax.shard_map(
        body,
        mesh=fine,
        in_specs=(tok, tok, par, par, par, outer, outer),
        out_specs=(tok, tok, par, par, par),
        check_vma=False,
    )
```

time: 135 us -> 156 us (1.16)
  the two profiles are of different devices: /device:TPU:1 before, /device:TPU:24 now
where the time goes in v2:
time: 156 us; the launch traced here: 155 us
  starting transfers between devices  68.6 us (44%)
  waiting for transfers between devices  61.8 us (40%)
  local copies, waits for them, and re-layouts  11.8 us (8%)
  Pallas kernels  9.6 us (6%)
  other arithmetic  2.26 us (1%)
    ppermute x3, waiting for transfers between devices, body(): up.append(lax.ppermute(up[-1], 'y', shift(1)))  34.8 us
    ppermute x3, starting transfers between devices, body(): up.append(lax.ppermute(up[-1], 'y', shift(1)))  14 us
    all_to_all x1, starting transfers between devices, replica_mean(): mine = lax.all_to_all(parts, REPLICA, 0, 0, tiled=True)  13.3 us
    unnamed x44, local copies, waits for them, and re-layouts  11.1 us
    pallas_call x5, Pallas kernels, call(): pl.pallas_call(kernel, out_shape=outs, grid_spec=pltpu.PrefetchScalarGrid...  9.6 us
    all_to_all x1, starting transfers between devices, replica_mean(): lax.all_to_all(jnp.broadcast_to(mean[None], parts.shape), REPLICA, 0, 0,...  8.77 us
    ppermute x1, waiting for transfers between devices, body(): far_back = lax.ppermute(far_got, 'zl', PAIR)  8.42 us
    all_to_all x1, waiting for transfers between devices, replica_mean(): lax.all_to_all(jnp.broadcast_to(mean[None], parts.shape), REPLICA, 0, 0,...  8.04 us
  transfers between devices with their start and end apart: 15, of which 6 were waited for; matrix products, arithmetic and copies ran while one was open for 1% of the time, Pallas kernels for 4%

profile of v2, /device:TPU:24, one launch (start us, length us, event | category | flops | bytes accessed | tf_op | source)
XLA Modules:
  0.0 155.0 jit_solution(4938015146555958958)
XLA Ops:
  0.6 2.1 %convert_bitcast_fusion = (bf16[32,8,512]{2,1,0:T(8,128)(2,1)}, bf16[256,512]{1,0:T(8,128)(2,1)S(1)}) fusion(f32[1,256,512]{2,1,0:T(8,128)} %param.9), kind=kLoop, calls=%fused_computation.2 | loop fusion | flops 262144 | bytes 1048576 | tf_op jit(solution)/shard_map/convert_element_type | solution.py:142
  2.7 13.3 %all-to-all-start.1 = ((bf16[32,8,512]{2,1,0:T(8,128)(2,1)}), bf16[32,8,512]{2,1,0:T(8,128)(2,1)S(1)}, u32[]{:S(2)}, u32[]{:S(2)}) async-start(bf16[32,8,512]{2,1,0:T(8,128)(2,1)} %get-tuple-element.33), calls=%async_computation.1 | async-start | bytes 524288 | tf_op jit(solution)/shard_map/all_to_all | solution.py:131
  16.0 3.4 %collective-permute-start.1 = (bf16[128,512]{1,0:T(8,128)(2,1)S(1)}, bf16[128,512]{1,0:T(8,128)(2,1)S(1)}, u32[]{:S(2)}, u32[]{:S(2)}) collective-permute-start(bf16[128,512]{1,0:T(8,128)(2,1)S(1)} %copy-done.11), channel_id=1, source_target_pairs={{0,1},{1,0},{2,3},{3,2},{4,5},{5,4},{6,7},{7,6},{8,9},{9,8},{10,11... | collective-permute-start | bytes 393224 | tf_op jit(solution)/shard_map/ppermute | solution.py:144
  19.4 7.8 %collective-permute-done.1.cot_got = bf16[128,512]{1,0:T(8,128)(2,1)S(1)} collective-permute-done((bf16[128,512]{1,0:T(8,128)(2,1)S(1)}, bf16[128,512]{1,0:T(8,128)(2,1)S(1)}, u32[]{:S(2)}, u32[]{:S(2)}) %collective-permute-start.1) | collective-permute-done | bytes 131104 | tf_op jit(solution)/shard_map/ppermute | solution.py:144
  27.2 4.8 %collective-permute-start.2 = (bf16[512,512]{1,0:T(8,128)(2,1)S(1)}, bf16[512,512]{1,0:T(8,128)(2,1)S(1)}, u32[]{:S(2)}, u32[]{:S(2)}) collective-permute-start(bf16[512,512]{1,0:T(8,128)(2,1)S(1)} %pad_maximum_fusion.refs_0_), channel_id=1, source_target_pairs={{0,2},{2,4},{4,6},{6,8},{8,10},{10,12},{12,14},{14,0},{1,3},{3,5},... | collective-permute-start | bytes 1572872 | tf_op jit(solution)/shard_map/ppermute | solution.py:155
  32.9 8.8 %all-to-all-start.2 = ((bf16[32,8,512]{2,1,0:T(8,128)(2,1)}), bf16[32,8,512]{2,1,0:T(8,128)(2,1)S(1)}, u32[]{:S(2)}, u32[]{:S(2)}) async-start(bf16[32,8,512]{2,1,0:T(8,128)(2,1)} %broadcast_in_dim.15), calls=%async_computation.2 | async-start | bytes 524288 | tf_op jit(solution)/shard_map/all_to_all | solution.py:133
  41.7 1.9 %collective-permute-start.3 = (bf16[512,512]{1,0:T(8,128)(2,1)S(1)}, bf16[512,512]{1,0:T(8,128)(2,1)}, u32[]{:S(2)}, u32[]{:S(2)}) collective-permute-start(bf16[512,512]{1,0:T(8,128)(2,1)S(1)} %pad_maximum_fusion.refs_0_), channel_id=1, source_target_pairs={{0,14},{2,0},{4,2},{6,4},{8,6},{10,8},{12,10},{14,12},{1,15},{3,1}... | collective-permute-start | bytes 1572872 | tf_op jit(solution)/shard_map/ppermute | solution.py:156
  46.1 8.0 %all-to-all-done.2 = bf16[32,8,512]{2,1,0:T(8,128)(2,1)S(1)} async-done(((bf16[32,8,512]{2,1,0:T(8,128)(2,1)}), bf16[32,8,512]{2,1,0:T(8,128)(2,1)S(1)}, u32[]{:S(2)}, u32[]{:S(2)}) %all-to-all-start.2) | async-done | bytes 262176 | tf_op jit(solution)/shard_map/all_to_all | solution.py:133
  54.9 6.5 %all-to-all-start = ((bf16[16,128,256]{2,1,0:T(8,128)(2,1)}), bf16[16,128,256]{2,1,0:T(8,128)(2,1)S(1)}, u32[]{:S(2)}, u32[]{:S(2)}) async-start(bf16[16,128,256]{2,1,0:T(8,128)(2,1)} %copy-done.14), calls=%async_computation | async-start | bytes 2097152 | tf_op jit(solution)/shard_map/all_to_all | solution.py:162
  61.4 4.6 %collective-permute-start.4 = (bf16[512,512]{1,0:T(8,128)(2,1)S(1)}, bf16[512,512]{1,0:T(8,128)(2,1)S(1)}, u32[]{:S(2)}, u32[]{:S(2)}) collective-permute-start(bf16[512,512]{1,0:T(8,128)(2,1)S(1)} %collective-permute-done.2.refs_1_), channel_id=1, source_target_pairs={{0,2},{2,4},{4,6},{6,8},{8,10},{10,12},{12,14},{14,0},{1,3},{3,5},... | collective-permute-start | bytes 1572872 | tf_op jit(solution)/shard_map/ppermute | solution.py:155
  66.0 2.1 %collective-permute-start.5 = (bf16[512,512]{1,0:T(8,128)(2,1)}, bf16[512,512]{1,0:T(8,128)(2,1)S(1)}, u32[]{:S(2)}, u32[]{:S(2)}) collective-permute-start(bf16[512,512]{1,0:T(8,128)(2,1)} %collective-permute-done.3.refs_2_), channel_id=1, source_target_pairs={{0,14},{2,0},{4,2},{6,4},{8,6},{10,8},{12,10},{14,12},{1,15},{3,1}... | collective-permute-start | bytes 1572872 | tf_op jit(solution)/shard_map/ppermute | solution.py:156
  68.1 28.7 %collective-permute-done.4.refs_3_ = bf16[512,512]{1,0:T(8,128)(2,1)S(1)} collective-permute-done((bf16[512,512]{1,0:T(8,128)(2,1)S(1)}, bf16[512,512]{1,0:T(8,128)(2,1)S(1)}, u32[]{:S(2)}, u32[]{:S(2)}) %collective-permute-start.4) | collective-permute-done | bytes 524320 | tf_op jit(solution)/shard_map/ppermute | solution.py:155
  96.8 4.6 %collective-permute-start.6 = (bf16[512,512]{1,0:T(8,128)(2,1)S(1)}, bf16[512,512]{1,0:T(8,128)(2,1)S(1)}, u32[]{:S(2)}, u32[]{:S(2)}) collective-permute-start(bf16[512,512]{1,0:T(8,128)(2,1)S(1)} %collective-permute-done.4.refs_3_), channel_id=1, source_target_pairs={{0,2},{2,4},{4,6},{6,8},{8,10},{10,12},{12,14},{14,0},{1,3},{3,5},... | collective-permute-start | bytes 1572872 | tf_op jit(solution)/shard_map/ppermute | solution.py:155
  101.4 3.4 %collective-permute-start = (bf16[128,2048]{1,0:T(8,128)(2,1)}, bf16[128,2048]{1,0:T(8,128)(2,1)S(1)}, u32[]{:S(2)}, u32[]{:S(2)}) collective-permute-start(bf16[128,2048]{1,0:T(8,128)(2,1)} %copy-done.21), channel_id=1, source_target_pairs={{0,1},{1,0},{2,3},{3,2},{4,5},{5,4},{6,7},{7,6},{8,9},{9,8},{10,11... | collective-permute-start | bytes 1572872 | tf_op jit(solution)/shard_map/ppermute | solution.py:160
  104.8 1.9 %collective-permute-start.7 = (bf16[512,512]{1,0:T(8,128)(2,1)S(1)}, bf16[512,512]{1,0:T(8,128)(2,1)S(1)}, u32[]{:S(2)}, u32[]{:S(2)}) collective-permute-start(bf16[512,512]{1,0:T(8,128)(2,1)S(1)} %collective-permute-done.5.refs_4_), channel_id=1, source_target_pairs={{0,14},{2,0},{4,2},{6,4},{8,6},{10,8},{12,10},{14,12},{1,15},{3,1}... | collective-permute-start | bytes 1572872 | tf_op jit(solution)/shard_map/ppermute | solution.py:156
  106.7 6.1 %collective-permute-done.6.refs_5_ = bf16[512,512]{1,0:T(8,128)(2,1)S(1)} collective-permute-done((bf16[512,512]{1,0:T(8,128)(2,1)S(1)}, bf16[512,512]{1,0:T(8,128)(2,1)S(1)}, u32[]{:S(2)}, u32[]{:S(2)}) %collective-permute-start.6) | collective-permute-done | bytes 524320 | tf_op jit(solution)/shard_map/ppermute | solution.py:155
  112.8 5.6 %collective-permute-start.9 = (bf16[256,512]{1,0:T(8,128)(2,1)S(1)}, bf16[256,512]{1,0:T(8,128)(2,1)S(1)}, u32[]{:S(2)}, u32[]{:S(2)}) collective-permute-start(bf16[256,512]{1,0:T(8,128)(2,1)S(1)} %slice.8), channel_id=1, source_target_pairs={{0,2},{2,4},{4,6},{6,8},{8,10},{10,12},{12,14},{14,0},{1,3},{3,5},... | collective-permute-start | bytes 786440 | tf_op jit(solution)/shard_map/ppermute | solution.py:157
  118.4 2.8 %collective-permute-done.7.refs_6_ = bf16[512,512]{1,0:T(8,128)(2,1)S(1)} collective-permute-done((bf16[512,512]{1,0:T(8,128)(2,1)S(1)}, bf16[512,512]{1,0:T(8,128)(2,1)S(1)}, u32[]{:S(2)}, u32[]{:S(2)}) %collective-permute-start.7) | collective-permute-done | bytes 524320 | tf_op jit(solution)/shard_map/ppermute | solution.py:156
  121.2 2.6 %shard_map.111 = (bf16[128,1792]{1,0:T(8,128)(2,1)S(1)}, bf16[128,1792]{1,0:T(8,128)(2,1)S(1)}, f32[256,512]{1,0:T(8,128)S(1)}) custom-call(s32[2]{0:T(128)S(1)} %pad_add_fusion.place, bf16[128,4096]{1,0:T(8,128)(2,1)S(1)} %copy-done, bf16[128,2048]{1,0:T(8,128)(2,1)S(1)} %collective-permute-done.got, bf16[128,512]{1,0:T(8,128)(2,1)S(1)} %copy-done.11, ...), custom_call_target="tpu_custom_call" | custom-call | flops 939524096 | bytes 6946816 | tf_op jit(solution)/shard_map/pallas_call | solution.py:40
  123.9 2.5 %collective-permute-start.8 = (bf16[128,1792]{1,0:T(8,128)(2,1)S(1)}, bf16[128,1792]{1,0:T(8,128)(2,1)S(1)}, u32[]{:S(2)}, u32[]{:S(2)}) collective-permute-start(bf16[128,1792]{1,0:T(8,128)(2,1)S(1)} %get-tuple-element.21), channel_id=1, source_target_pairs={{0,1},{1,0},{2,3},{3,2},{4,5},{5,4},{6,7},{7,6},{8,9},{9,8},{10,11... | collective-permute-start | bytes 1376264 | tf_op jit(solution)/shard_map/ppermute | solution.py:174
  126.4 1.9 %collective-permute-start.11 = (bf16[256,512]{1,0:T(8,128)(2,1)S(1)}, bf16[256,512]{1,0:T(8,128)(2,1)S(1)}, u32[]{:S(2)}, u32[]{:S(2)}) collective-permute-start(bf16[256,512]{1,0:T(8,128)(2,1)S(1)} %slice.9), channel_id=1, source_target_pairs={{0,14},{2,0},{4,2},{6,4},{8,6},{10,8},{12,10},{14,12},{1,15},{3,1}... | collective-permute-start | bytes 786440 | tf_op jit(solution)/shard_map/ppermute | solution.py:158
  129.2 3.4 %collective-permute-start.10 = (bf16[128,768]{1,0:T(8,128)(2,1)S(1)}, bf16[128,768]{1,0:T(8,128)(2,1)S(1)}, u32[]{:S(2)}, u32[]{:S(2)}) collective-permute-start(bf16[128,768]{1,0:T(8,128)(2,1)S(1)} %get-tuple-element.24), channel_id=1, source_target_pairs={{0,1},{1,0},{2,3},{3,2},{4,5},{5,4},{6,7},{7,6},{8,9},{9,8},{10,11... | collective-permute-start | bytes 589832 | tf_op jit(solution)/shard_map/ppermute | solution.py:180
  132.5 8.4 %collective-permute-done.10.far = bf16[128,768]{1,0:T(8,128)(2,1)S(1)} collective-permute-done((bf16[128,768]{1,0:T(8,128)(2,1)S(1)}, bf16[128,768]{1,0:T(8,128)(2,1)S(1)}, u32[]{:S(2)}, u32[]{:S(2)}) %collective-permute-start.10) | collective-permute-done | bytes 196640 | tf_op jit(solution)/shard_map/ppermute | solution.py:180
  151.3 3.7 %shard_map.114 = (f32[256,512]{1,0:T(8,128)}, bf16[256,512]{1,0:T(8,128)(2,1)}, bf16[256,512]{1,0:T(8,128)(2,1)}) custom-call(s32[2]{0:T(128)S(1)} %pad_add_fusion.place, bf16[16,128,256]{2,1,0:T(8,128)(2,1)S(1)} %all-to-all-done.slab, f32[256,512]{1,0:T(8,128)S(1)} %bitcast.12, bf16[256,512]{1,0:T(8,128)(2,1)S(1)} %bitcast.14, ...), custom_call_target="tpu_custom_call" | custom-call | flops 536870912 | bytes 7864320 | tf_op jit(solution)/shard_map/pallas_call | solution.py:40
  (64 shorter events, 15.3 us)
Async XLA Ops:
  2.7 13.3 %copy-start.11 = (bf16[128,512]{1,0:T(8,128)(2,1)S(1)}, bf16[128,512]{1,0:T(8,128)(2,1)}, u32[]{:S(2)}) copy-start(bf16[128,512]{1,0:T(8,128)(2,1)} %cot.3) | copy-start | bytes 393220
  2.7 29.4 %all-to-all-start.1 = ((bf16[32,8,512]{2,1,0:T(8,128)(2,1)}), bf16[32,8,512]{2,1,0:T(8,128)(2,1)S(1)}, u32[]{:S(2)}, u32[]{:S(2)}) async-start(bf16[32,8,512]{2,1,0:T(8,128)(2,1)} %get-tuple-element.33), calls=%async_computation.1 | async-start | bytes 524288 | tf_op jit(solution)/shard_map/all_to_all | solution.py:131
  16.0 11.2 %collective-permute-start.1 = (bf16[128,512]{1,0:T(8,128)(2,1)S(1)}, bf16[128,512]{1,0:T(8,128)(2,1)S(1)}, u32[]{:S(2)}, u32[]{:S(2)}) collective-permute-start(bf16[128,512]{1,0:T(8,128)(2,1)S(1)} %copy-done.11), channel_id=1, source_target_pairs={{0,1},{1,0},{2,3},{3,2},{4,5},{5,4},{6,7},{7,6},{8,9},{9,8},{10,11... | collective-permute-start | bytes 393224 | tf_op jit(solution)/shard_map/ppermute | solution.py:144
  27.2 16.5 %copy-start = (bf16[128,4096]{1,0:T(8,128)(2,1)S(1)}, bf16[128,4096]{1,0:T(8,128)(2,1)}, u32[]{:S(2)}) copy-start(bf16[128,4096]{1,0:T(8,128)(2,1)} %tok.5) | copy-start | bytes 3145732
  27.2 18.9 %collective-permute-start.2 = (bf16[512,512]{1,0:T(8,128)(2,1)S(1)}, bf16[512,512]{1,0:T(8,128)(2,1)S(1)}, u32[]{:S(2)}, u32[]{:S(2)}) collective-permute-start(bf16[512,512]{1,0:T(8,128)(2,1)S(1)} %pad_maximum_fusion.refs_0_), channel_id=1, source_target_pairs={{0,2},{2,4},{4,6},{6,8},{8,10},{10,12},{12,14},{14,0},{1,3},{3,5},... | collective-permute-start | bytes 1572872 | tf_op jit(solution)/shard_map/ppermute | solution.py:155
  32.9 21.3 %all-to-all-start.2 = ((bf16[32,8,512]{2,1,0:T(8,128)(2,1)}), bf16[32,8,512]{2,1,0:T(8,128)(2,1)S(1)}, u32[]{:S(2)}, u32[]{:S(2)}) async-start(bf16[32,8,512]{2,1,0:T(8,128)(2,1)} %broadcast_in_dim.15), calls=%async_computation.2 | async-start | bytes 524288 | tf_op jit(solution)/shard_map/all_to_all | solution.py:133
  41.7 24.4 %collective-permute-start.3 = (bf16[512,512]{1,0:T(8,128)(2,1)S(1)}, bf16[512,512]{1,0:T(8,128)(2,1)}, u32[]{:S(2)}, u32[]{:S(2)}) collective-permute-start(bf16[512,512]{1,0:T(8,128)(2,1)S(1)} %pad_maximum_fusion.refs_0_), channel_id=1, source_target_pairs={{0,14},{2,0},{4,2},{6,4},{8,6},{10,8},{12,10},{14,12},{1,15},{3,1}... | collective-permute-start | bytes 1572872 | tf_op jit(solution)/shard_map/ppermute | solution.py:156
  46.1 15.3 %copy-start.4 = (bf16[512,512]{1,0:T(8,128)(2,1)}, bf16[512,512]{1,0:T(8,128)(2,1)S(1)}, u32[]{:S(2)}) copy-start(bf16[512,512]{1,0:T(8,128)(2,1)S(1)} %collective-permute-done.2.refs_1_) | copy-start | bytes 1572868
  54.9 88.5 %all-to-all-start = ((bf16[16,128,256]{2,1,0:T(8,128)(2,1)}), bf16[16,128,256]{2,1,0:T(8,128)(2,1)S(1)}, u32[]{:S(2)}, u32[]{:S(2)}) async-start(bf16[16,128,256]{2,1,0:T(8,128)(2,1)} %copy-done.14), calls=%async_computation | async-start | bytes 2097152 | tf_op jit(solution)/shard_map/all_to_all | solution.py:162
  61.4 35.4 %collective-permute-start.4 = (bf16[512,512]{1,0:T(8,128)(2,1)S(1)}, bf16[512,512]{1,0:T(8,128)(2,1)S(1)}, u32[]{:S(2)}, u32[]{:S(2)}) collective-permute-start(bf16[512,512]{1,0:T(8,128)(2,1)S(1)} %collective-permute-done.2.refs_1_), channel_id=1, source_target_pairs={{0,2},{2,4},{4,6},{6,8},{8,10},{10,12},{12,14},{14,0},{1,3},{3,5},... | collective-permute-start | bytes 1572872 | tf_op jit(solution)/shard_map/ppermute | solution.py:155
  66.0 55.2 %copy-start.5 = (bf16[512,512]{1,0:T(8,128)(2,1)S(1)}, bf16[512,512]{1,0:T(8,128)(2,1)}, u32[]{:S(2)}) copy-start(bf16[512,512]{1,0:T(8,128)(2,1)} %copy-done.4) | copy-start | bytes 1572868
  66.0 38.7 %collective-permute-start.5 = (bf16[512,512]{1,0:T(8,128)(2,1)}, bf16[512,512]{1,0:T(8,128)(2,1)S(1)}, u32[]{:S(2)}, u32[]{:S(2)}) collective-permute-start(bf16[512,512]{1,0:T(8,128)(2,1)} %collective-permute-done.3.refs_2_), channel_id=1, source_target_pairs={{0,14},{2,0},{4,2},{6,4},{8,6},{10,8},{12,10},{14,12},{1,15},{3,1}... | collective-permute-start | bytes 1572872 | tf_op jit(solution)/shard_map/ppermute | solution.py:156
  96.8 27.0 %copy-start.7 = (bf16[512,512]{1,0:T(8,128)(2,1)}, bf16[512,512]{1,0:T(8,128)(2,1)S(1)}, u32[]{:S(2)}) copy-start(bf16[512,512]{1,0:T(8,128)(2,1)S(1)} %collective-permute-done.4.refs_3_) | copy-start | bytes 1572868
  96.8 16.0 %collective-permute-start.6 = (bf16[512,512]{1,0:T(8,128)(2,1)S(1)}, bf16[512,512]{1,0:T(8,128)(2,1)S(1)}, u32[]{:S(2)}, u32[]{:S(2)}) collective-permute-start(bf16[512,512]{1,0:T(8,128)(2,1)S(1)} %collective-permute-done.4.refs_3_), channel_id=1, source_target_pairs={{0,2},{2,4},{4,6},{6,8},{8,10},{10,12},{12,14},{14,0},{1,3},{3,5},... | collective-permute-start | bytes 1572872 | tf_op jit(solution)/shard_map/ppermute | solution.py:155
  101.4 17.0 %collective-permute-start = (bf16[128,2048]{1,0:T(8,128)(2,1)}, bf16[128,2048]{1,0:T(8,128)(2,1)S(1)}, u32[]{:S(2)}, u32[]{:S(2)}) collective-permute-start(bf16[128,2048]{1,0:T(8,128)(2,1)} %copy-done.21), channel_id=1, source_target_pairs={{0,1},{1,0},{2,3},{3,2},{4,5},{5,4},{6,7},{7,6},{8,9},{9,8},{10,11... | collective-permute-start | bytes 1572872 | tf_op jit(solution)/shard_map/ppermute | solution.py:160
  104.8 19.1 %copy-start.9 = (bf16[512,512]{1,0:T(8,128)(2,1)}, bf16[512,512]{1,0:T(8,128)(2,1)S(1)}, u32[]{:S(2)}) copy-start(bf16[512,512]{1,0:T(8,128)(2,1)S(1)} %collective-permute-done.5.refs_4_) | copy-start | bytes 1572868
  104.8 16.4 %collective-permute-start.7 = (bf16[512,512]{1,0:T(8,128)(2,1)S(1)}, bf16[512,512]{1,0:T(8,128)(2,1)S(1)}, u32[]{:S(2)}, u32[]{:S(2)}) collective-permute-start(bf16[512,512]{1,0:T(8,128)(2,1)S(1)} %collective-permute-done.5.refs_4_), channel_id=1, source_target_pairs={{0,14},{2,0},{4,2},{6,4},{8,6},{10,8},{12,10},{14,12},{1,15},{3,1}... | collective-permute-start | bytes 1572872 | tf_op jit(solution)/shard_map/ppermute | solution.py:156
  112.8 15.5 %collective-permute-start.9 = (bf16[256,512]{1,0:T(8,128)(2,1)S(1)}, bf16[256,512]{1,0:T(8,128)(2,1)S(1)}, u32[]{:S(2)}, u32[]{:S(2)}) collective-permute-start(bf16[256,512]{1,0:T(8,128)(2,1)S(1)} %slice.8), channel_id=1, source_target_pairs={{0,2},{2,4},{4,6},{6,8},{8,10},{10,12},{12,14},{14,0},{1,3},{3,5},... | collective-permute-start | bytes 786440 | tf_op jit(solution)/shard_map/ppermute | solution.py:157
  121.2 5.1 %copy-start.1 = (bf16[512,512]{1,0:T(8,128)(2,1)}, bf16[512,512]{1,0:T(8,128)(2,1)S(1)}, u32[]{:S(2)}) copy-start(bf16[512,512]{1,0:T(8,128)(2,1)S(1)} %collective-permute-done.7.refs_6_) | copy-start | bytes 1572868
  123.9 17.1 %collective-permute-start.8 = (bf16[128,1792]{1,0:T(8,128)(2,1)S(1)}, bf16[128,1792]{1,0:T(8,128)(2,1)S(1)}, u32[]{:S(2)}, u32[]{:S(2)}) collective-permute-start(bf16[128,1792]{1,0:T(8,128)(2,1)S(1)} %get-tuple-element.21), channel_id=1, source_target_pairs={{0,1},{1,0},{2,3},{3,2},{4,5},{5,4},{6,7},{7,6},{8,9},{9,8},{10,11... | collective-permute-start | bytes 1376264 | tf_op jit(solution)/shard_map/ppermute | solution.py:174
  126.4 16.3 %collective-permute-start.11 = (bf16[256,512]{1,0:T(8,128)(2,1)S(1)}, bf16[256,512]{1,0:T(8,128)(2,1)S(1)}, u32[]{:S(2)}, u32[]{:S(2)}) collective-permute-start(bf16[256,512]{1,0:T(8,128)(2,1)S(1)} %slice.9), channel_id=1, source_target_pairs={{0,14},{2,0},{4,2},{6,4},{8,6},{10,8},{12,10},{14,12},{1,15},{3,1}... | collective-permute-start | bytes 786440 | tf_op jit(solution)/shard_map/ppermute | solution.py:158
  129.2 11.8 %collective-permute-start.10 = (bf16[128,768]{1,0:T(8,128)(2,1)S(1)}, bf16[128,768]{1,0:T(8,128)(2,1)S(1)}, u32[]{:S(2)}, u32[]{:S(2)}) collective-permute-start(bf16[128,768]{1,0:T(8,128)(2,1)S(1)} %get-tuple-element.24), channel_id=1, source_target_pairs={{0,1},{1,0},{2,3},{3,2},{4,5},{5,4},{6,7},{7,6},{8,9},{9,8},{10,11... | collective-permute-start | bytes 589832 | tf_op jit(solution)/shard_map/ppermute | solution.py:180
  141.0 2.4 %copy-start.3 = (f32[1,256,512]{2,1,0:T(8,128)S(1)}, f32[1,256,512]{2,1,0:T(8,128)}, u32[]{:S(2)}) copy-start(f32[1,256,512]{2,1,0:T(8,128)} %param.9) | copy-start | bytes 1572868
  141.0 2.4 %copy-start.13 = (bf16[32,8,512]{2,1,0:T(8,128)(2,1)S(1)}, bf16[32,8,512]{2,1,0:T(8,128)(2,1)}, u32[]{:S(2)}) copy-start(bf16[32,8,512]{2,1,0:T(8,128)(2,1)} %copy-done.12) | copy-start | bytes 786436
  (13 other events, 13.5 us)

commit v3 on v1

v3 whole, which is shorter than its diff:
```python
import functools
import math

import jax
import jax.numpy as jnp
from jax import lax
from jax.experimental import pallas as pl
from jax.experimental.pallas import tpu as pltpu
from jax.sharding import Mesh, PartitionSpec as P

SIZES = (4, 4, 2, 8, 2)
NAMES = ("zh", "x", "core", "y", "zl")
REPLICA = ("zh", "x", "core")
FSDP = ("y", "zl")
PAIR = [(0, 1), (1, 0)]
BF16 = jnp.bfloat16
F32 = jnp.float32
YS = 8
REPLICAS = 32
ROWS = 256
TOK = 128
KV = 512
MIB = 1 << 20


def whole(shape):
    return pl.BlockSpec(shape, lambda *_: (0,) * len(shape))


def call(kernel, place, args, in_specs, outs, flops, scratch=()):
    size = sum(math.prod(a.shape) * a.dtype.itemsize for a in args)
    size += sum(math.prod(o.shape) * o.dtype.itemsize for o in outs)
    return pl.pallas_call(
        kernel,
        out_shape=outs,
        grid_spec=pltpu.PrefetchScalarGridSpec(
            num_scalar_prefetch=0 if place is None else 1,
            grid=(1,),
            in_specs=in_specs,
            out_specs=[whole(o.shape) for o in outs],
            scratch_shapes=scratch,
        ),
        compiler_params=pltpu.CompilerParams(vmem_limit_bytes=56 * MIB),
        cost_estimate=pl.CostEstimate(flops=flops, bytes_accessed=size, transcendentals=0),
    )(*([] if place is None else [place]), *args)


def lanes(index):
    return pl.ds(pl.multiple_of(index * ROWS, ROWS), ROWS)


def pack_kernel(weight, cot, packed):
    packed[:ROWS] = weight[...].astype(BF16)
    packed[ROWS:] = cot[...]


def split_kernel(place, tok, cot, blocks, other):
    other[:, YS * ROWS :] = cot[...]
    for f in range(YS):
        blocks[f] = tok[:, 2 * f * ROWS : (2 * f + 2) * ROWS]
        other[:, f * ROWS : (f + 1) * ROWS] = tok[:, lanes(2 * f + 1 - place[1])]


def product_kernel(factor, place, tok, cot, got, both, own, ahead, to_return):
    cots = jnp.concatenate([cot[...], got[:, YS * ROWS :]], 0)
    total = None
    for f in range(YS):
        w = both[f, :ROWS]
        cols = slice(f * ROWS, (f + 1) * ROWS)
        x = jnp.concatenate([tok[:, lanes(2 * f + place[1])], got[:, cols]], 0)
        part = jnp.dot(x, w, preferred_element_type=F32)
        total = part if f == 0 else total + part
        ig = lax.dot_general(cots, w, (((1,), (1,)), ((), ())), preferred_element_type=F32)
        ig = (ig * factor).astype(BF16)
        own[:, cols] = ig[:TOK]
        to_return[:, cols] = ig[TOK:]
    ahead[...] = total[:TOK] * factor
    to_return[:, YS * ROWS :] = (total[TOK:] * factor).astype(BF16)


def join_kernel(place, own, ahead, returned, projected, input_grad):
    zl = place[1]
    for f in range(YS):
        cols = slice(f * ROWS, (f + 1) * ROWS)
        input_grad[:, lanes(2 * f + zl)] = own[:, cols]
        input_grad[:, lanes(2 * f + 1 - zl)] = returned[:, cols]
    projected[...] = (ahead[...] + returned[:, YS * ROWS :].astype(F32)).astype(BF16)


def grad_kernel(factor, place, slab, both, keep, send):
    for out, col in ((send, 1 - place[1]), (keep, place[1])):
        total = None
        for f in range(0, YS, 2):
            x = slab[f : f + 2, :, lanes(col)].reshape(2 * TOK, ROWS)
            c = jnp.concatenate([both[f, ROWS:], both[f + 1, ROWS:]], 0)
            part = lax.dot_general(x, c, (((0,), (0,)), ((), ())), preferred_element_type=F32)
            total = part if f == 0 else total + part
        out[...] = (total * factor).astype(out.dtype)


def step_kernel(place, keep, sent, weight, moment, second, outer, momentum, half_sum, half_got, new_weight, new_moment, new_second):
    grad = keep[...] + sent[...].astype(F32)
    local = weight[...]
    outer_wide = outer[...].astype(F32)
    a, b = half_sum[...].astype(F32), half_got[...].astype(F32)
    low = place[2] == 0
    mean = jnp.concatenate([jnp.where(low, a, b), jnp.where(low, b, a)], 0) * (1.0 / REPLICAS)
    average = outer_wide - mean
    velocity = 0.9 * momentum[...].astype(F32) + average
    outer_new = outer_wide - 0.7 * (average + 0.9 * velocity)
    first_new = 0.8 * moment[...].astype(F32) + 0.2 * grad
    second_new = 0.95 * second[...].astype(F32) + 0.05 * grad * grad
    inner = local - 0.05 * (first_new / (jnp.sqrt(second_new) + 1e-08) + 0.1 * local)
    new_weight[...] = 0.5 * inner + 0.5 * outer_new
    new_moment[...] = first_new.astype(BF16)
    new_second[...] = second_new.astype(BF16)


def ring_shift(size, k):
    return [(i, (i + k) % size) for i in range(size)]


def add_pair(part):
    return (part[0].astype(F32) + part[1].astype(F32)).astype(BF16)


def ring_step(total, axis, k):
    return add_pair((total, lax.ppermute(total, axis, ring_shift(4, k))))


def core_sum(packed):
    core = lax.axis_index("core")
    n = ROWS // 2
    mine = lax.dynamic_slice_in_dim(packed, core * n, n)
    return add_pair((mine, lax.ppermute(lax.dynamic_slice_in_dim(packed, (1 - core) * n, n), "core", PAIR)))


def body(tokens, cotangent, weight, moment, second, outer_params, momentum):
    factor = 1.0 / math.sqrt(tokens.shape[1])
    place = jnp.stack([lax.axis_index("y"), lax.axis_index("zl"), lax.axis_index("core")]).astype(jnp.int32)
    sds = jax.ShapeDtypeStruct
    half = YS * ROWS
    flops = 2 * 2 * TOK * half * KV

    def run(kernel, args, outs, cost=0):
        return call(kernel, place, args, [whole(a.shape) for a in args], outs, cost)

    (packed,) = call(
        pack_kernel, None, [weight[0], cotangent],
        [pl.BlockSpec((ROWS, KV), lambda i: (0, 0)), pl.BlockSpec((TOK, KV), lambda i: (0, 0))],
        [sds((ROWS + TOK, KV), BF16)], 0,
    )
    both = lax.all_gather(packed, "y", axis=0, tiled=False)
    blocks, other = run(
        split_kernel, [tokens, cotangent], [sds((YS, TOK, 2 * ROWS), BF16), sds((TOK, half + KV), BF16)]
    )
    got = lax.ppermute(other, "zl", PAIR)

    packed, other = lax.optimization_barrier((packed, other))
    half_sum, got = lax.optimization_barrier((core_sum(packed), got))
    half_sum = ring_step(half_sum, "x", 2)
    blocks, half_sum = lax.optimization_barrier((blocks, half_sum))
    slab = lax.all_to_all(blocks, "y", 0, 0, tiled=True)
    half_sum = ring_step(half_sum, "x", 1)
    half_sum = ring_step(ring_step(half_sum, "zh", 2), "zh", 1)
    slab, half_sum = lax.optimization_barrier((slab, half_sum))

    own, ahead, to_return = run(
        functools.partial(product_kernel, factor), [tokens, cotangent, got, both],
        [sds((TOK, half), BF16), sds((TOK, KV), F32), sds((TOK, half + KV), BF16)], 2 * flops,
    )
    returned = lax.ppermute(to_return, "zl", PAIR)
    keep, send = run(
        functools.partial(grad_kernel, factor), [slab, both], [sds((ROWS, KV), F32), sds((ROWS, KV), BF16)], flops
    )
    send, half_sum = lax.optimization_barrier((send, half_sum))
    sent = lax.ppermute(send, "zl", PAIR)
    half_got = lax.ppermute(half_sum, "core", PAIR)
    projected, input_grad = run(
        join_kernel, [own, ahead, returned], [sds((TOK, KV), BF16), sds(tokens.shape, BF16)]
    )
    sent, projected = lax.optimization_barrier((sent, projected))
    new_weight, new_moment, new_second = run(
        step_kernel, [keep, sent, weight[0], moment[0], second[0], outer_params, momentum, half_sum, half_got],
        [sds((ROWS, KV), F32), sds((ROWS, KV), BF16), sds((ROWS, KV), BF16)], 40 * ROWS * KV,
    )
    return projected, input_grad, new_weight[None], new_moment[None], new_second[None]


def solution(mesh):
    fine = Mesh(mesh.devices.reshape(SIZES), NAMES)
    tok = P(NAMES, None)
    par = P(REPLICA, FSDP, None)
    outer = P(FSDP, None)
    return jax.shard_map(
        body,
        mesh=fine,
        in_specs=(tok, tok, par, par, par, outer, outer),
        out_specs=(tok, tok, par, par, par),
        check_vma=False,
    )
```

time: 135 us -> 126 us (0.933)
  the two profiles are of different devices: /device:TPU:1 before, /device:TPU:24 now
where the time goes in v3:
time: 126 us; the launch traced here: 125 us
  starting transfers between devices  44.7 us (35%)
  waiting for transfers between devices  39 us (31%)
  Pallas kernels  22 us (17%)
  between operations  14.2 us (11%)
  local copies, waits for them, and re-layouts  3.5 us (3%)
  other arithmetic  1.74 us (1%)
    ppermute x4, starting transfers between devices, ring_step(): return add_pair((total, lax.ppermute(total, axis, ring_shift(4, k))))  23.5 us
    pallas_call x6, Pallas kernels, call(): pl.pallas_call(kernel, out_shape=outs, grid_spec=pltpu.PrefetchScalarGrid...  22 us
    ppermute x4, waiting for transfers between devices, ring_step(): return add_pair((total, lax.ppermute(total, axis, ring_shift(4, k))))  11.9 us
    ppermute x1, waiting for transfers between devices, body(): got = lax.ppermute(other, 'zl', PAIR)  9.82 us
    all_gather x1, waiting for transfers between devices, body(): both = lax.all_gather(packed, 'y', axis=0, tiled=False)  9.39 us
    all_to_all x1, starting transfers between devices, body(): slab = lax.all_to_all(blocks, 'y', 0, 0, tiled=True)  7.33 us
    ppermute x1, waiting for transfers between devices, body(): returned = lax.ppermute(to_return, 'zl', PAIR)  6.53 us
    ppermute x1, starting transfers between devices, body(): got = lax.ppermute(other, 'zl', PAIR)  4.28 us
  transfers between devices with their start and end apart: 11, of which 7 were waited for; matrix products, arithmetic and copies ran while one was open for 2% of the time, Pallas kernels for 13%

profile of v3, /device:TPU:24, one launch (start us, length us, event | category | flops | bytes accessed | tf_op | source)
XLA Modules:
  0.0 125.2 jit_solution(16850821619145337389)
XLA Ops:
  7.2 1.8 %shard_map.111 = bf16[384,512]{1,0:T(8,128)(2,1)} custom-call(f32[256,512]{1,0:T(8,128)} %bitcast.12, bf16[128,512]{1,0:T(8,128)(2,1)} %cot.5), custom_call_target="tpu_custom_call" | custom-call | bytes 1048576 | tf_op jit(solution)/shard_map/pallas_call | solution.py:33
  9.8 3.2 %shard_map.110 = (bf16[8,128,512]{2,1,0:T(8,128)(2,1)}, bf16[128,2560]{1,0:T(8,128)(2,1)}) custom-call(s32[3]{0:T(128)} %pad_add_fusion.place, bf16[128,4096]{1,0:T(8,128)(2,1)} %tok.3, bf16[128,512]{1,0:T(8,128)(2,1)} %cot.5), custom_call_target="tpu_custom_call" | custom-call | bytes 2883584 | tf_op jit(solution)/shard_map/pallas_call | solution.py:33
  13.0 4.3 %collective-permute-start.1 = (bf16[128,2560]{1,0:T(8,128)(2,1)}, bf16[128,2560]{1,0:T(8,128)(2,1)S(1)}, u32[]{:S(2)}, u32[]{:S(2)}) collective-permute-start(bf16[128,2560]{1,0:T(8,128)(2,1)} %get-tuple-element.29), channel_id=1, source_target_pairs={{0,1},{1,0},{2,3},{3,2},{4,5},{5,4},{6,7},{7,6},{8,9},{9,8},{10,11... | collective-permute-start | bytes 1966088 | tf_op jit(solution)/shard_map/ppermute | solution.py:157
  18.2 1.9 %collective-permute-start = (bf16[128,512]{1,0:T(8,128)(2,1)S(1)}, bf16[128,512]{1,0:T(8,128)(2,1)S(1)}, u32[]{:S(2)}, u32[]{:S(2)}) collective-permute-start(bf16[128,512]{1,0:T(8,128)(2,1)S(1)} %constant_dynamic-slice_fusion), channel_id=1, source_target_pairs={{0,16},{16,0},{1,17},{17,1},{2,18},{18,2},{3,19},{19,3},{4,20},{20... | collective-permute-start | bytes 393224 | tf_op jit(solution)/shard_map/ppermute | solution.py:135
  20.1 1.3 %collective-permute-done = bf16[128,512]{1,0:T(8,128)(2,1)S(1)} collective-permute-done((bf16[128,512]{1,0:T(8,128)(2,1)S(1)}, bf16[128,512]{1,0:T(8,128)(2,1)S(1)}, u32[]{:S(2)}, u32[]{:S(2)}) %collective-permute-start) | collective-permute-done | bytes 131104 | tf_op jit(solution)/shard_map/ppermute | solution.py:135
  22.4 9.8 %collective-permute-done.1.got = bf16[128,2560]{1,0:T(8,128)(2,1)S(1)} collective-permute-done((bf16[128,2560]{1,0:T(8,128)(2,1)}, bf16[128,2560]{1,0:T(8,128)(2,1)S(1)}, u32[]{:S(2)}, u32[]{:S(2)}) %collective-permute-start.1) | collective-permute-done | bytes 655392 | tf_op jit(solution)/shard_map/ppermute | solution.py:157
  32.2 4.9 %collective-permute-start.2 = (bf16[128,512]{1,0:T(8,128)(2,1)S(1)}, bf16[128,512]{1,0:T(8,128)(2,1)S(1)}, u32[]{:S(2)}, u32[]{:S(2)}) collective-permute-start(bf16[128,512]{1,0:T(8,128)(2,1)S(1)} %add_convert_fusion.4), channel_id=1, source_target_pairs={{0,64},{32,96},{64,0},{96,32},{1,65},{33,97},{65,1},{97,33},{2,66}... | collective-permute-start | bytes 393224 | tf_op jit(solution)/shard_map/ppermute | solution.py:128
  37.1 3.4 %collective-permute-done.2 = bf16[128,512]{1,0:T(8,128)(2,1)S(1)} collective-permute-done((bf16[128,512]{1,0:T(8,128)(2,1)S(1)}, bf16[128,512]{1,0:T(8,128)(2,1)S(1)}, u32[]{:S(2)}, u32[]{:S(2)}) %collective-permute-start.2) | collective-permute-done | bytes 131104 | tf_op jit(solution)/shard_map/ppermute | solution.py:128
  40.6 7.3 %all-to-all-start = ((bf16[8,128,512]{2,1,0:T(8,128)(2,1)}), bf16[8,128,512]{2,1,0:T(8,128)(2,1)S(1)}, u32[]{:S(2)}, u32[]{:S(2)}) async-start(bf16[8,128,512]{2,1,0:T(8,128)(2,1)} %get-tuple-element.32), calls=%async_computation | async-start | bytes 2097152 | tf_op jit(solution)/shard_map/all_to_all | solution.py:163
  47.9 3.4 %collective-permute-start.3 = (bf16[128,512]{1,0:T(8,128)(2,1)S(1)}, bf16[128,512]{1,0:T(8,128)(2,1)S(1)}, u32[]{:S(2)}, u32[]{:S(2)}) collective-permute-start(bf16[128,512]{1,0:T(8,128)(2,1)S(1)} %add_convert_fusion.3), channel_id=1, source_target_pairs={{0,32},{32,64},{64,96},{96,0},{1,33},{33,65},{65,97},{97,1},{2,34}... | collective-permute-start | bytes 393224 | tf_op jit(solution)/shard_map/ppermute | solution.py:128
  51.3 4.7 %collective-permute-done.3 = bf16[128,512]{1,0:T(8,128)(2,1)S(1)} collective-permute-done((bf16[128,512]{1,0:T(8,128)(2,1)S(1)}, bf16[128,512]{1,0:T(8,128)(2,1)S(1)}, u32[]{:S(2)}, u32[]{:S(2)}) %collective-permute-start.3) | collective-permute-done | bytes 131104 | tf_op jit(solution)/shard_map/ppermute | solution.py:128
  56.0 10.3 %collective-permute-start.4 = (bf16[128,512]{1,0:T(8,128)(2,1)S(1)}, bf16[128,512]{1,0:T(8,128)(2,1)S(1)}, u32[]{:S(2)}, u32[]{:S(2)}) collective-permute-start(bf16[128,512]{1,0:T(8,128)(2,1)S(1)} %add_convert_fusion.2), channel_id=1, source_target_pairs={{0,256},{128,384},{256,0},{384,128},{1,257},{129,385},{257,1},{385... | collective-permute-start | bytes 393224 | tf_op jit(solution)/shard_map/ppermute | solution.py:128
  66.3 3.9 %collective-permute-done.4 = bf16[128,512]{1,0:T(8,128)(2,1)S(1)} collective-permute-done((bf16[128,512]{1,0:T(8,128)(2,1)S(1)}, bf16[128,512]{1,0:T(8,128)(2,1)S(1)}, u32[]{:S(2)}, u32[]{:S(2)}) %collective-permute-start.4) | collective-permute-done | bytes 131104 | tf_op jit(solution)/shard_map/ppermute | solution.py:128
  70.2 4.9 %collective-permute-start.5 = (bf16[128,512]{1,0:T(8,128)(2,1)S(1)}, bf16[128,512]{1,0:T(8,128)(2,1)S(1)}, u32[]{:S(2)}, u32[]{:S(2)}) collective-permute-start(bf16[128,512]{1,0:T(8,128)(2,1)S(1)} %add_convert_fusion.1), channel_id=1, source_target_pairs={{0,128},{128,256},{256,384},{384,0},{1,129},{129,257},{257,385},{3... | collective-permute-start | bytes 393224 | tf_op jit(solution)/shard_map/ppermute | solution.py:128
  75.0 9.4 %all-gather.3.cloned.1.call-done = bf16[3072,512]{1,0:T(8,128)(2,1)} async-done(((bf16[384,512]{1,0:T(8,128)(2,1)}), bf16[3072,512]{1,0:T(8,128)(2,1)}) %all-gather.3.cloned.1.call-update) | async-done | bytes 3145744 | tf_op jit(solution)/shard_map/all_gather | solution.py:153
  84.4 5.5 %shard_map.113 = (bf16[128,2048]{1,0:T(8,128)(2,1)}, f32[128,512]{1,0:T(8,128)}, bf16[128,2560]{1,0:T(8,128)(2,1)}) custom-call(s32[3]{0:T(128)} %pad_add_fusion.place, bf16[128,4096]{1,0:T(8,128)(2,1)} %tok.3, bf16[128,512]{1,0:T(8,128)(2,1)} %cot.5, bf16[128,2560]{1,0:T(8,128)(2,1)} %copy-done.1, bf16[8,384,512]{2,1,0:T(8,128)(2,1)} %bitcast.10), custom_call_target="tpu_custom_call" | custom-call | flops 1073741824 | bytes 6422528 | tf_op jit(solution)/shard_map/pallas_call | solution.py:33
  89.9 3.6 %collective-permute-start.7 = (bf16[128,2560]{1,0:T(8,128)(2,1)}, bf16[128,2560]{1,0:T(8,128)(2,1)S(1)}, u32[]{:S(2)}, u32[]{:S(2)}) collective-permute-start(bf16[128,2560]{1,0:T(8,128)(2,1)} %get-tuple-element.41), channel_id=1, source_target_pairs={{0,1},{1,0},{2,3},{3,2},{4,5},{5,4},{6,7},{7,6},{8,9},{9,8},{10,11... | collective-permute-start | bytes 1966088 | tf_op jit(solution)/shard_map/ppermute | solution.py:172
  93.6 1.0 copy-done
  94.5 4.4 %shard_map.112 = (f32[256,512]{1,0:T(8,128)}, bf16[256,512]{1,0:T(8,128)(2,1)}) custom-call(s32[3]{0:T(128)} %pad_add_fusion.place, bf16[8,128,512]{2,1,0:T(8,128)(2,1)} %copy-done, bf16[8,384,512]{2,1,0:T(8,128)(2,1)} %bitcast.11), custom_call_target="tpu_custom_call" | custom-call | flops 536870912 | bytes 4980736 | tf_op jit(solution)/shard_map/pallas_call | solution.py:33
  99.0 2.2 %collective-permute-start.6 = (bf16[256,512]{1,0:T(8,128)(2,1)}, bf16[256,512]{1,0:T(8,128)(2,1)S(1)}, u32[]{:S(2)}, u32[]{:S(2)}) collective-permute-start(bf16[256,512]{1,0:T(8,128)(2,1)} %get-tuple-element.37), channel_id=1, source_target_pairs={{0,1},{1,0},{2,3},{3,2},{4,5},{5,4},{6,7},{7,6},{8,9},{9,8},{10,11... | collective-permute-start | bytes 786440 | tf_op jit(solution)/shard_map/ppermute | solution.py:177
  101.2 1.9 %collective-permute-start.8 = (bf16[128,512]{1,0:T(8,128)(2,1)S(1)}, bf16[128,512]{1,0:T(8,128)(2,1)S(1)}, u32[]{:S(2)}, u32[]{:S(2)}) collective-permute-start(bf16[128,512]{1,0:T(8,128)(2,1)S(1)} %add_convert_fusion.half_sum), channel_id=1, source_target_pairs={{0,16},{16,0},{1,17},{17,1},{2,18},{18,2},{3,19},{19,3},{4,20},{20... | collective-permute-start | bytes 393224 | tf_op jit(solution)/shard_map/ppermute | solution.py:178
  103.1 6.5 %collective-permute-done.7.returned = bf16[128,2560]{1,0:T(8,128)(2,1)S(1)} collective-permute-done((bf16[128,2560]{1,0:T(8,128)(2,1)}, bf16[128,2560]{1,0:T(8,128)(2,1)S(1)}, u32[]{:S(2)}, u32[]{:S(2)}) %collective-permute-start.7) | collective-permute-done | bytes 655392 | tf_op jit(solution)/shard_map/ppermute | solution.py:172
  110.5 3.1 %shard_map.114 = (bf16[128,512]{1,0:T(8,128)(2,1)}, bf16[128,4096]{1,0:T(8,128)(2,1)}) custom-call(s32[3]{0:T(128)} %pad_add_fusion.place, bf16[128,2048]{1,0:T(8,128)(2,1)} %get-tuple-element.39.own, f32[128,512]{1,0:T(8,128)} %get-tuple-element.40.ahead, bf16[128,2560]{1,0:T(8,128)(2,1)} %copy-done.2), custom_call_target="tpu_custom_call" | custom-call | bytes 2621440 | tf_op jit(solution)/shard_map/pallas_call | solution.py:33
  114.4 3.9 %shard_map.115 = (f32[256,512]{1,0:T(8,128)}, bf16[256,512]{1,0:T(8,128)(2,1)}, bf16[256,512]{1,0:T(8,128)(2,1)}) custom-call(s32[3]{0:T(128)} %pad_add_fusion.place, f32[256,512]{1,0:T(8,128)} %get-tuple-element.45.keep, bf16[256,512]{1,0:T(8,128)(2,1)} %copy-done.4, f32[256,512]{1,0:T(8,128)} %bitcast.13, bf16[256,512]{1,0:T(8,128)(2,1)} %bitcast.14, ...), custom_call_target="tpu_custom_call" | custom-call | flops 5242880 | bytes 3670016 | tf_op jit(solution)/shard_map/pallas_call | solution.py:33
  (24 shorter events, 4.3 us)
Async XLA Ops:
  7.2 77.3 %all-gather.3.cloned.1.call-start = ((), (), s32[]{:S(2)}) async-start(), calls=%async_computation.1 | async-start | bytes 3538944 | tf_op jit(solution)/shard_map/all_gather | solution.py:153
  13.0 19.2 %collective-permute-start.1 = (bf16[128,2560]{1,0:T(8,128)(2,1)}, bf16[128,2560]{1,0:T(8,128)(2,1)S(1)}, u32[]{:S(2)}, u32[]{:S(2)}) collective-permute-start(bf16[128,2560]{1,0:T(8,128)(2,1)} %get-tuple-element.29), channel_id=1, source_target_pairs={{0,1},{1,0},{2,3},{3,2},{4,5},{5,4},{6,7},{7,6},{8,9},{9,8},{10,11... | collective-permute-start | bytes 1966088 | tf_op jit(solution)/shard_map/ppermute | solution.py:157
  18.2 3.2 %collective-permute-start = (bf16[128,512]{1,0:T(8,128)(2,1)S(1)}, bf16[128,512]{1,0:T(8,128)(2,1)S(1)}, u32[]{:S(2)}, u32[]{:S(2)}) collective-permute-start(bf16[128,512]{1,0:T(8,128)(2,1)S(1)} %constant_dynamic-slice_fusion), channel_id=1, source_target_pairs={{0,16},{16,0},{1,17},{17,1},{2,18},{18,2},{3,19},{19,3},{4,20},{20... | collective-permute-start | bytes 393224 | tf_op jit(solution)/shard_map/ppermute | solution.py:135
  32.2 52.3 %copy-start.1 = (bf16[128,2560]{1,0:T(8,128)(2,1)}, bf16[128,2560]{1,0:T(8,128)(2,1)S(1)}, u32[]{:S(2)}) copy-start(bf16[128,2560]{1,0:T(8,128)(2,1)S(1)} %collective-permute-done.1.got) | copy-start | bytes 1966084
  32.2 8.4 %collective-permute-start.2 = (bf16[128,512]{1,0:T(8,128)(2,1)S(1)}, bf16[128,512]{1,0:T(8,128)(2,1)S(1)}, u32[]{:S(2)}, u32[]{:S(2)}) collective-permute-start(bf16[128,512]{1,0:T(8,128)(2,1)S(1)} %add_convert_fusion.4), channel_id=1, source_target_pairs={{0,64},{32,96},{64,0},{96,32},{1,65},{33,97},{65,1},{97,33},{2,66}... | collective-permute-start | bytes 393224 | tf_op jit(solution)/shard_map/ppermute | solution.py:128
  40.6 53.0 %all-to-all-start = ((bf16[8,128,512]{2,1,0:T(8,128)(2,1)}), bf16[8,128,512]{2,1,0:T(8,128)(2,1)S(1)}, u32[]{:S(2)}, u32[]{:S(2)}) async-start(bf16[8,128,512]{2,1,0:T(8,128)(2,1)} %get-tuple-element.32), calls=%async_computation | async-start | bytes 2097152 | tf_op jit(solution)/shard_map/all_to_all | solution.py:163
  47.9 8.1 %collective-permute-start.3 = (bf16[128,512]{1,0:T(8,128)(2,1)S(1)}, bf16[128,512]{1,0:T(8,128)(2,1)S(1)}, u32[]{:S(2)}, u32[]{:S(2)}) collective-permute-start(bf16[128,512]{1,0:T(8,128)(2,1)S(1)} %add_convert_fusion.3), channel_id=1, source_target_pairs={{0,32},{32,64},{64,96},{96,0},{1,33},{33,65},{65,97},{97,1},{2,34}... | collective-permute-start | bytes 393224 | tf_op jit(solution)/shard_map/ppermute | solution.py:128
  56.0 14.1 %collective-permute-start.4 = (bf16[128,512]{1,0:T(8,128)(2,1)S(1)}, bf16[128,512]{1,0:T(8,128)(2,1)S(1)}, u32[]{:S(2)}, u32[]{:S(2)}) collective-permute-start(bf16[128,512]{1,0:T(8,128)(2,1)S(1)} %add_convert_fusion.2), channel_id=1, source_target_pairs={{0,256},{128,384},{256,0},{384,128},{1,257},{129,385},{257,1},{385... | collective-permute-start | bytes 393224 | tf_op jit(solution)/shard_map/ppermute | solution.py:128
  70.2 23.3 %collective-permute-start.5 = (bf16[128,512]{1,0:T(8,128)(2,1)S(1)}, bf16[128,512]{1,0:T(8,128)(2,1)S(1)}, u32[]{:S(2)}, u32[]{:S(2)}) collective-permute-start(bf16[128,512]{1,0:T(8,128)(2,1)S(1)} %add_convert_fusion.1), channel_id=1, source_target_pairs={{0,128},{128,256},{256,384},{384,0},{1,129},{129,257},{257,385},{3... | collective-permute-start | bytes 393224 | tf_op jit(solution)/shard_map/ppermute | solution.py:128
  89.9 19.8 %collective-permute-start.7 = (bf16[128,2560]{1,0:T(8,128)(2,1)}, bf16[128,2560]{1,0:T(8,128)(2,1)S(1)}, u32[]{:S(2)}, u32[]{:S(2)}) collective-permute-start(bf16[128,2560]{1,0:T(8,128)(2,1)} %get-tuple-element.41), channel_id=1, source_target_pairs={{0,1},{1,0},{2,3},{3,2},{4,5},{5,4},{6,7},{7,6},{8,9},{9,8},{10,11... | collective-permute-start | bytes 1966088 | tf_op jit(solution)/shard_map/ppermute | solution.py:172
  93.5 20.1 %copy-start.3 = (bf16[128,512]{1,0:T(8,128)(2,1)}, bf16[128,512]{1,0:T(8,128)(2,1)S(1)}, u32[]{:S(2)}) copy-start(bf16[128,512]{1,0:T(8,128)(2,1)S(1)} %add_convert_fusion.half_sum) | copy-start | bytes 393220
  93.5 1.0 copy-start
  99.0 14.7 %collective-permute-start.6 = (bf16[256,512]{1,0:T(8,128)(2,1)}, bf16[256,512]{1,0:T(8,128)(2,1)S(1)}, u32[]{:S(2)}, u32[]{:S(2)}) collective-permute-start(bf16[256,512]{1,0:T(8,128)(2,1)} %get-tuple-element.37), channel_id=1, source_target_pairs={{0,1},{1,0},{2,3},{3,2},{4,5},{5,4},{6,7},{7,6},{8,9},{9,8},{10,11... | collective-permute-start | bytes 786440 | tf_op jit(solution)/shard_map/ppermute | solution.py:177
  101.2 12.4 %collective-permute-start.8 = (bf16[128,512]{1,0:T(8,128)(2,1)S(1)}, bf16[128,512]{1,0:T(8,128)(2,1)S(1)}, u32[]{:S(2)}, u32[]{:S(2)}) collective-permute-start(bf16[128,512]{1,0:T(8,128)(2,1)S(1)} %add_convert_fusion.half_sum), channel_id=1, source_target_pairs={{0,16},{16,0},{1,17},{17,1},{2,18},{18,2},{3,19},{19,3},{4,20},{20... | collective-permute-start | bytes 393224 | tf_op jit(solution)/shard_map/ppermute | solution.py:178
  109.7 0.9 copy-start.2
  113.6 0.7 copy-start.4
  113.7 0.7 copy-start.5
Sparse Core Ops, SparseCore 0:
  10.7 73.7 all-gather.2

commit v4 on v3

--- a/solution.py
+++ b/solution.py
@@ -40,7 +40,7 @@
             out_specs=[whole(o.shape) for o in outs],
             scratch_shapes=scratch,
         ),
-        compiler_params=pltpu.CompilerParams(vmem_limit_bytes=56 * MIB),
+        compiler_params=pltpu.CompilerParams(vmem_limit_bytes=62 * MIB),
         cost_estimate=pl.CostEstimate(flops=flops, bytes_accessed=size, transcendentals=0),
     )(*([] if place is None else [place]), *args)
 
@@ -157,12 +157,11 @@
     got = lax.ppermute(other, "zl", PAIR)
 
     packed, other = lax.optimization_barrier((packed, other))
-    half_sum, got = lax.optimization_barrier((core_sum(packed), got))
-    half_sum = ring_step(half_sum, "x", 2)
-    blocks, half_sum = lax.optimization_barrier((blocks, half_sum))
     slab = lax.all_to_all(blocks, "y", 0, 0, tiled=True)
-    half_sum = ring_step(half_sum, "x", 1)
-    half_sum = ring_step(ring_step(half_sum, "zh", 2), "zh", 1)
+    half_sum = ring_step(ring_step(core_sum(packed), "x", 2), "x", 1)
+    half_sum = ring_step(half_sum, "zh", 2)
+    half_sum, slab = lax.optimization_barrier((half_sum, slab))
+    half_sum = ring_step(half_sum, "zh", 1)
     slab, half_sum = lax.optimization_barrier((slab, half_sum))
 
     own, ahead, to_return = run(

time: 126 us -> 119 us (0.944)
  the two profiles are of different devices: /device:TPU:24 before, /device:TPU:1 now
where the time goes in v4:
time: 119 us; the launch traced here: 118 us
  starting transfers between devices  43 us (36%)
  waiting for transfers between devices  37 us (31%)
  Pallas kernels  22 us (18%)
  between operations  14.2 us (12%)
    pallas_call x6, Pallas kernels, call(): pl.pallas_call(kernel, out_shape=outs, grid_spec=pltpu.PrefetchScalarGrid...  22 us
    ppermute x4, waiting for transfers between devices, ring_step(): return add_pair((total, lax.ppermute(total, axis, ring_shift(4, k))))  21.2 us
    ppermute x4, starting transfers between devices, ring_step(): return add_pair((total, lax.ppermute(total, axis, ring_shift(4, k))))  18 us
    all_to_all x1, starting transfers between devices, body(): slab = lax.all_to_all(blocks, 'y', 0, 0, tiled=True)  7.78 us
    all_gather x1, waiting for transfers between devices, body(): both = lax.all_gather(packed, 'y', axis=0, tiled=False)  7.62 us
    ppermute x1, waiting for transfers between devices, body(): returned = lax.ppermute(to_return, 'zl', PAIR)  4.83 us
    ppermute x1, starting transfers between devices, core_sum(): lax.ppermute(lax.dynamic_slice_in_dim(packed, (1 - core) * n, n), 'core',...  4.71 us
    ppermute x1, starting transfers between devices, body(): returned = lax.ppermute(to_return, 'zl', PAIR)  4 us
  transfers between devices with their start and end apart: 11, of which 7 were waited for; matrix products, arithmetic and copies ran while one was open for 1% of the time, Pallas kernels for 14%

profile of v4, /device:TPU:1, one launch (start us, length us, event | category | flops | bytes accessed | tf_op | source)
XLA Modules:
  0.0 117.8 jit_solution(9011264461606819694)
XLA Ops:
  7.2 1.8 %shard_map.110 = bf16[384,512]{1,0:T(8,128)(2,1)} custom-call(f32[256,512]{1,0:T(8,128)} %bitcast.12, bf16[128,512]{1,0:T(8,128)(2,1)} %cot.5), custom_call_target="tpu_custom_call" | custom-call | bytes 1048576 | tf_op jit(solution)/shard_map/pallas_call | solution.py:33
  9.7 3.2 %shard_map.111 = (bf16[8,128,512]{2,1,0:T(8,128)(2,1)}, bf16[128,2560]{1,0:T(8,128)(2,1)}) custom-call(s32[3]{0:T(128)} %pad_add_fusion.place, bf16[128,4096]{1,0:T(8,128)(2,1)} %tok.3, bf16[128,512]{1,0:T(8,128)(2,1)} %cot.5), custom_call_target="tpu_custom_call" | custom-call | bytes 2883584 | tf_op jit(solution)/shard_map/pallas_call | solution.py:33
  12.9 7.8 %all-to-all-start = ((bf16[8,128,512]{2,1,0:T(8,128)(2,1)}), bf16[8,128,512]{2,1,0:T(8,128)(2,1)S(1)}, u32[]{:S(2)}, u32[]{:S(2)}) async-start(bf16[8,128,512]{2,1,0:T(8,128)(2,1)} %get-tuple-element.28), calls=%async_computation | async-start | bytes 2097152 | tf_op jit(solution)/shard_map/all_to_all | solution.py:160
  20.8 4.7 %collective-permute-start = (bf16[128,512]{1,0:T(8,128)(2,1)S(1)}, bf16[128,512]{1,0:T(8,128)(2,1)S(1)}, u32[]{:S(2)}, u32[]{:S(2)}) collective-permute-start(bf16[128,512]{1,0:T(8,128)(2,1)S(1)} %constant_dynamic-slice_fusion), channel_id=1, source_target_pairs={{0,16},{16,0},{1,17},{17,1},{2,18},{18,2},{3,19},{19,3},{4,20},{20... | collective-permute-start | bytes 393224 | tf_op jit(solution)/shard_map/ppermute | solution.py:135
  25.5 1.0 collective-permute-done
  26.5 2.8 %collective-permute-start.1 = (bf16[128,512]{1,0:T(8,128)(2,1)S(1)}, bf16[128,512]{1,0:T(8,128)(2,1)S(1)}, u32[]{:S(2)}, u32[]{:S(2)}) collective-permute-start(bf16[128,512]{1,0:T(8,128)(2,1)S(1)} %add_convert_fusion.4), channel_id=1, source_target_pairs={{0,64},{32,96},{64,0},{96,32},{1,65},{33,97},{65,1},{97,33},{2,66}... | collective-permute-start | bytes 393224 | tf_op jit(solution)/shard_map/ppermute | solution.py:128
  29.3 5.3 %collective-permute-done.1 = bf16[128,512]{1,0:T(8,128)(2,1)S(1)} collective-permute-done((bf16[128,512]{1,0:T(8,128)(2,1)S(1)}, bf16[128,512]{1,0:T(8,128)(2,1)S(1)}, u32[]{:S(2)}, u32[]{:S(2)}) %collective-permute-start.1) | collective-permute-done | bytes 131104 | tf_op jit(solution)/shard_map/ppermute | solution.py:128
  34.6 1.9 %collective-permute-start.2 = (bf16[128,512]{1,0:T(8,128)(2,1)S(1)}, bf16[128,512]{1,0:T(8,128)(2,1)S(1)}, u32[]{:S(2)}, u32[]{:S(2)}) collective-permute-start(bf16[128,512]{1,0:T(8,128)(2,1)S(1)} %add_convert_fusion.3), channel_id=1, source_target_pairs={{0,32},{32,64},{64,96},{96,0},{1,33},{33,65},{65,97},{97,1},{2,34}... | collective-permute-start | bytes 393224 | tf_op jit(solution)/shard_map/ppermute | solution.py:128
  36.6 3.4 %collective-permute-start.6 = (bf16[128,2560]{1,0:T(8,128)(2,1)S(1)}, bf16[128,2560]{1,0:T(8,128)(2,1)}, u32[]{:S(2)}, u32[]{:S(2)}) collective-permute-start(bf16[128,2560]{1,0:T(8,128)(2,1)S(1)} %copy-done.5), channel_id=1, source_target_pairs={{0,1},{1,0},{2,3},{3,2},{4,5},{5,4},{6,7},{7,6},{8,9},{9,8},{10,11... | collective-permute-start | bytes 1966088 | tf_op jit(solution)/shard_map/ppermute | solution.py:157
  40.0 2.0 %collective-permute-done.2 = bf16[128,512]{1,0:T(8,128)(2,1)S(1)} collective-permute-done((bf16[128,512]{1,0:T(8,128)(2,1)S(1)}, bf16[128,512]{1,0:T(8,128)(2,1)S(1)}, u32[]{:S(2)}, u32[]{:S(2)}) %collective-permute-start.2) | collective-permute-done | bytes 131104 | tf_op jit(solution)/shard_map/ppermute | solution.py:128
  42.0 8.8 %collective-permute-start.3 = (bf16[128,512]{1,0:T(8,128)(2,1)S(1)}, bf16[128,512]{1,0:T(8,128)(2,1)S(1)}, u32[]{:S(2)}, u32[]{:S(2)}) collective-permute-start(bf16[128,512]{1,0:T(8,128)(2,1)S(1)} %add_convert_fusion.2), channel_id=1, source_target_pairs={{0,256},{128,384},{256,0},{384,128},{1,257},{129,385},{257,1},{385... | collective-permute-start | bytes 393224 | tf_op jit(solution)/shard_map/ppermute | solution.py:128
  50.8 13.9 %collective-permute-done.3 = bf16[128,512]{1,0:T(8,128)(2,1)S(1)} collective-permute-done((bf16[128,512]{1,0:T(8,128)(2,1)S(1)}, bf16[128,512]{1,0:T(8,128)(2,1)S(1)}, u32[]{:S(2)}, u32[]{:S(2)}) %collective-permute-start.3) | collective-permute-done | bytes 131104 | tf_op jit(solution)/shard_map/ppermute | solution.py:128
  64.7 4.5 %collective-permute-start.4 = (bf16[128,512]{1,0:T(8,128)(2,1)S(1)}, bf16[128,512]{1,0:T(8,128)(2,1)S(1)}, u32[]{:S(2)}, u32[]{:S(2)}) collective-permute-start(bf16[128,512]{1,0:T(8,128)(2,1)S(1)} %add_convert_fusion.1), channel_id=1, source_target_pairs={{0,128},{128,256},{256,384},{384,0},{1,129},{129,257},{257,385},{3... | collective-permute-start | bytes 393224 | tf_op jit(solution)/shard_map/ppermute | solution.py:128
  69.3 7.6 %all-gather.3.cloned.1.call-done = bf16[3072,512]{1,0:T(8,128)(2,1)} async-done(((bf16[384,512]{1,0:T(8,128)(2,1)}), bf16[3072,512]{1,0:T(8,128)(2,1)}) %all-gather.3.cloned.1.call-update) | async-done | bytes 3145744 | tf_op jit(solution)/shard_map/all_gather | solution.py:153
  76.9 5.5 %shard_map.113 = (bf16[128,2048]{1,0:T(8,128)(2,1)}, f32[128,512]{1,0:T(8,128)}, bf16[128,2560]{1,0:T(8,128)(2,1)}) custom-call(s32[3]{0:T(128)} %pad_add_fusion.place, bf16[128,4096]{1,0:T(8,128)(2,1)} %tok.3, bf16[128,512]{1,0:T(8,128)(2,1)} %cot.5, bf16[128,2560]{1,0:T(8,128)(2,1)} %collective-permute-done.6.got, bf16[8,384,512]{2,1,0:T(8,128)(2,1)} %bitcast.10), custom_call_target="tpu_custom_call" | custom-call | flops 1073741824 | bytes 6422528 | tf_op jit(solution)/shard_map/pallas_call | solution.py:33
  82.3 4.0 %collective-permute-start.7 = (bf16[128,2560]{1,0:T(8,128)(2,1)}, bf16[128,2560]{1,0:T(8,128)(2,1)}, u32[]{:S(2)}, u32[]{:S(2)}) collective-permute-start(bf16[128,2560]{1,0:T(8,128)(2,1)} %get-tuple-element.37), channel_id=1, source_target_pairs={{0,1},{1,0},{2,3},{3,2},{4,5},{5,4},{6,7},{7,6},{8,9},{9,8},{10,11... | collective-permute-start | bytes 1966088 | tf_op jit(solution)/shard_map/ppermute | solution.py:171
  86.4 4.4 %shard_map.112 = (f32[256,512]{1,0:T(8,128)}, bf16[256,512]{1,0:T(8,128)(2,1)}) custom-call(s32[3]{0:T(128)} %pad_add_fusion.place, bf16[8,128,512]{2,1,0:T(8,128)(2,1)} %copy-done, bf16[8,384,512]{2,1,0:T(8,128)(2,1)} %bitcast.11), custom_call_target="tpu_custom_call" | custom-call | flops 536870912 | bytes 4980736 | tf_op jit(solution)/shard_map/pallas_call | solution.py:33
  90.9 1.9 %collective-permute-start.5 = (bf16[256,512]{1,0:T(8,128)(2,1)}, bf16[256,512]{1,0:T(8,128)(2,1)S(1)}, u32[]{:S(2)}, u32[]{:S(2)}) collective-permute-start(bf16[256,512]{1,0:T(8,128)(2,1)} %get-tuple-element.34), channel_id=1, source_target_pairs={{0,1},{1,0},{2,3},{3,2},{4,5},{5,4},{6,7},{7,6},{8,9},{9,8},{10,11... | collective-permute-start | bytes 786440 | tf_op jit(solution)/shard_map/ppermute | solution.py:176
  92.8 3.2 %collective-permute-start.8 = (bf16[128,512]{1,0:T(8,128)(2,1)S(1)}, bf16[128,512]{1,0:T(8,128)(2,1)S(1)}, u32[]{:S(2)}, u32[]{:S(2)}) collective-permute-start(bf16[128,512]{1,0:T(8,128)(2,1)S(1)} %add_convert_fusion.half_sum), channel_id=1, source_target_pairs={{0,16},{16,0},{1,17},{17,1},{2,18},{18,2},{3,19},{19,3},{4,20},{20... | collective-permute-start | bytes 393224 | tf_op jit(solution)/shard_map/ppermute | solution.py:177
  95.9 4.8 %collective-permute-done.7.returned = bf16[128,2560]{1,0:T(8,128)(2,1)} collective-permute-done((bf16[128,2560]{1,0:T(8,128)(2,1)}, bf16[128,2560]{1,0:T(8,128)(2,1)}, u32[]{:S(2)}, u32[]{:S(2)}) %collective-permute-start.7) | collective-permute-done | bytes 655392 | tf_op jit(solution)/shard_map/ppermute | solution.py:171
  100.8 3.1 %shard_map.114 = (bf16[128,512]{1,0:T(8,128)(2,1)}, bf16[128,4096]{1,0:T(8,128)(2,1)}) custom-call(s32[3]{0:T(128)} %pad_add_fusion.place, bf16[128,2048]{1,0:T(8,128)(2,1)} %get-tuple-element.35.own, f32[128,512]{1,0:T(8,128)} %get-tuple-element.36.ahead, bf16[128,2560]{1,0:T(8,128)(2,1)} %collective-permute-done.7.returned), custom_call_target="tpu_custom_call" | custom-call | bytes 2621440 | tf_op jit(solution)/shard_map/pallas_call | solution.py:33
  103.9 2.4 %collective-permute-done.5.sent = bf16[256,512]{1,0:T(8,128)(2,1)S(1)} collective-permute-done((bf16[256,512]{1,0:T(8,128)(2,1)}, bf16[256,512]{1,0:T(8,128)(2,1)S(1)}, u32[]{:S(2)}, u32[]{:S(2)}) %collective-permute-start.5) | collective-permute-done | bytes 262176 | tf_op jit(solution)/shard_map/ppermute | solution.py:176
  106.3 0.7 copy-done.3
  107.0 3.9 %shard_map.115 = (f32[256,512]{1,0:T(8,128)}, bf16[256,512]{1,0:T(8,128)(2,1)}, bf16[256,512]{1,0:T(8,128)(2,1)}) custom-call(s32[3]{0:T(128)} %pad_add_fusion.place, f32[256,512]{1,0:T(8,128)} %get-tuple-element.41.keep, bf16[256,512]{1,0:T(8,128)(2,1)} %copy-done.3, f32[256,512]{1,0:T(8,128)} %bitcast.13, bf16[256,512]{1,0:T(8,128)(2,1)} %bitcast.14, ...), custom_call_target="tpu_custom_call" | custom-call | flops 5242880 | bytes 3670016 | tf_op jit(solution)/shard_map/pallas_call | solution.py:33
  (24 shorter events, 1.0 us)
Async XLA Ops:
  7.2 69.7 %all-gather.3.cloned.1.call-start = ((), (), s32[]{:S(2)}) async-start(), calls=%async_computation.1 | async-start | bytes 3538944 | tf_op jit(solution)/shard_map/all_gather | solution.py:153
  9.1 11.7 %copy-start.1 = (bf16[384,512]{1,0:T(8,128)(2,1)S(1)}, bf16[384,512]{1,0:T(8,128)(2,1)}, u32[]{:S(2)}) copy-start(bf16[384,512]{1,0:T(8,128)(2,1)} %shard_map.110) | copy-start | bytes 1179652
  12.9 23.6 %copy-start.5 = (bf16[128,2560]{1,0:T(8,128)(2,1)S(1)}, bf16[128,2560]{1,0:T(8,128)(2,1)}, u32[]{:S(2)}) copy-start(bf16[128,2560]{1,0:T(8,128)(2,1)} %get-tuple-element.26) | copy-start | bytes 1966084
  12.9 51.8 %all-to-all-start = ((bf16[8,128,512]{2,1,0:T(8,128)(2,1)}), bf16[8,128,512]{2,1,0:T(8,128)(2,1)S(1)}, u32[]{:S(2)}, u32[]{:S(2)}) async-start(bf16[8,128,512]{2,1,0:T(8,128)(2,1)} %get-tuple-element.28), calls=%async_computation | async-start | bytes 2097152 | tf_op jit(solution)/shard_map/all_to_all | solution.py:160
  20.8 5.7 %collective-permute-start = (bf16[128,512]{1,0:T(8,128)(2,1)S(1)}, bf16[128,512]{1,0:T(8,128)(2,1)S(1)}, u32[]{:S(2)}, u32[]{:S(2)}) collective-permute-start(bf16[128,512]{1,0:T(8,128)(2,1)S(1)} %constant_dynamic-slice_fusion), channel_id=1, source_target_pairs={{0,16},{16,0},{1,17},{17,1},{2,18},{18,2},{3,19},{19,3},{4,20},{20... | collective-permute-start | bytes 393224 | tf_op jit(solution)/shard_map/ppermute | solution.py:135
  26.5 8.1 %collective-permute-start.1 = (bf16[128,512]{1,0:T(8,128)(2,1)S(1)}, bf16[128,512]{1,0:T(8,128)(2,1)S(1)}, u32[]{:S(2)}, u32[]{:S(2)}) collective-permute-start(bf16[128,512]{1,0:T(8,128)(2,1)S(1)} %add_convert_fusion.4), channel_id=1, source_target_pairs={{0,64},{32,96},{64,0},{96,32},{1,65},{33,97},{65,1},{97,33},{2,66}... | collective-permute-start | bytes 393224 | tf_op jit(solution)/shard_map/ppermute | solution.py:128
  34.6 7.3 %collective-permute-start.2 = (bf16[128,512]{1,0:T(8,128)(2,1)S(1)}, bf16[128,512]{1,0:T(8,128)(2,1)S(1)}, u32[]{:S(2)}, u32[]{:S(2)}) collective-permute-start(bf16[128,512]{1,0:T(8,128)(2,1)S(1)} %add_convert_fusion.3), channel_id=1, source_target_pairs={{0,32},{32,64},{64,96},{96,0},{1,33},{33,65},{65,97},{97,1},{2,34}... | collective-permute-start | bytes 393224 | tf_op jit(solution)/shard_map/ppermute | solution.py:128
  36.6 32.7 %collective-permute-start.6 = (bf16[128,2560]{1,0:T(8,128)(2,1)S(1)}, bf16[128,2560]{1,0:T(8,128)(2,1)}, u32[]{:S(2)}, u32[]{:S(2)}) collective-permute-start(bf16[128,2560]{1,0:T(8,128)(2,1)S(1)} %copy-done.5), channel_id=1, source_target_pairs={{0,1},{1,0},{2,3},{3,2},{4,5},{5,4},{6,7},{7,6},{8,9},{9,8},{10,11... | collective-permute-start | bytes 1966088 | tf_op jit(solution)/shard_map/ppermute | solution.py:157
  42.0 22.7 %collective-permute-start.3 = (bf16[128,512]{1,0:T(8,128)(2,1)S(1)}, bf16[128,512]{1,0:T(8,128)(2,1)S(1)}, u32[]{:S(2)}, u32[]{:S(2)}) collective-permute-start(bf16[128,512]{1,0:T(8,128)(2,1)S(1)} %add_convert_fusion.2), channel_id=1, source_target_pairs={{0,256},{128,384},{256,0},{384,128},{1,257},{129,385},{257,1},{385... | collective-permute-start | bytes 393224 | tf_op jit(solution)/shard_map/ppermute | solution.py:128
  64.7 21.7 %copy-start = (bf16[8,128,512]{2,1,0:T(8,128)(2,1)}, bf16[8,128,512]{2,1,0:T(8,128)(2,1)S(1)}, u32[]{:S(2)}) copy-start(bf16[8,128,512]{2,1,0:T(8,128)(2,1)S(1)} %all-to-all-done.slab) | copy-start | bytes 3145732
  64.7 21.6 %collective-permute-start.4 = (bf16[128,512]{1,0:T(8,128)(2,1)S(1)}, bf16[128,512]{1,0:T(8,128)(2,1)S(1)}, u32[]{:S(2)}, u32[]{:S(2)}) collective-permute-start(bf16[128,512]{1,0:T(8,128)(2,1)S(1)} %add_convert_fusion.1), channel_id=1, source_target_pairs={{0,128},{128,256},{256,384},{384,0},{1,129},{129,257},{257,385},{3... | collective-permute-start | bytes 393224 | tf_op jit(solution)/shard_map/ppermute | solution.py:128
  82.3 18.4 %collective-permute-start.7 = (bf16[128,2560]{1,0:T(8,128)(2,1)}, bf16[128,2560]{1,0:T(8,128)(2,1)}, u32[]{:S(2)}, u32[]{:S(2)}) collective-permute-start(bf16[128,2560]{1,0:T(8,128)(2,1)} %get-tuple-element.37), channel_id=1, source_target_pairs={{0,1},{1,0},{2,3},{3,2},{4,5},{5,4},{6,7},{7,6},{8,9},{9,8},{10,11... | collective-permute-start | bytes 1966088 | tf_op jit(solution)/shard_map/ppermute | solution.py:171
  86.4 19.9 %copy-start.2 = (bf16[128,512]{1,0:T(8,128)(2,1)}, bf16[128,512]{1,0:T(8,128)(2,1)S(1)}, u32[]{:S(2)}) copy-start(bf16[128,512]{1,0:T(8,128)(2,1)S(1)} %add_convert_fusion.half_sum) | copy-start | bytes 393220
  90.9 15.4 %collective-permute-start.5 = (bf16[256,512]{1,0:T(8,128)(2,1)}, bf16[256,512]{1,0:T(8,128)(2,1)S(1)}, u32[]{:S(2)}, u32[]{:S(2)}) collective-permute-start(bf16[256,512]{1,0:T(8,128)(2,1)} %get-tuple-element.34), channel_id=1, source_target_pairs={{0,1},{1,0},{2,3},{3,2},{4,5},{5,4},{6,7},{7,6},{8,9},{9,8},{10,11... | collective-permute-start | bytes 786440 | tf_op jit(solution)/shard_map/ppermute | solution.py:176
  92.8 13.5 %collective-permute-start.8 = (bf16[128,512]{1,0:T(8,128)(2,1)S(1)}, bf16[128,512]{1,0:T(8,128)(2,1)S(1)}, u32[]{:S(2)}, u32[]{:S(2)}) collective-permute-start(bf16[128,512]{1,0:T(8,128)(2,1)S(1)} %add_convert_fusion.half_sum), channel_id=1, source_target_pairs={{0,16},{16,0},{1,17},{17,1},{2,18},{18,2},{3,19},{19,3},{4,20},{20... | collective-permute-start | bytes 393224 | tf_op jit(solution)/shard_map/ppermute | solution.py:177
  106.3 0.7 copy-start.3
  106.3 0.7 copy-start.4
Sparse Core Ops, SparseCore 0:
  10.7 66.1 all-gather.2

commit v5 on v4

--- a/solution.py
+++ b/solution.py
@@ -45,6 +45,10 @@
     )(*([] if place is None else [place]), *args)
 
 
+def cut(array, shape, indices):
+    return [(array, pl.BlockSpec(shape, functools.partial(lambda index, *_: index, index))) for index in indices]
+
+
 def lanes(index):
     return pl.ds(pl.multiple_of(index * ROWS, ROWS), ROWS)
 
@@ -54,20 +58,24 @@
     packed[ROWS:] = cot[...]
 
 
-def split_kernel(place, tok, cot, blocks, other):
+def split_kernel(place, cot, *refs):
+    tok, (blocks, other) = refs[:4], refs[4:]
     other[:, YS * ROWS :] = cot[...]
     for f in range(YS):
-        blocks[f] = tok[:, 2 * f * ROWS : (2 * f + 2) * ROWS]
-        other[:, f * ROWS : (f + 1) * ROWS] = tok[:, lanes(2 * f + 1 - place[1])]
-
-
-def product_kernel(factor, place, tok, cot, got, both, own, ahead, to_return):
-    cots = jnp.concatenate([cot[...], got[:, YS * ROWS :]], 0)
+        i, j = divmod(f, 2)
+        blocks[f] = tok[i][:, 2 * j * ROWS : (2 * j + 2) * ROWS]
+        other[:, f * ROWS : (f + 1) * ROWS] = tok[i][:, lanes(2 * j + 1 - place[1])]
+
+
+def product_kernel(factor, place, cot, *refs):
+    tok, got, both, (own, ahead, to_return) = refs[:4], refs[4:9], refs[9:13], refs[13:]
+    cots = jnp.concatenate([cot[...], got[4][...]], 0)
     total = None
     for f in range(YS):
-        w = both[f, :ROWS]
+        i, j = divmod(f, 2)
+        w = both[i][j]
         cols = slice(f * ROWS, (f + 1) * ROWS)
-        x = jnp.concatenate([tok[:, lanes(2 * f + place[1])], got[:, cols]], 0)
+        x = jnp.concatenate([tok[i][:, lanes(2 * j + place[1])], got[i][:, j * ROWS : (j + 1) * ROWS]], 0)
         part = jnp.dot(x, w, preferred_element_type=F32)
         total = part if f == 0 else total + part
         ig = lax.dot_general(cots, w, (((1,), (1,)), ((), ())), preferred_element_type=F32)
@@ -87,14 +95,15 @@
     projected[...] = (ahead[...] + returned[:, YS * ROWS :].astype(F32)).astype(BF16)
 
 
-def grad_kernel(factor, place, slab, both, keep, send):
+def grad_kernel(factor, place, *refs):
+    slab, cots, (keep, send) = refs[:4], refs[4:8], refs[8:]
     for out, col in ((send, 1 - place[1]), (keep, place[1])):
         total = None
-        for f in range(0, YS, 2):
-            x = slab[f : f + 2, :, lanes(col)].reshape(2 * TOK, ROWS)
-            c = jnp.concatenate([both[f, ROWS:], both[f + 1, ROWS:]], 0)
+        for i in range(4):
+            x = slab[i][:, :, lanes(col)].reshape(2 * TOK, ROWS)
+            c = cots[i][...].reshape(2 * TOK, KV)
             part = lax.dot_general(x, c, (((0,), (0,)), ((), ())), preferred_element_type=F32)
-            total = part if f == 0 else total + part
+            total = part if i == 0 else total + part
         out[...] = (total * factor).astype(out.dtype)
 
 
@@ -142,8 +151,12 @@
     half = YS * ROWS
     flops = 2 * 2 * TOK * half * KV
 
-    def run(kernel, args, outs, cost=0):
-        return call(kernel, place, args, [whole(a.shape) for a in args], outs, cost)
+    def run(kernel, args, outs, cost=0, cuts=()):
+        specs = [whole(a.shape) for a in args] + [s for _, s in cuts]
+        return call(kernel, place, args + [a for a, _ in cuts], specs, outs, cost)
+
+    fours = range(4)
+    token_cuts = cut(tokens, (TOK, 4 * ROWS), [(0, i) for i in fours])
 
     (packed,) = call(
         pack_kernel, None, [weight[0], cotangent],
@@ -152,7 +165,7 @@
     )
     both = lax.all_gather(packed, "y", axis=0, tiled=False)
     blocks, other = run(
-        split_kernel, [tokens, cotangent], [sds((YS, TOK, 2 * ROWS), BF16), sds((TOK, half + KV), BF16)]
+        split_kernel, [cotangent], [sds((YS, TOK, 2 * ROWS), BF16), sds((TOK, half + KV), BF16)], 0, token_cuts
     )
     got = lax.ppermute(other, "zl", PAIR)
 
@@ -165,12 +178,14 @@
     slab, half_sum = lax.optimization_barrier((slab, half_sum))
 
     own, ahead, to_return = run(
-        functools.partial(product_kernel, factor), [tokens, cotangent, got, both],
+        functools.partial(product_kernel, factor), [cotangent],
         [sds((TOK, half), BF16), sds((TOK, KV), F32), sds((TOK, half + KV), BF16)], 2 * flops,
+        token_cuts + cut(got, (TOK, KV), [(0, i) for i in range(5)]) + cut(both, (2, ROWS, KV), [(i, 0, 0) for i in fours]),
     )
     returned = lax.ppermute(to_return, "zl", PAIR)
     keep, send = run(
-        functools.partial(grad_kernel, factor), [slab, both], [sds((ROWS, KV), F32), sds((ROWS, KV), BF16)], flops
+        functools.partial(grad_kernel, factor), [], [sds((ROWS, KV), F32), sds((ROWS, KV), BF16)], flops,
+        cut(slab, (2, TOK, 2 * ROWS), [(i, 0, 0) for i in fours]) + cut(both, (2, TOK, KV), [(i, 2, 0) for i in fours]),
     )
     send, half_sum = lax.optimization_barrier((send, half_sum))
     sent = lax.ppermute(send, "zl", PAIR)

time: 119 us -> 118 us (level)
  transfers between devices with their start and end apart: 11 -> 11, of which waited for: 7 -> 7; matrix products, arithmetic and copies ran while one was open for 1% -> 1% of each run, Pallas kernels for 14% -> 13%
where the time goes in v5:
time: 118 us; the launch traced here: 117 us
  starting transfers between devices  43 us (36%)
  waiting for transfers between devices  36.9 us (31%)
  Pallas kernels  21 us (18%)
  between operations  14.2 us (12%)
  local copies, waits for them, and re-layouts  1.63 us (1%)
    ppermute x4, waiting for transfers between devices, ring_step(): return add_pair((total, lax.ppermute(total, axis, ring_shift(4, k))))  21.2 us
    pallas_call x6, Pallas kernels, call(): pl.pallas_call(kernel, out_shape=outs, grid_spec=pltpu.PrefetchScalarGrid...  21 us
    ppermute x4, starting transfers between devices, ring_step(): return add_pair((total, lax.ppermute(total, axis, ring_shift(4, k))))  18 us
    all_to_all x1, starting transfers between devices, body(): slab = lax.all_to_all(blocks, 'y', 0, 0, tiled=True)  7.78 us
    all_gather x1, waiting for transfers between devices, body(): both = lax.all_gather(packed, 'y', axis=0, tiled=False)  7.61 us
    ppermute x1, waiting for transfers between devices, body(): returned = lax.ppermute(to_return, 'zl', PAIR)  5.43 us
    ppermute x1, starting transfers between devices, core_sum(): lax.ppermute(lax.dynamic_slice_in_dim(packed, (1 - core) * n, n), 'core',...  4.71 us
    ppermute x1, starting transfers between devices, body(): returned = lax.ppermute(to_return, 'zl', PAIR)  4.01 us
  transfers between devices with their start and end apart: 11, of which 7 were waited for; matrix products, arithmetic and copies ran while one was open for 1% of the time, Pallas kernels for 13%

profile of v5, /device:TPU:1, one launch (start us, length us, event | category | flops | bytes accessed | tf_op | source)
XLA Modules:
  0.0 117.5 jit_solution(18132139402447321495)
XLA Ops:
  7.2 1.8 %shard_map.110 = bf16[384,512]{1,0:T(8,128)(2,1)} custom-call(f32[256,512]{1,0:T(8,128)} %bitcast.18, bf16[128,512]{1,0:T(8,128)(2,1)} %cot.5), custom_call_target="tpu_custom_call" | custom-call | bytes 1048576 | tf_op jit(solution)/shard_map/pallas_call | solution.py:33
  9.7 3.3 %shard_map.111 = (bf16[8,128,512]{2,1,0:T(8,128)(2,1)}, bf16[128,2560]{1,0:T(8,128)(2,1)}) custom-call(s32[3]{0:T(128)} %pad_add_fusion.place, bf16[128,512]{1,0:T(8,128)(2,1)} %cot.5, bf16[128,4096]{1,0:T(8,128)(2,1)} %refs_3_.3, bf16[128,4096]{1,0:T(8,128)(2,1)} %refs_3_.3, bf16[128,4096]{1,0:T(8,128)(2,1)} %refs_3_.3, bf16[128,4096]{1,0:T(8,128)(2,1)} %refs_3_.3), custom_call_target="tpu_custom_call" | custom-call | bytes 6029312 | tf_op jit(solution)/shard_map/pallas_call | solution.py:33
  13.1 7.8 %all-to-all-start = ((bf16[8,128,512]{2,1,0:T(8,128)(2,1)}), bf16[8,128,512]{2,1,0:T(8,128)(2,1)S(1)}, u32[]{:S(2)}, u32[]{:S(2)}) async-start(bf16[8,128,512]{2,1,0:T(8,128)(2,1)} %get-tuple-element.28), calls=%async_computation | async-start | bytes 2097152 | tf_op jit(solution)/shard_map/all_to_all | solution.py:173
  20.9 4.7 %collective-permute-start = (bf16[128,512]{1,0:T(8,128)(2,1)S(1)}, bf16[128,512]{1,0:T(8,128)(2,1)S(1)}, u32[]{:S(2)}, u32[]{:S(2)}) collective-permute-start(bf16[128,512]{1,0:T(8,128)(2,1)S(1)} %constant_dynamic-slice_fusion), channel_id=1, source_target_pairs={{0,16},{16,0},{1,17},{17,1},{2,18},{18,2},{3,19},{19,3},{4,20},{20... | collective-permute-start | bytes 393224 | tf_op jit(solution)/shard_map/ppermute | solution.py:144
  25.6 1.0 collective-permute-done
  26.6 2.8 %collective-permute-start.1 = (bf16[128,512]{1,0:T(8,128)(2,1)S(1)}, bf16[128,512]{1,0:T(8,128)(2,1)S(1)}, u32[]{:S(2)}, u32[]{:S(2)}) collective-permute-start(bf16[128,512]{1,0:T(8,128)(2,1)S(1)} %add_convert_fusion.4), channel_id=1, source_target_pairs={{0,64},{32,96},{64,0},{96,32},{1,65},{33,97},{65,1},{97,33},{2,66}... | collective-permute-start | bytes 393224 | tf_op jit(solution)/shard_map/ppermute | solution.py:137
  29.4 5.3 %collective-permute-done.1 = bf16[128,512]{1,0:T(8,128)(2,1)S(1)} collective-permute-done((bf16[128,512]{1,0:T(8,128)(2,1)S(1)}, bf16[128,512]{1,0:T(8,128)(2,1)S(1)}, u32[]{:S(2)}, u32[]{:S(2)}) %collective-permute-start.1) | collective-permute-done | bytes 131104 | tf_op jit(solution)/shard_map/ppermute | solution.py:137
  34.8 1.9 %collective-permute-start.2 = (bf16[128,512]{1,0:T(8,128)(2,1)S(1)}, bf16[128,512]{1,0:T(8,128)(2,1)S(1)}, u32[]{:S(2)}, u32[]{:S(2)}) collective-permute-start(bf16[128,512]{1,0:T(8,128)(2,1)S(1)} %add_convert_fusion.3), channel_id=1, source_target_pairs={{0,32},{32,64},{64,96},{96,0},{1,33},{33,65},{65,97},{97,1},{2,34}... | collective-permute-start | bytes 393224 | tf_op jit(solution)/shard_map/ppermute | solution.py:137
  36.7 3.3 %collective-permute-start.6 = (bf16[128,2560]{1,0:T(8,128)(2,1)S(1)}, bf16[128,2560]{1,0:T(8,128)(2,1)S(1)}, u32[]{:S(2)}, u32[]{:S(2)}) collective-permute-start(bf16[128,2560]{1,0:T(8,128)(2,1)S(1)} %copy-done.7), channel_id=1, source_target_pairs={{0,1},{1,0},{2,3},{3,2},{4,5},{5,4},{6,7},{7,6},{8,9},{9,8},{10,11... | collective-permute-start | bytes 1966088 | tf_op jit(solution)/shard_map/ppermute | solution.py:170
  40.0 2.0 %collective-permute-done.2 = bf16[128,512]{1,0:T(8,128)(2,1)S(1)} collective-permute-done((bf16[128,512]{1,0:T(8,128)(2,1)S(1)}, bf16[128,512]{1,0:T(8,128)(2,1)S(1)}, u32[]{:S(2)}, u32[]{:S(2)}) %collective-permute-start.2) | collective-permute-done | bytes 131104 | tf_op jit(solution)/shard_map/ppermute | solution.py:137
  42.1 8.8 %collective-permute-start.3 = (bf16[128,512]{1,0:T(8,128)(2,1)S(1)}, bf16[128,512]{1,0:T(8,128)(2,1)S(1)}, u32[]{:S(2)}, u32[]{:S(2)}) collective-permute-start(bf16[128,512]{1,0:T(8,128)(2,1)S(1)} %add_convert_fusion.2), channel_id=1, source_target_pairs={{0,256},{128,384},{256,0},{384,128},{1,257},{129,385},{257,1},{385... | collective-permute-start | bytes 393224 | tf_op jit(solution)/shard_map/ppermute | solution.py:137
  50.9 13.9 %collective-permute-done.3 = bf16[128,512]{1,0:T(8,128)(2,1)S(1)} collective-permute-done((bf16[128,512]{1,0:T(8,128)(2,1)S(1)}, bf16[128,512]{1,0:T(8,128)(2,1)S(1)}, u32[]{:S(2)}, u32[]{:S(2)}) %collective-permute-start.3) | collective-permute-done | bytes 131104 | tf_op jit(solution)/shard_map/ppermute | solution.py:137
  64.8 4.5 %collective-permute-start.4 = (bf16[128,512]{1,0:T(8,128)(2,1)S(1)}, bf16[128,512]{1,0:T(8,128)(2,1)S(1)}, u32[]{:S(2)}, u32[]{:S(2)}) collective-permute-start(bf16[128,512]{1,0:T(8,128)(2,1)S(1)} %add_convert_fusion.1), channel_id=1, source_target_pairs={{0,128},{128,256},{256,384},{384,0},{1,129},{129,257},{257,385},{3... | collective-permute-start | bytes 393224 | tf_op jit(solution)/shard_map/ppermute | solution.py:137
  69.4 7.6 %all-gather.3.cloned.1.call-done = bf16[3072,512]{1,0:T(8,128)(2,1)} async-done(((bf16[384,512]{1,0:T(8,128)(2,1)}), bf16[3072,512]{1,0:T(8,128)(2,1)}) %all-gather.3.cloned.1.call-update) | async-done | bytes 3145744 | tf_op jit(solution)/shard_map/all_gather | solution.py:166
  77.0 5.1 %shard_map.113 = (bf16[128,2048]{1,0:T(8,128)(2,1)}, f32[128,512]{1,0:T(8,128)}, bf16[128,2560]{1,0:T(8,128)(2,1)}) custom-call(s32[3]{0:T(128)} %pad_add_fusion.place, bf16[128,512]{1,0:T(8,128)(2,1)} %cot.5, bf16[128,4096]{1,0:T(8,128)(2,1)} %refs_3_.3, bf16[128,4096]{1,0:T(8,128)(2,1)} %refs_3_.3, bf16[128,4096]{1,0:T(8,128)(2,1)} %refs_3_.3, ...), custom_call_target="tpu_custom_call" | custom-call | flops 1073741824 | bytes 21626880 | tf_op jit(solution)/shard_map/pallas_call | solution.py:33
  82.1 4.0 %collective-permute-start.7 = (bf16[128,2560]{1,0:T(8,128)(2,1)}, bf16[128,2560]{1,0:T(8,128)(2,1)S(1)}, u32[]{:S(2)}, u32[]{:S(2)}) collective-permute-start(bf16[128,2560]{1,0:T(8,128)(2,1)} %get-tuple-element.37), channel_id=1, source_target_pairs={{0,1},{1,0},{2,3},{3,2},{4,5},{5,4},{6,7},{7,6},{8,9},{9,8},{10,11... | collective-permute-start | bytes 1966088 | tf_op jit(solution)/shard_map/ppermute | solution.py:185
  86.1 3.7 %shard_map.112 = (f32[256,512]{1,0:T(8,128)}, bf16[256,512]{1,0:T(8,128)(2,1)}) custom-call(s32[3]{0:T(128)} %pad_add_fusion.place, bf16[8,128,512]{2,1,0:T(8,128)(2,1)} %copy-done, bf16[8,128,512]{2,1,0:T(8,128)(2,1)} %copy-done, bf16[8,128,512]{2,1,0:T(8,128)(2,1)} %copy-done, bf16[8,128,512]{2,1,0:T(8,128)(2,1)} %copy-done, ...), custom_call_target="tpu_custom_call" | custom-call | flops 536870912 | bytes 17563648 | tf_op jit(solution)/shard_map/pallas_call | solution.py:33
  89.9 1.9 %collective-permute-start.5 = (bf16[256,512]{1,0:T(8,128)(2,1)}, bf16[256,512]{1,0:T(8,128)(2,1)S(1)}, u32[]{:S(2)}, u32[]{:S(2)}) collective-permute-start(bf16[256,512]{1,0:T(8,128)(2,1)} %get-tuple-element.34), channel_id=1, source_target_pairs={{0,1},{1,0},{2,3},{3,2},{4,5},{5,4},{6,7},{7,6},{8,9},{9,8},{10,11... | collective-permute-start | bytes 786440 | tf_op jit(solution)/shard_map/ppermute | solution.py:191
  91.8 3.2 %collective-permute-start.8 = (bf16[128,512]{1,0:T(8,128)(2,1)S(1)}, bf16[128,512]{1,0:T(8,128)(2,1)S(1)}, u32[]{:S(2)}, u32[]{:S(2)}) collective-permute-start(bf16[128,512]{1,0:T(8,128)(2,1)S(1)} %add_convert_fusion.half_sum), channel_id=1, source_target_pairs={{0,16},{16,0},{1,17},{17,1},{2,18},{18,2},{3,19},{19,3},{4,20},{20... | collective-permute-start | bytes 393224 | tf_op jit(solution)/shard_map/ppermute | solution.py:192
  94.9 5.4 %collective-permute-done.7.returned = bf16[128,2560]{1,0:T(8,128)(2,1)S(1)} collective-permute-done((bf16[128,2560]{1,0:T(8,128)(2,1)}, bf16[128,2560]{1,0:T(8,128)(2,1)S(1)}, u32[]{:S(2)}, u32[]{:S(2)}) %collective-permute-start.7) | collective-permute-done | bytes 655392 | tf_op jit(solution)/shard_map/ppermute | solution.py:185
  100.4 0.9 copy-done.3
  101.2 3.1 %shard_map.114 = (bf16[128,512]{1,0:T(8,128)(2,1)}, bf16[128,4096]{1,0:T(8,128)(2,1)}) custom-call(s32[3]{0:T(128)} %pad_add_fusion.place, bf16[128,2048]{1,0:T(8,128)(2,1)} %get-tuple-element.35.own, f32[128,512]{1,0:T(8,128)} %get-tuple-element.36.ahead, bf16[128,2560]{1,0:T(8,128)(2,1)} %copy-done.3), custom_call_target="tpu_custom_call" | custom-call | bytes 2621440 | tf_op jit(solution)/shard_map/pallas_call | solution.py:33
  104.3 1.6 %collective-permute-done.5.sent = bf16[256,512]{1,0:T(8,128)(2,1)S(1)} collective-permute-done((bf16[256,512]{1,0:T(8,128)(2,1)}, bf16[256,512]{1,0:T(8,128)(2,1)S(1)}, u32[]{:S(2)}, u32[]{:S(2)}) %collective-permute-start.5) | collective-permute-done | bytes 262176 | tf_op jit(solution)/shard_map/ppermute | solution.py:191
  106.7 3.9 %shard_map.115 = (f32[256,512]{1,0:T(8,128)}, bf16[256,512]{1,0:T(8,128)(2,1)}, bf16[256,512]{1,0:T(8,128)(2,1)}) custom-call(s32[3]{0:T(128)} %pad_add_fusion.place, f32[256,512]{1,0:T(8,128)} %get-tuple-element.41.keep, bf16[256,512]{1,0:T(8,128)(2,1)} %copy-done.5, f32[256,512]{1,0:T(8,128)} %bitcast.19, bf16[256,512]{1,0:T(8,128)(2,1)} %bitcast.20, ...), custom_call_target="tpu_custom_call" | custom-call | flops 5242880 | bytes 3670016 | tf_op jit(solution)/shard_map/pallas_call | solution.py:33
  (28 shorter events, 1.7 us)
Async XLA Ops:
  7.2 69.8 %all-gather.3.cloned.1.call-start = ((), (), s32[]{:S(2)}) async-start(), calls=%async_computation.1 | async-start | bytes 3538944 | tf_op jit(solution)/shard_map/all_gather | solution.py:166
  9.7 11.1 %copy-start.2 = (bf16[384,512]{1,0:T(8,128)(2,1)S(1)}, bf16[384,512]{1,0:T(8,128)(2,1)}, u32[]{:S(2)}) copy-start(bf16[384,512]{1,0:T(8,128)(2,1)} %shard_map.110) | copy-start | bytes 1179652
  13.1 23.6 %copy-start.7 = (bf16[128,2560]{1,0:T(8,128)(2,1)S(1)}, bf16[128,2560]{1,0:T(8,128)(2,1)}, u32[]{:S(2)}) copy-start(bf16[128,2560]{1,0:T(8,128)(2,1)} %get-tuple-element.26) | copy-start | bytes 1966084
  13.1 51.8 %all-to-all-start = ((bf16[8,128,512]{2,1,0:T(8,128)(2,1)}), bf16[8,128,512]{2,1,0:T(8,128)(2,1)S(1)}, u32[]{:S(2)}, u32[]{:S(2)}) async-start(bf16[8,128,512]{2,1,0:T(8,128)(2,1)} %get-tuple-element.28), calls=%async_computation | async-start | bytes 2097152 | tf_op jit(solution)/shard_map/all_to_all | solution.py:173
  20.9 5.7 %collective-permute-start = (bf16[128,512]{1,0:T(8,128)(2,1)S(1)}, bf16[128,512]{1,0:T(8,128)(2,1)S(1)}, u32[]{:S(2)}, u32[]{:S(2)}) collective-permute-start(bf16[128,512]{1,0:T(8,128)(2,1)S(1)} %constant_dynamic-slice_fusion), channel_id=1, source_target_pairs={{0,16},{16,0},{1,17},{17,1},{2,18},{18,2},{3,19},{19,3},{4,20},{20... | collective-permute-start | bytes 393224 | tf_op jit(solution)/shard_map/ppermute | solution.py:144
  26.6 8.1 %collective-permute-start.1 = (bf16[128,512]{1,0:T(8,128)(2,1)S(1)}, bf16[128,512]{1,0:T(8,128)(2,1)S(1)}, u32[]{:S(2)}, u32[]{:S(2)}) collective-permute-start(bf16[128,512]{1,0:T(8,128)(2,1)S(1)} %add_convert_fusion.4), channel_id=1, source_target_pairs={{0,64},{32,96},{64,0},{96,32},{1,65},{33,97},{65,1},{97,33},{2,66}... | collective-permute-start | bytes 393224 | tf_op jit(solution)/shard_map/ppermute | solution.py:137
  34.8 7.3 %collective-permute-start.2 = (bf16[128,512]{1,0:T(8,128)(2,1)S(1)}, bf16[128,512]{1,0:T(8,128)(2,1)S(1)}, u32[]{:S(2)}, u32[]{:S(2)}) collective-permute-start(bf16[128,512]{1,0:T(8,128)(2,1)S(1)} %add_convert_fusion.3), channel_id=1, source_target_pairs={{0,32},{32,64},{64,96},{96,0},{1,33},{33,65},{65,97},{97,1},{2,34}... | collective-permute-start | bytes 393224 | tf_op jit(solution)/shard_map/ppermute | solution.py:137
  36.7 32.7 %collective-permute-start.6 = (bf16[128,2560]{1,0:T(8,128)(2,1)S(1)}, bf16[128,2560]{1,0:T(8,128)(2,1)S(1)}, u32[]{:S(2)}, u32[]{:S(2)}) collective-permute-start(bf16[128,2560]{1,0:T(8,128)(2,1)S(1)} %copy-done.7), channel_id=1, source_target_pairs={{0,1},{1,0},{2,3},{3,2},{4,5},{5,4},{6,7},{7,6},{8,9},{9,8},{10,11... | collective-permute-start | bytes 1966088 | tf_op jit(solution)/shard_map/ppermute | solution.py:170
  42.1 22.7 %collective-permute-start.3 = (bf16[128,512]{1,0:T(8,128)(2,1)S(1)}, bf16[128,512]{1,0:T(8,128)(2,1)S(1)}, u32[]{:S(2)}, u32[]{:S(2)}) collective-permute-start(bf16[128,512]{1,0:T(8,128)(2,1)S(1)} %add_convert_fusion.2), channel_id=1, source_target_pairs={{0,256},{128,384},{256,0},{384,128},{1,257},{129,385},{257,1},{385... | collective-permute-start | bytes 393224 | tf_op jit(solution)/shard_map/ppermute | solution.py:137
  64.8 17.2 %copy-start = (bf16[8,128,512]{2,1,0:T(8,128)(2,1)}, bf16[8,128,512]{2,1,0:T(8,128)(2,1)S(1)}, u32[]{:S(2)}) copy-start(bf16[8,128,512]{2,1,0:T(8,128)(2,1)S(1)} %all-to-all-done.refs_0_.refs_1_.refs_2_.refs_3_) | copy-start | bytes 3145732
  64.8 21.2 %collective-permute-start.4 = (bf16[128,512]{1,0:T(8,128)(2,1)S(1)}, bf16[128,512]{1,0:T(8,128)(2,1)S(1)}, u32[]{:S(2)}, u32[]{:S(2)}) collective-permute-start(bf16[128,512]{1,0:T(8,128)(2,1)S(1)} %add_convert_fusion.1), channel_id=1, source_target_pairs={{0,128},{128,256},{256,384},{384,0},{1,129},{129,257},{257,385},{3... | collective-permute-start | bytes 393224 | tf_op jit(solution)/shard_map/ppermute | solution.py:137
  69.4 7.6 %copy-start.1 = (bf16[128,2560]{1,0:T(8,128)(2,1)}, bf16[128,2560]{1,0:T(8,128)(2,1)S(1)}, u32[]{:S(2)}) copy-start(bf16[128,2560]{1,0:T(8,128)(2,1)S(1)} %collective-permute-done.6.refs_4_.refs_5_.refs_6_.refs_7_.refs_8_) | copy-start | bytes 1966084
  82.1 18.3 %collective-permute-start.7 = (bf16[128,2560]{1,0:T(8,128)(2,1)}, bf16[128,2560]{1,0:T(8,128)(2,1)S(1)}, u32[]{:S(2)}, u32[]{:S(2)}) collective-permute-start(bf16[128,2560]{1,0:T(8,128)(2,1)} %get-tuple-element.37), channel_id=1, source_target_pairs={{0,1},{1,0},{2,3},{3,2},{4,5},{5,4},{6,7},{7,6},{8,9},{9,8},{10,11... | collective-permute-start | bytes 1966088 | tf_op jit(solution)/shard_map/ppermute | solution.py:185
  86.1 5.7 %copy-start.4 = (bf16[128,512]{1,0:T(8,128)(2,1)}, bf16[128,512]{1,0:T(8,128)(2,1)S(1)}, u32[]{:S(2)}) copy-start(bf16[128,512]{1,0:T(8,128)(2,1)S(1)} %add_convert_fusion.half_sum) | copy-start | bytes 393220
  89.9 16.1 %collective-permute-start.5 = (bf16[256,512]{1,0:T(8,128)(2,1)}, bf16[256,512]{1,0:T(8,128)(2,1)S(1)}, u32[]{:S(2)}, u32[]{:S(2)}) collective-permute-start(bf16[256,512]{1,0:T(8,128)(2,1)} %get-tuple-element.34), channel_id=1, source_target_pairs={{0,1},{1,0},{2,3},{3,2},{4,5},{5,4},{6,7},{7,6},{8,9},{9,8},{10,11... | collective-permute-start | bytes 786440 | tf_op jit(solution)/shard_map/ppermute | solution.py:191
  91.8 14.2 %collective-permute-start.8 = (bf16[128,512]{1,0:T(8,128)(2,1)S(1)}, bf16[128,512]{1,0:T(8,128)(2,1)S(1)}, u32[]{:S(2)}, u32[]{:S(2)}) collective-permute-start(bf16[128,512]{1,0:T(8,128)(2,1)S(1)} %add_convert_fusion.half_sum), channel_id=1, source_target_pairs={{0,16},{16,0},{1,17},{17,1},{2,18},{18,2},{3,19},{19,3},{4,20},{20... | collective-permute-start | bytes 393224 | tf_op jit(solution)/shard_map/ppermute | solution.py:192
  100.4 0.9 copy-start.3
  106.0 0.7 copy-start.5
  106.0 0.7 copy-start.6
Sparse Core Ops, SparseCore 0:
  10.7 66.2 all-gather.2

commit v6 on v5

--- a/solution.py
+++ b/solution.py
@@ -40,7 +40,7 @@
             out_specs=[whole(o.shape) for o in outs],
             scratch_shapes=scratch,
         ),
-        compiler_params=pltpu.CompilerParams(vmem_limit_bytes=62 * MIB),
+        compiler_params=pltpu.CompilerParams(vmem_limit_bytes=64 * MIB - (128 << 10)),
         cost_estimate=pl.CostEstimate(flops=flops, bytes_accessed=size, transcendentals=0),
     )(*([] if place is None else [place]), *args)
 
@@ -58,12 +58,18 @@
     packed[ROWS:] = cot[...]
 
 
-def split_kernel(place, cot, *refs):
-    tok, (blocks, other) = refs[:4], refs[4:]
-    other[:, YS * ROWS :] = cot[...]
+def split_kernel(*refs):
+    tok, blocks = refs[:4], refs[4]
     for f in range(YS):
         i, j = divmod(f, 2)
         blocks[f] = tok[i][:, 2 * j * ROWS : (2 * j + 2) * ROWS]
+
+
+def other_kernel(place, cot, *refs):
+    tok, other = refs[:4], refs[4]
+    other[:, YS * ROWS :] = cot[...]
+    for f in range(YS):
+        i, j = divmod(f, 2)
         other[:, f * ROWS : (f + 1) * ROWS] = tok[i][:, lanes(2 * j + 1 - place[1])]
 
 
@@ -164,9 +170,10 @@
         [sds((ROWS + TOK, KV), BF16)], 0,
     )
     both = lax.all_gather(packed, "y", axis=0, tiled=False)
-    blocks, other = run(
-        split_kernel, [cotangent], [sds((YS, TOK, 2 * ROWS), BF16), sds((TOK, half + KV), BF16)], 0, token_cuts
-    )
+    (blocks,) = call(
+        split_kernel, None, [tokens] * 4, [s for _, s in token_cuts], [sds((YS, TOK, 2 * ROWS), BF16)], 0
+    )
+    (other,) = run(other_kernel, [cotangent], [sds((TOK, half + KV), BF16)], 0, token_cuts)
     got = lax.ppermute(other, "zl", PAIR)
 
     packed, other = lax.optimization_barrier((packed, other))

time: 118 us -> 116 us (0.983)
  waiting for transfers between devices: 36.9 us -> 30.9 us
  other arithmetic: 0.82 us -> 3.96 us
  Pallas kernels: 21 us -> 22.7 us
  starting transfers between devices: 43 us -> 41.7 us
    all_gather x1, waiting for transfers between devices: 7.61 us -> 1.66 us  [body(): both = lax.all_gather(packed, 'y', axis=0, tiled=False)]
    convert_element_type x5, other arithmetic: 0.17 us -> 3.37 us  [add_pair(): return (part[0].astype(F32) + part[1].astype(F32)).astype(BF16)]
    ppermute x1, waiting for transfers between devices: 5.43 us -> 2.81 us  [body(): returned = lax.ppermute(to_return, 'zl', PAIR)]
    ppermute x4, waiting for transfers between devices: 21.2 us -> 23 us  [ring_step(): return add_pair((total, lax.ppermute(total, axis, ring_shift(4, k))))]
    pallas_call x6 -> x7, Pallas kernels: 21 us -> 22.7 us  [call(): pl.pallas_call(kernel, out_shape=outs, grid_spec=pltpu.PrefetchScalarGrid...]
    unnamed x16 -> x0, local copies, waits for them, and re-layouts: 1.62 us -> none
    ppermute x4, starting transfers between devices: 18 us -> 16.5 us  [ring_step(): return add_pair((total, lax.ppermute(total, axis, ring_shift(4, k))))]
  transfers between devices with their start and end apart: 11 -> 11, of which waited for: 7 -> 7; matrix products, arithmetic and copies ran while one was open for 1% -> 4% of each run, Pallas kernels for 13% -> 15%
where the time goes in v6:
time: 116 us; the launch traced here: 114 us
  starting transfers between devices  41.7 us (36%)
  waiting for transfers between devices  30.9 us (27%)
  Pallas kernels  22.7 us (20%)
  between operations  14.1 us (12%)
  other arithmetic  3.96 us (3%)
    ppermute x4, waiting for transfers between devices, ring_step(): return add_pair((total, lax.ppermute(total, axis, ring_shift(4, k))))  23 us
    pallas_call x7, Pallas kernels, call(): pl.pallas_call(kernel, out_shape=outs, grid_spec=pltpu.PrefetchScalarGrid...  22.7 us
    ppermute x4, starting transfers between devices, ring_step(): return add_pair((total, lax.ppermute(total, axis, ring_shift(4, k))))  16.5 us
    all_to_all x1, starting transfers between devices, body(): slab = lax.all_to_all(blocks, 'y', 0, 0, tiled=True)  7.65 us
    ppermute x1, starting transfers between devices, core_sum(): lax.ppermute(lax.dynamic_slice_in_dim(packed, (1 - core) * n, n), 'core',...  5.41 us
    ppermute x1, starting transfers between devices, body(): returned = lax.ppermute(to_return, 'zl', PAIR)  3.96 us
    ppermute x1, starting transfers between devices, body(): half_got = lax.ppermute(half_sum, 'core', PAIR)  3.69 us
    convert_element_type x5, other arithmetic, add_pair(): return (part[0].astype(F32) + part[1].astype(F32)).astype(BF16)  3.37 us
  transfers between devices with their start and end apart: 11, of which 7 were waited for; matrix products, arithmetic and copies ran while one was open for 4% of the time, Pallas kernels for 15%

profile of v6, /device:TPU:1, one launch (start us, length us, event | category | flops | bytes accessed | tf_op | source)
XLA Modules:
  0.0 114.4 jit_solution(17784442623894575724)
XLA Ops:
  7.2 1.8 %shard_map.110 = bf16[384,512]{1,0:T(8,128)(2,1)} custom-call(f32[256,512]{1,0:T(8,128)} %bitcast.18, bf16[128,512]{1,0:T(8,128)(2,1)} %cot.5), custom_call_target="tpu_custom_call" | custom-call | bytes 1048576 | tf_op jit(solution)/shard_map/pallas_call | solution.py:33
  9.1 2.2 %shard_map.112 = bf16[8,128,512]{2,1,0:T(8,128)(2,1)} custom-call(bf16[128,4096]{1,0:T(8,128)(2,1)} %refs_3_.5, bf16[128,4096]{1,0:T(8,128)(2,1)} %refs_3_.5, bf16[128,4096]{1,0:T(8,128)(2,1)} %refs_3_.5, bf16[128,4096]{1,0:T(8,128)(2,1)} %refs_3_.5), custom_call_target="tpu_custom_call" | custom-call | bytes 5242880 | tf_op jit(solution)/shard_map/pallas_call | solution.py:33
  11.3 7.7 %all-to-all-start = ((bf16[8,128,512]{2,1,0:T(8,128)(2,1)}), bf16[8,128,512]{2,1,0:T(8,128)(2,1)}, u32[]{:S(2)}, u32[]{:S(2)}) async-start(bf16[8,128,512]{2,1,0:T(8,128)(2,1)} %shard_map.112), calls=%async_computation | async-start | bytes 2097152 | tf_op jit(solution)/shard_map/all_to_all | solution.py:180
  19.6 2.8 %shard_map.111 = bf16[128,2560]{1,0:T(8,128)(2,1)} custom-call(s32[3]{0:T(128)} %pad_add_fusion.place, bf16[128,512]{1,0:T(8,128)(2,1)} %cot.5, bf16[128,4096]{1,0:T(8,128)(2,1)} %refs_3_.5, bf16[128,4096]{1,0:T(8,128)(2,1)} %refs_3_.5, bf16[128,4096]{1,0:T(8,128)(2,1)} %refs_3_.5, bf16[128,4096]{1,0:T(8,128)(2,1)} %refs_3_.5), custom_call_target="tpu_custom_call" | custom-call | bytes 4980736 | tf_op jit(solution)/shard_map/pallas_call | solution.py:33
  23.3 5.4 %collective-permute-start = (bf16[128,512]{1,0:T(8,128)(2,1)S(1)}, bf16[128,512]{1,0:T(8,128)(2,1)S(1)}, u32[]{:S(2)}, u32[]{:S(2)}) collective-permute-start(bf16[128,512]{1,0:T(8,128)(2,1)S(1)} %constant_dynamic-slice_fusion), channel_id=1, source_target_pairs={{0,16},{16,0},{1,17},{17,1},{2,18},{18,2},{3,19},{19,3},{4,20},{20... | collective-permute-start | bytes 393224 | tf_op jit(solution)/shard_map/ppermute | solution.py:150
  30.6 2.1 %collective-permute-start.1 = (bf16[128,512]{1,0:T(8,128)(2,1)S(1)}, bf16[128,512]{1,0:T(8,128)(2,1)S(1)}, u32[]{:S(2)}, u32[]{:S(2)}) collective-permute-start(bf16[128,512]{1,0:T(8,128)(2,1)S(1)} %add_convert_fusion.4), channel_id=1, source_target_pairs={{0,64},{32,96},{64,0},{96,32},{1,65},{33,97},{65,1},{97,33},{2,66}... | collective-permute-start | bytes 393224 | tf_op jit(solution)/shard_map/ppermute | solution.py:143
  32.7 6.1 %collective-permute-done.1 = bf16[128,512]{1,0:T(8,128)(2,1)S(1)} collective-permute-done((bf16[128,512]{1,0:T(8,128)(2,1)S(1)}, bf16[128,512]{1,0:T(8,128)(2,1)S(1)}, u32[]{:S(2)}, u32[]{:S(2)}) %collective-permute-start.1) | collective-permute-done | bytes 131104 | tf_op jit(solution)/shard_map/ppermute | solution.py:143
  38.9 1.9 %collective-permute-start.2 = (bf16[128,512]{1,0:T(8,128)(2,1)S(1)}, bf16[128,512]{1,0:T(8,128)(2,1)S(1)}, u32[]{:S(2)}, u32[]{:S(2)}) collective-permute-start(bf16[128,512]{1,0:T(8,128)(2,1)S(1)} %add_convert_fusion.3), channel_id=1, source_target_pairs={{0,32},{32,64},{64,96},{96,0},{1,33},{33,65},{65,97},{97,1},{2,34}... | collective-permute-start | bytes 393224 | tf_op jit(solution)/shard_map/ppermute | solution.py:143
  40.8 2.6 %collective-permute-start.6 = (bf16[128,2560]{1,0:T(8,128)(2,1)}, bf16[128,2560]{1,0:T(8,128)(2,1)}, u32[]{:S(2)}, u32[]{:S(2)}) collective-permute-start(bf16[128,2560]{1,0:T(8,128)(2,1)} %shard_map.111), channel_id=1, source_target_pairs={{0,1},{1,0},{2,3},{3,2},{4,5},{5,4},{6,7},{7,6},{8,9},{9,8},{10,11... | collective-permute-start | bytes 1966088 | tf_op jit(solution)/shard_map/ppermute | solution.py:177
  43.5 2.8 %collective-permute-done.2 = bf16[128,512]{1,0:T(8,128)(2,1)S(1)} collective-permute-done((bf16[128,512]{1,0:T(8,128)(2,1)S(1)}, bf16[128,512]{1,0:T(8,128)(2,1)S(1)}, u32[]{:S(2)}, u32[]{:S(2)}) %collective-permute-start.2) | collective-permute-done | bytes 131104 | tf_op jit(solution)/shard_map/ppermute | solution.py:143
  46.3 8.0 %collective-permute-start.3 = (bf16[128,512]{1,0:T(8,128)(2,1)S(1)}, bf16[128,512]{1,0:T(8,128)(2,1)S(1)}, u32[]{:S(2)}, u32[]{:S(2)}) collective-permute-start(bf16[128,512]{1,0:T(8,128)(2,1)S(1)} %add_convert_fusion.2), channel_id=1, source_target_pairs={{0,256},{128,384},{256,0},{384,128},{1,257},{129,385},{257,1},{385... | collective-permute-start | bytes 393224 | tf_op jit(solution)/shard_map/ppermute | solution.py:143
  54.2 14.1 %collective-permute-done.3 = bf16[128,512]{1,0:T(8,128)(2,1)S(1)} collective-permute-done((bf16[128,512]{1,0:T(8,128)(2,1)S(1)}, bf16[128,512]{1,0:T(8,128)(2,1)S(1)}, u32[]{:S(2)}, u32[]{:S(2)}) %collective-permute-start.3) | collective-permute-done | bytes 131104 | tf_op jit(solution)/shard_map/ppermute | solution.py:143
  69.0 4.5 %collective-permute-start.4 = (bf16[128,512]{1,0:T(8,128)(2,1)}, bf16[128,512]{1,0:T(8,128)(2,1)}, u32[]{:S(2)}, u32[]{:S(2)}) collective-permute-start(bf16[128,512]{1,0:T(8,128)(2,1)} %add_convert_fusion.1), channel_id=1, source_target_pairs={{0,128},{128,256},{256,384},{384,0},{1,129},{129,257},{257,385},{3... | collective-permute-start | bytes 393224 | tf_op jit(solution)/shard_map/ppermute | solution.py:143
  73.5 1.7 %all-gather.3.cloned.1.call-done = bf16[3072,512]{1,0:T(8,128)(2,1)} async-done(((bf16[384,512]{1,0:T(8,128)(2,1)}), bf16[3072,512]{1,0:T(8,128)(2,1)}) %all-gather.3.cloned.1.call-update) | async-done | bytes 3145744 | tf_op jit(solution)/shard_map/all_gather | solution.py:172
  75.2 5.1 %shard_map.114 = (bf16[128,2048]{1,0:T(8,128)(2,1)}, f32[128,512]{1,0:T(8,128)}, bf16[128,2560]{1,0:T(8,128)(2,1)}) custom-call(s32[3]{0:T(128)} %pad_add_fusion.place, bf16[128,512]{1,0:T(8,128)(2,1)} %cot.5, bf16[128,4096]{1,0:T(8,128)(2,1)} %refs_3_.5, bf16[128,4096]{1,0:T(8,128)(2,1)} %refs_3_.5, bf16[128,4096]{1,0:T(8,128)(2,1)} %refs_3_.5, ...), custom_call_target="tpu_custom_call" | custom-call | flops 1073741824 | bytes 21626880 | tf_op jit(solution)/shard_map/pallas_call | solution.py:33
  80.2 4.0 %collective-permute-start.7 = (bf16[128,2560]{1,0:T(8,128)(2,1)}, bf16[128,2560]{1,0:T(8,128)(2,1)}, u32[]{:S(2)}, u32[]{:S(2)}) collective-permute-start(bf16[128,2560]{1,0:T(8,128)(2,1)} %get-tuple-element.33), channel_id=1, source_target_pairs={{0,1},{1,0},{2,3},{3,2},{4,5},{5,4},{6,7},{7,6},{8,9},{9,8},{10,11... | collective-permute-start | bytes 1966088 | tf_op jit(solution)/shard_map/ppermute | solution.py:192
  84.2 1.7 %add_convert_fusion.half_sum = bf16[128,512]{1,0:T(8,128)(2,1)} fusion(bf16[128,512]{1,0:T(8,128)(2,1)} %collective-permute-done.4, bf16[128,512]{1,0:T(8,128)(2,1)} %add_convert_fusion.1), kind=kLoop, calls=%fused_computation | loop fusion | flops 262144 | bytes 393216 | tf_op jit(solution)/shard_map/convert_element_type | solution.py:139
  85.9 3.7 %shard_map.113 = (f32[256,512]{1,0:T(8,128)}, bf16[256,512]{1,0:T(8,128)(2,1)}) custom-call(s32[3]{0:T(128)} %pad_add_fusion.place, bf16[8,128,512]{2,1,0:T(8,128)(2,1)} %all-to-all-done.refs_0_.refs_1_.refs_2_.refs_3_, bf16[8,128,512]{2,1,0:T(8,128)(2,1)} %all-to-all-done.refs_0_.refs_1_.refs_2_.refs_3_, ...), custom_call_target="tpu_custom_call" | custom-call | flops 536870912 | bytes 17563648 | tf_op jit(solution)/shard_map/pallas_call | solution.py:33
  89.6 1.9 %collective-permute-start.5 = (bf16[256,512]{1,0:T(8,128)(2,1)}, bf16[256,512]{1,0:T(8,128)(2,1)}, u32[]{:S(2)}, u32[]{:S(2)}) collective-permute-start(bf16[256,512]{1,0:T(8,128)(2,1)} %get-tuple-element.30), channel_id=1, source_target_pairs={{0,1},{1,0},{2,3},{3,2},{4,5},{5,4},{6,7},{7,6},{8,9},{9,8},{10,11... | collective-permute-start | bytes 786440 | tf_op jit(solution)/shard_map/ppermute | solution.py:198
  91.5 3.7 %collective-permute-start.8 = (bf16[128,512]{1,0:T(8,128)(2,1)}, bf16[128,512]{1,0:T(8,128)(2,1)}, u32[]{:S(2)}, u32[]{:S(2)}) collective-permute-start(bf16[128,512]{1,0:T(8,128)(2,1)} %add_convert_fusion.half_sum), channel_id=1, source_target_pairs={{0,16},{16,0},{1,17},{17,1},{2,18},{18,2},{3,19},{19,3},{4,20},{20... | collective-permute-start | bytes 393224 | tf_op jit(solution)/shard_map/ppermute | solution.py:199
  95.2 2.8 %collective-permute-done.7.returned = bf16[128,2560]{1,0:T(8,128)(2,1)} collective-permute-done((bf16[128,2560]{1,0:T(8,128)(2,1)}, bf16[128,2560]{1,0:T(8,128)(2,1)}, u32[]{:S(2)}, u32[]{:S(2)}) %collective-permute-start.7) | collective-permute-done | bytes 655392 | tf_op jit(solution)/shard_map/ppermute | solution.py:192
  98.0 3.1 %shard_map.115 = (bf16[128,512]{1,0:T(8,128)(2,1)}, bf16[128,4096]{1,0:T(8,128)(2,1)}) custom-call(s32[3]{0:T(128)} %pad_add_fusion.place, bf16[128,2048]{1,0:T(8,128)(2,1)} %get-tuple-element.31.own, f32[128,512]{1,0:T(8,128)} %get-tuple-element.32.ahead, bf16[128,2560]{1,0:T(8,128)(2,1)} %collective-permute-done.7.returned), custom_call_target="tpu_custom_call" | custom-call | bytes 2621440 | tf_op jit(solution)/shard_map/pallas_call | solution.py:33
  101.1 2.5 %collective-permute-done.5.sent = bf16[256,512]{1,0:T(8,128)(2,1)} collective-permute-done((bf16[256,512]{1,0:T(8,128)(2,1)}, bf16[256,512]{1,0:T(8,128)(2,1)}, u32[]{:S(2)}, u32[]{:S(2)}) %collective-permute-start.5) | collective-permute-done | bytes 262176 | tf_op jit(solution)/shard_map/ppermute | solution.py:198
  103.6 3.9 %shard_map.116 = (f32[256,512]{1,0:T(8,128)}, bf16[256,512]{1,0:T(8,128)(2,1)}, bf16[256,512]{1,0:T(8,128)(2,1)}) custom-call(s32[3]{0:T(128)} %pad_add_fusion.place, f32[256,512]{1,0:T(8,128)} %get-tuple-element.37.keep, bf16[256,512]{1,0:T(8,128)(2,1)} %collective-permute-done.5.sent, f32[256,512]{1,0:T(8,128)} %bitcast.19, bf16[256,512]{1,0:T(8,128)(2,1)} %bitcast.20, ...), custom_call_target="tpu_custom_call" | custom-call | flops 5242880 | bytes 3670016 | tf_op jit(solution)/shard_map/pallas_call | solution.py:33
  (13 shorter events, 4.2 us)
Async XLA Ops:
  7.2 68.0 %all-gather.3.cloned.1.call-start = ((), (), s32[]{:S(2)}) async-start(), calls=%async_computation.1 | async-start | bytes 3538944 | tf_op jit(solution)/shard_map/all_gather | solution.py:172
  11.3 57.7 %all-to-all-start = ((bf16[8,128,512]{2,1,0:T(8,128)(2,1)}), bf16[8,128,512]{2,1,0:T(8,128)(2,1)}, u32[]{:S(2)}, u32[]{:S(2)}) async-start(bf16[8,128,512]{2,1,0:T(8,128)(2,1)} %shard_map.112), calls=%async_computation | async-start | bytes 2097152 | tf_op jit(solution)/shard_map/all_to_all | solution.py:180
  23.3 6.4 %collective-permute-start = (bf16[128,512]{1,0:T(8,128)(2,1)S(1)}, bf16[128,512]{1,0:T(8,128)(2,1)S(1)}, u32[]{:S(2)}, u32[]{:S(2)}) collective-permute-start(bf16[128,512]{1,0:T(8,128)(2,1)S(1)} %constant_dynamic-slice_fusion), channel_id=1, source_target_pairs={{0,16},{16,0},{1,17},{17,1},{2,18},{18,2},{3,19},{19,3},{4,20},{20... | collective-permute-start | bytes 393224 | tf_op jit(solution)/shard_map/ppermute | solution.py:150
  30.6 8.2 %collective-permute-start.1 = (bf16[128,512]{1,0:T(8,128)(2,1)S(1)}, bf16[128,512]{1,0:T(8,128)(2,1)S(1)}, u32[]{:S(2)}, u32[]{:S(2)}) collective-permute-start(bf16[128,512]{1,0:T(8,128)(2,1)S(1)} %add_convert_fusion.4), channel_id=1, source_target_pairs={{0,64},{32,96},{64,0},{96,32},{1,65},{33,97},{65,1},{97,33},{2,66}... | collective-permute-start | bytes 393224 | tf_op jit(solution)/shard_map/ppermute | solution.py:143
  38.9 7.3 %collective-permute-start.2 = (bf16[128,512]{1,0:T(8,128)(2,1)S(1)}, bf16[128,512]{1,0:T(8,128)(2,1)S(1)}, u32[]{:S(2)}, u32[]{:S(2)}) collective-permute-start(bf16[128,512]{1,0:T(8,128)(2,1)S(1)} %add_convert_fusion.3), channel_id=1, source_target_pairs={{0,32},{32,64},{64,96},{96,0},{1,33},{33,65},{65,97},{97,1},{2,34}... | collective-permute-start | bytes 393224 | tf_op jit(solution)/shard_map/ppermute | solution.py:143
  40.8 32.7 %collective-permute-start.6 = (bf16[128,2560]{1,0:T(8,128)(2,1)}, bf16[128,2560]{1,0:T(8,128)(2,1)}, u32[]{:S(2)}, u32[]{:S(2)}) collective-permute-start(bf16[128,2560]{1,0:T(8,128)(2,1)} %shard_map.111), channel_id=1, source_target_pairs={{0,1},{1,0},{2,3},{3,2},{4,5},{5,4},{6,7},{7,6},{8,9},{9,8},{10,11... | collective-permute-start | bytes 1966088 | tf_op jit(solution)/shard_map/ppermute | solution.py:177
  46.3 22.0 %collective-permute-start.3 = (bf16[128,512]{1,0:T(8,128)(2,1)S(1)}, bf16[128,512]{1,0:T(8,128)(2,1)S(1)}, u32[]{:S(2)}, u32[]{:S(2)}) collective-permute-start(bf16[128,512]{1,0:T(8,128)(2,1)S(1)} %add_convert_fusion.2), channel_id=1, source_target_pairs={{0,256},{128,384},{256,0},{384,128},{1,257},{129,385},{257,1},{385... | collective-permute-start | bytes 393224 | tf_op jit(solution)/shard_map/ppermute | solution.py:143
  69.0 15.2 %collective-permute-start.4 = (bf16[128,512]{1,0:T(8,128)(2,1)}, bf16[128,512]{1,0:T(8,128)(2,1)}, u32[]{:S(2)}, u32[]{:S(2)}) collective-permute-start(bf16[128,512]{1,0:T(8,128)(2,1)} %add_convert_fusion.1), channel_id=1, source_target_pairs={{0,128},{128,256},{256,384},{384,0},{1,129},{129,257},{257,385},{3... | collective-permute-start | bytes 393224 | tf_op jit(solution)/shard_map/ppermute | solution.py:143
  80.2 17.8 %collective-permute-start.7 = (bf16[128,2560]{1,0:T(8,128)(2,1)}, bf16[128,2560]{1,0:T(8,128)(2,1)}, u32[]{:S(2)}, u32[]{:S(2)}) collective-permute-start(bf16[128,2560]{1,0:T(8,128)(2,1)} %get-tuple-element.33), channel_id=1, source_target_pairs={{0,1},{1,0},{2,3},{3,2},{4,5},{5,4},{6,7},{7,6},{8,9},{9,8},{10,11... | collective-permute-start | bytes 1966088 | tf_op jit(solution)/shard_map/ppermute | solution.py:192
  89.6 14.0 %collective-permute-start.5 = (bf16[256,512]{1,0:T(8,128)(2,1)}, bf16[256,512]{1,0:T(8,128)(2,1)}, u32[]{:S(2)}, u32[]{:S(2)}) collective-permute-start(bf16[256,512]{1,0:T(8,128)(2,1)} %get-tuple-element.30), channel_id=1, source_target_pairs={{0,1},{1,0},{2,3},{3,2},{4,5},{5,4},{6,7},{7,6},{8,9},{9,8},{10,11... | collective-permute-start | bytes 786440 | tf_op jit(solution)/shard_map/ppermute | solution.py:198
  91.5 12.1 %collective-permute-start.8 = (bf16[128,512]{1,0:T(8,128)(2,1)}, bf16[128,512]{1,0:T(8,128)(2,1)}, u32[]{:S(2)}, u32[]{:S(2)}) collective-permute-start(bf16[128,512]{1,0:T(8,128)(2,1)} %add_convert_fusion.half_sum), channel_id=1, source_target_pairs={{0,16},{16,0},{1,17},{17,1},{2,18},{18,2},{3,19},{19,3},{4,20},{20... | collective-permute-start | bytes 393224 | tf_op jit(solution)/shard_map/ppermute | solution.py:199
Sparse Core Ops, SparseCore 0:
  10.7 64.4 all-gather.2

commit v7 on v6

--- a/solution.py
+++ b/solution.py
@@ -181,8 +181,8 @@
     half_sum = ring_step(ring_step(core_sum(packed), "x", 2), "x", 1)
     half_sum = ring_step(half_sum, "zh", 2)
     half_sum, slab = lax.optimization_barrier((half_sum, slab))
-    half_sum = ring_step(half_sum, "zh", 1)
-    slab, half_sum = lax.optimization_barrier((slab, half_sum))
+    came = lax.ppermute(half_sum, "zh", ring_shift(4, 1))
+    slab, came = lax.optimization_barrier((slab, came))
 
     own, ahead, to_return = run(
         functools.partial(product_kernel, factor), [cotangent],
@@ -194,8 +194,9 @@
         functools.partial(grad_kernel, factor), [], [sds((ROWS, KV), F32), sds((ROWS, KV), BF16)], flops,
         cut(slab, (2, TOK, 2 * ROWS), [(i, 0, 0) for i in fours]) + cut(both, (2, TOK, KV), [(i, 2, 0) for i in fours]),
     )
-    send, half_sum = lax.optimization_barrier((send, half_sum))
+    send, came = lax.optimization_barrier((send, came))
     sent = lax.ppermute(send, "zl", PAIR)
+    half_sum = add_pair((half_sum, came))
     half_got = lax.ppermute(half_sum, "core", PAIR)
     projected, input_grad = run(
         join_kernel, [own, ahead, returned], [sds((TOK, KV), BF16), sds(tokens.shape, BF16)]

time: 116 us -> 137 us (1.18)
  waiting for transfers between devices: 30.9 us -> 48.6 us
  starting transfers between devices: 41.7 us -> 44.8 us
    ppermute x0 -> x1, waiting for transfers between devices: none -> 19.8 us  [body(): came = lax.ppermute(half_sum, 'zh', ring_shift(4, 1))]
    all_gather x1, waiting for transfers between devices: 1.66 us -> 20.3 us  [body(): both = lax.all_gather(packed, 'y', axis=0, tiled=False)]
    ppermute x4 -> x3, waiting for transfers between devices: 23 us -> 7.54 us  [ring_step(): return add_pair((total, lax.ppermute(total, axis, ring_shift(4, k))))]
    ppermute x0 -> x1, starting transfers between devices: none -> 5.8 us  [body(): came = lax.ppermute(half_sum, 'zh', ring_shift(4, 1))]
    ppermute x4 -> x3, starting transfers between devices: 16.5 us -> 12 us  [ring_step(): return add_pair((total, lax.ppermute(total, axis, ring_shift(4, k))))]
    ppermute x1, waiting for transfers between devices: 2.81 us -> 0.01 us  [body(): returned = lax.ppermute(to_return, 'zl', PAIR)]
    ppermute x1, waiting for transfers between devices: 2.5 us -> 0.01 us  [body(): sent = lax.ppermute(send, 'zl', PAIR)]
    ppermute x1, starting transfers between devices: 2.62 us -> 4 us  [body(): got = lax.ppermute(other, 'zl', PAIR)]
  transfers between devices with their start and end apart: 11 -> 11, of which waited for: 7 -> 5; matrix products, arithmetic and copies ran while one was open for 4% -> 4% of each run, Pallas kernels for 15% -> 12%
where the time goes in v7:
time: 137 us
  waiting for transfers between devices  48.6 us (35%)
  starting transfers between devices  44.8 us (33%)
  Pallas kernels  22.7 us (17%)
  between operations  14.2 us (10%)
  other arithmetic  4.93 us (4%)
  local copies, waits for them, and re-layouts  1.55 us (1%)
    pallas_call x7, Pallas kernels, call(): pl.pallas_call(kernel, out_shape=outs, grid_spec=pltpu.PrefetchScalarGrid...  22.7 us
    all_gather x1, waiting for transfers between devices, body(): both = lax.all_gather(packed, 'y', axis=0, tiled=False)  20.3 us
    ppermute x1, waiting for transfers between devices, body(): came = lax.ppermute(half_sum, 'zh', ring_shift(4, 1))  19.8 us
    ppermute x3, starting transfers between devices, ring_step(): return add_pair((total, lax.ppermute(total, axis, ring_shift(4, k))))  12 us
    all_to_all x1, starting transfers between devices, body(): slab = lax.all_to_all(blocks, 'y', 0, 0, tiled=True)  7.65 us
    ppermute x3, waiting for transfers between devices, ring_step(): return add_pair((total, lax.ppermute(total, axis, ring_shift(4, k))))  7.54 us
    ppermute x1, starting transfers between devices, body(): came = lax.ppermute(half_sum, 'zh', ring_shift(4, 1))  5.8 us
    ppermute x1, starting transfers between devices, core_sum(): lax.ppermute(lax.dynamic_slice_in_dim(packed, (1 - core) * n, n), 'core',...  5.41 us
  transfers between devices with their start and end apart: 11, of which 5 were waited for; matrix products, arithmetic and copies ran while one was open for 4% of the time, Pallas kernels for 12%

profile of v7, /device:TPU:1, one launch (start us, length us, event | category | flops | bytes accessed | tf_op | source)
XLA Modules:
  0.0 136.7 jit_solution(905496063620412956)
XLA Ops:
  7.2 1.8 %shard_map.110 = bf16[384,512]{1,0:T(8,128)(2,1)} custom-call(f32[256,512]{1,0:T(8,128)} %bitcast.18, bf16[128,512]{1,0:T(8,128)(2,1)} %cot.5), custom_call_target="tpu_custom_call" | custom-call | bytes 1048576 | tf_op jit(solution)/shard_map/pallas_call | solution.py:33
  9.1 2.2 %shard_map.112 = bf16[8,128,512]{2,1,0:T(8,128)(2,1)} custom-call(bf16[128,4096]{1,0:T(8,128)(2,1)} %refs_3_.5, bf16[128,4096]{1,0:T(8,128)(2,1)} %refs_3_.5, bf16[128,4096]{1,0:T(8,128)(2,1)} %refs_3_.5, bf16[128,4096]{1,0:T(8,128)(2,1)} %refs_3_.5), custom_call_target="tpu_custom_call" | custom-call | bytes 5242880 | tf_op jit(solution)/shard_map/pallas_call | solution.py:33
  11.3 7.7 %all-to-all-start = ((bf16[8,128,512]{2,1,0:T(8,128)(2,1)}), bf16[8,128,512]{2,1,0:T(8,128)(2,1)}, u32[]{:S(2)}, u32[]{:S(2)}) async-start(bf16[8,128,512]{2,1,0:T(8,128)(2,1)} %shard_map.112), calls=%async_computation | async-start | bytes 2097152 | tf_op jit(solution)/shard_map/all_to_all | solution.py:180
  19.6 2.8 %shard_map.111 = bf16[128,2560]{1,0:T(8,128)(2,1)} custom-call(s32[3]{0:T(128)} %pad_add_fusion.place, bf16[128,512]{1,0:T(8,128)(2,1)} %cot.5, bf16[128,4096]{1,0:T(8,128)(2,1)} %refs_3_.5, bf16[128,4096]{1,0:T(8,128)(2,1)} %refs_3_.5, bf16[128,4096]{1,0:T(8,128)(2,1)} %refs_3_.5, bf16[128,4096]{1,0:T(8,128)(2,1)} %refs_3_.5), custom_call_target="tpu_custom_call" | custom-call | bytes 4980736 | tf_op jit(solution)/shard_map/pallas_call | solution.py:33
  23.3 5.4 %collective-permute-start = (bf16[128,512]{1,0:T(8,128)(2,1)S(1)}, bf16[128,512]{1,0:T(8,128)(2,1)S(1)}, u32[]{:S(2)}, u32[]{:S(2)}) collective-permute-start(bf16[128,512]{1,0:T(8,128)(2,1)S(1)} %constant_dynamic-slice_fusion), channel_id=1, source_target_pairs={{0,16},{16,0},{1,17},{17,1},{2,18},{18,2},{3,19},{19,3},{4,20},{20... | collective-permute-start | bytes 393224 | tf_op jit(solution)/shard_map/ppermute | solution.py:150
  28.7 1.0 collective-permute-done
  30.6 2.1 %collective-permute-start.1 = (bf16[128,512]{1,0:T(8,128)(2,1)S(1)}, bf16[128,512]{1,0:T(8,128)(2,1)S(1)}, u32[]{:S(2)}, u32[]{:S(2)}) collective-permute-start(bf16[128,512]{1,0:T(8,128)(2,1)S(1)} %add_convert_fusion.4), channel_id=1, source_target_pairs={{0,64},{32,96},{64,0},{96,32},{1,65},{33,97},{65,1},{97,33},{2,66}... | collective-permute-start | bytes 393224 | tf_op jit(solution)/shard_map/ppermute | solution.py:143
  32.7 4.0 %collective-permute-start.6 = (bf16[128,2560]{1,0:T(8,128)(2,1)}, bf16[128,2560]{1,0:T(8,128)(2,1)}, u32[]{:S(2)}, u32[]{:S(2)}) collective-permute-start(bf16[128,2560]{1,0:T(8,128)(2,1)} %shard_map.111), channel_id=1, source_target_pairs={{0,1},{1,0},{2,3},{3,2},{4,5},{5,4},{6,7},{7,6},{8,9},{9,8},{10,11... | collective-permute-start | bytes 1966088 | tf_op jit(solution)/shard_map/ppermute | solution.py:177
  36.7 2.1 %collective-permute-done.1 = bf16[128,512]{1,0:T(8,128)(2,1)S(1)} collective-permute-done((bf16[128,512]{1,0:T(8,128)(2,1)S(1)}, bf16[128,512]{1,0:T(8,128)(2,1)S(1)}, u32[]{:S(2)}, u32[]{:S(2)}) %collective-permute-start.1) | collective-permute-done | bytes 131104 | tf_op jit(solution)/shard_map/ppermute | solution.py:143
  38.9 1.9 %collective-permute-start.2 = (bf16[128,512]{1,0:T(8,128)(2,1)S(1)}, bf16[128,512]{1,0:T(8,128)(2,1)S(1)}, u32[]{:S(2)}, u32[]{:S(2)}) collective-permute-start(bf16[128,512]{1,0:T(8,128)(2,1)S(1)} %add_convert_fusion.3), channel_id=1, source_target_pairs={{0,32},{32,64},{64,96},{96,0},{1,33},{33,65},{65,97},{97,1},{2,34}... | collective-permute-start | bytes 393224 | tf_op jit(solution)/shard_map/ppermute | solution.py:143
  40.8 5.4 %collective-permute-done.2 = bf16[128,512]{1,0:T(8,128)(2,1)S(1)} collective-permute-done((bf16[128,512]{1,0:T(8,128)(2,1)S(1)}, bf16[128,512]{1,0:T(8,128)(2,1)S(1)}, u32[]{:S(2)}, u32[]{:S(2)}) %collective-permute-start.2) | collective-permute-done | bytes 131104 | tf_op jit(solution)/shard_map/ppermute | solution.py:143
  46.9 8.0 %collective-permute-start.3 = (bf16[128,512]{1,0:T(8,128)(2,1)}, bf16[128,512]{1,0:T(8,128)(2,1)}, u32[]{:S(2)}, u32[]{:S(2)}) collective-permute-start(bf16[128,512]{1,0:T(8,128)(2,1)} %add_convert_fusion.2), channel_id=1, source_target_pairs={{0,256},{128,384},{256,0},{384,128},{1,257},{129,385},{257,1},{385... | collective-permute-start | bytes 393224 | tf_op jit(solution)/shard_map/ppermute | solution.py:143
  54.9 20.3 %all-gather.3.cloned.1.call-done = bf16[3072,512]{1,0:T(8,128)(2,1)} async-done(((bf16[384,512]{1,0:T(8,128)(2,1)}), bf16[3072,512]{1,0:T(8,128)(2,1)}) %all-gather.3.cloned.1.call-update) | async-done | bytes 3145744 | tf_op jit(solution)/shard_map/all_gather | solution.py:172
  75.2 5.1 %shard_map.114 = (bf16[128,2048]{1,0:T(8,128)(2,1)}, f32[128,512]{1,0:T(8,128)}, bf16[128,2560]{1,0:T(8,128)(2,1)}) custom-call(s32[3]{0:T(128)} %pad_add_fusion.place, bf16[128,512]{1,0:T(8,128)(2,1)} %cot.5, bf16[128,4096]{1,0:T(8,128)(2,1)} %refs_3_.5, bf16[128,4096]{1,0:T(8,128)(2,1)} %refs_3_.5, bf16[128,4096]{1,0:T(8,128)(2,1)} %refs_3_.5, ...), custom_call_target="tpu_custom_call" | custom-call | flops 1073741824 | bytes 21626880 | tf_op jit(solution)/shard_map/pallas_call | solution.py:33
  80.2 4.0 %collective-permute-start.7 = (bf16[128,2560]{1,0:T(8,128)(2,1)}, bf16[128,2560]{1,0:T(8,128)(2,1)}, u32[]{:S(2)}, u32[]{:S(2)}) collective-permute-start(bf16[128,2560]{1,0:T(8,128)(2,1)} %get-tuple-element.33), channel_id=1, source_target_pairs={{0,1},{1,0},{2,3},{3,2},{4,5},{5,4},{6,7},{7,6},{8,9},{9,8},{10,11... | collective-permute-start | bytes 1966088 | tf_op jit(solution)/shard_map/ppermute | solution.py:192
  84.2 1.0 add_convert_fusion.1
  85.9 5.8 %collective-permute-start.4 = (bf16[128,512]{1,0:T(8,128)(2,1)S(1)}, bf16[128,512]{1,0:T(8,128)(2,1)}, u32[]{:S(2)}, u32[]{:S(2)}) collective-permute-start(bf16[128,512]{1,0:T(8,128)(2,1)S(1)} %add_convert_fusion.1), channel_id=1, source_target_pairs={{0,128},{128,256},{256,384},{384,0},{1,129},{129,257},{257,385},{3... | collective-permute-start | bytes 393224 | tf_op jit(solution)/shard_map/ppermute | solution.py:184
  91.7 19.8 %collective-permute-done.4 = bf16[128,512]{1,0:T(8,128)(2,1)} collective-permute-done((bf16[128,512]{1,0:T(8,128)(2,1)S(1)}, bf16[128,512]{1,0:T(8,128)(2,1)}, u32[]{:S(2)}, u32[]{:S(2)}) %collective-permute-start.4) | collective-permute-done | bytes 131104 | tf_op jit(solution)/shard_map/ppermute | solution.py:184
  111.4 3.7 %shard_map.113 = (f32[256,512]{1,0:T(8,128)}, bf16[256,512]{1,0:T(8,128)(2,1)}) custom-call(s32[3]{0:T(128)} %pad_add_fusion.place, bf16[8,128,512]{2,1,0:T(8,128)(2,1)} %all-to-all-done.refs_0_.refs_1_.refs_2_.refs_3_, bf16[8,128,512]{2,1,0:T(8,128)(2,1)} %all-to-all-done.refs_0_.refs_1_.refs_2_.refs_3_, ...), custom_call_target="tpu_custom_call" | custom-call | flops 536870912 | bytes 17563648 | tf_op jit(solution)/shard_map/pallas_call | solution.py:33
  115.2 1.9 %collective-permute-start.5 = (bf16[256,512]{1,0:T(8,128)(2,1)}, bf16[256,512]{1,0:T(8,128)(2,1)}, u32[]{:S(2)}, u32[]{:S(2)}) collective-permute-start(bf16[256,512]{1,0:T(8,128)(2,1)} %get-tuple-element.30), channel_id=1, source_target_pairs={{0,1},{1,0},{2,3},{3,2},{4,5},{5,4},{6,7},{7,6},{8,9},{9,8},{10,11... | collective-permute-start | bytes 786440 | tf_op jit(solution)/shard_map/ppermute | solution.py:198
  117.1 1.6 %add_convert_fusion.half_sum = bf16[128,512]{1,0:T(8,128)(2,1)} fusion(bf16[128,512]{1,0:T(8,128)(2,1)} %collective-permute-done.4, bf16[128,512]{1,0:T(8,128)(2,1)} %copy-done), kind=kLoop, calls=%fused_computation | loop fusion | flops 262144 | bytes 393216 | tf_op jit(solution)/shard_map/convert_element_type | solution.py:139
  118.7 4.1 %collective-permute-start.8 = (bf16[128,512]{1,0:T(8,128)(2,1)}, bf16[128,512]{1,0:T(8,128)(2,1)}, u32[]{:S(2)}, u32[]{:S(2)}) collective-permute-start(bf16[128,512]{1,0:T(8,128)(2,1)} %add_convert_fusion.half_sum), channel_id=1, source_target_pairs={{0,16},{16,0},{1,17},{17,1},{2,18},{18,2},{3,19},{19,3},{4,20},{20... | collective-permute-start | bytes 393224 | tf_op jit(solution)/shard_map/ppermute | solution.py:200
  122.8 3.1 %shard_map.115 = (bf16[128,512]{1,0:T(8,128)(2,1)}, bf16[128,4096]{1,0:T(8,128)(2,1)}) custom-call(s32[3]{0:T(128)} %pad_add_fusion.place, bf16[128,2048]{1,0:T(8,128)(2,1)} %get-tuple-element.31.own, f32[128,512]{1,0:T(8,128)} %get-tuple-element.32.ahead, bf16[128,2560]{1,0:T(8,128)(2,1)} %collective-permute-done.7.returned), custom_call_target="tpu_custom_call" | custom-call | bytes 2621440 | tf_op jit(solution)/shard_map/pallas_call | solution.py:33
  126.0 3.9 %shard_map.116 = (f32[256,512]{1,0:T(8,128)}, bf16[256,512]{1,0:T(8,128)(2,1)}, bf16[256,512]{1,0:T(8,128)(2,1)}) custom-call(s32[3]{0:T(128)} %pad_add_fusion.place, f32[256,512]{1,0:T(8,128)} %get-tuple-element.37.keep, bf16[256,512]{1,0:T(8,128)(2,1)} %collective-permute-done.5.sent, f32[256,512]{1,0:T(8,128)} %bitcast.19, bf16[256,512]{1,0:T(8,128)(2,1)} %bitcast.20, ...), custom_call_target="tpu_custom_call" | custom-call | flops 5242880 | bytes 3670016 | tf_op jit(solution)/shard_map/pallas_call | solution.py:33
  (15 shorter events, 3.9 us)
Async XLA Ops:
  7.2 68.0 %all-gather.3.cloned.1.call-start = ((), (), s32[]{:S(2)}) async-start(), calls=%async_computation.1 | async-start | bytes 3538944 | tf_op jit(solution)/shard_map/all_gather | solution.py:172
  11.3 73.9 %all-to-all-start = ((bf16[8,128,512]{2,1,0:T(8,128)(2,1)}), bf16[8,128,512]{2,1,0:T(8,128)(2,1)}, u32[]{:S(2)}, u32[]{:S(2)}) async-start(bf16[8,128,512]{2,1,0:T(8,128)(2,1)} %shard_map.112), calls=%async_computation | async-start | bytes 2097152 | tf_op jit(solution)/shard_map/all_to_all | solution.py:180
  23.3 6.4 %collective-permute-start = (bf16[128,512]{1,0:T(8,128)(2,1)S(1)}, bf16[128,512]{1,0:T(8,128)(2,1)S(1)}, u32[]{:S(2)}, u32[]{:S(2)}) collective-permute-start(bf16[128,512]{1,0:T(8,128)(2,1)S(1)} %constant_dynamic-slice_fusion), channel_id=1, source_target_pairs={{0,16},{16,0},{1,17},{17,1},{2,18},{18,2},{3,19},{19,3},{4,20},{20... | collective-permute-start | bytes 393224 | tf_op jit(solution)/shard_map/ppermute | solution.py:150
  30.6 8.2 %collective-permute-start.1 = (bf16[128,512]{1,0:T(8,128)(2,1)S(1)}, bf16[128,512]{1,0:T(8,128)(2,1)S(1)}, u32[]{:S(2)}, u32[]{:S(2)}) collective-permute-start(bf16[128,512]{1,0:T(8,128)(2,1)S(1)} %add_convert_fusion.4), channel_id=1, source_target_pairs={{0,64},{32,96},{64,0},{96,32},{1,65},{33,97},{65,1},{97,33},{2,66}... | collective-permute-start | bytes 393224 | tf_op jit(solution)/shard_map/ppermute | solution.py:143
  32.7 22.2 %collective-permute-start.6 = (bf16[128,2560]{1,0:T(8,128)(2,1)}, bf16[128,2560]{1,0:T(8,128)(2,1)}, u32[]{:S(2)}, u32[]{:S(2)}) collective-permute-start(bf16[128,2560]{1,0:T(8,128)(2,1)} %shard_map.111), channel_id=1, source_target_pairs={{0,1},{1,0},{2,3},{3,2},{4,5},{5,4},{6,7},{7,6},{8,9},{9,8},{10,11... | collective-permute-start | bytes 1966088 | tf_op jit(solution)/shard_map/ppermute | solution.py:177
  38.9 7.3 %collective-permute-start.2 = (bf16[128,512]{1,0:T(8,128)(2,1)S(1)}, bf16[128,512]{1,0:T(8,128)(2,1)S(1)}, u32[]{:S(2)}, u32[]{:S(2)}) collective-permute-start(bf16[128,512]{1,0:T(8,128)(2,1)S(1)} %add_convert_fusion.3), channel_id=1, source_target_pairs={{0,32},{32,64},{64,96},{96,0},{1,33},{33,65},{65,97},{97,1},{2,34}... | collective-permute-start | bytes 393224 | tf_op jit(solution)/shard_map/ppermute | solution.py:143
  46.9 37.3 %collective-permute-start.3 = (bf16[128,512]{1,0:T(8,128)(2,1)}, bf16[128,512]{1,0:T(8,128)(2,1)}, u32[]{:S(2)}, u32[]{:S(2)}) collective-permute-start(bf16[128,512]{1,0:T(8,128)(2,1)} %add_convert_fusion.2), channel_id=1, source_target_pairs={{0,256},{128,384},{256,0},{384,128},{1,257},{129,385},{257,1},{385... | collective-permute-start | bytes 393224 | tf_op jit(solution)/shard_map/ppermute | solution.py:143
  80.2 42.6 %collective-permute-start.7 = (bf16[128,2560]{1,0:T(8,128)(2,1)}, bf16[128,2560]{1,0:T(8,128)(2,1)}, u32[]{:S(2)}, u32[]{:S(2)}) collective-permute-start(bf16[128,2560]{1,0:T(8,128)(2,1)} %get-tuple-element.33), channel_id=1, source_target_pairs={{0,1},{1,0},{2,3},{3,2},{4,5},{5,4},{6,7},{7,6},{8,9},{9,8},{10,11... | collective-permute-start | bytes 1966088 | tf_op jit(solution)/shard_map/ppermute | solution.py:192
  85.2 0.7 copy-start
  85.9 25.6 %collective-permute-start.4 = (bf16[128,512]{1,0:T(8,128)(2,1)S(1)}, bf16[128,512]{1,0:T(8,128)(2,1)}, u32[]{:S(2)}, u32[]{:S(2)}) collective-permute-start(bf16[128,512]{1,0:T(8,128)(2,1)S(1)} %add_convert_fusion.1), channel_id=1, source_target_pairs={{0,128},{128,256},{256,384},{384,0},{1,129},{129,257},{257,385},{3... | collective-permute-start | bytes 393224 | tf_op jit(solution)/shard_map/ppermute | solution.py:184
  115.2 10.8 %collective-permute-start.5 = (bf16[256,512]{1,0:T(8,128)(2,1)}, bf16[256,512]{1,0:T(8,128)(2,1)}, u32[]{:S(2)}, u32[]{:S(2)}) collective-permute-start(bf16[256,512]{1,0:T(8,128)(2,1)} %get-tuple-element.30), channel_id=1, source_target_pairs={{0,1},{1,0},{2,3},{3,2},{4,5},{5,4},{6,7},{7,6},{8,9},{9,8},{10,11... | collective-permute-start | bytes 786440 | tf_op jit(solution)/shard_map/ppermute | solution.py:198
  118.7 7.2 %collective-permute-start.8 = (bf16[128,512]{1,0:T(8,128)(2,1)}, bf16[128,512]{1,0:T(8,128)(2,1)}, u32[]{:S(2)}, u32[]{:S(2)}) collective-permute-start(bf16[128,512]{1,0:T(8,128)(2,1)} %add_convert_fusion.half_sum), channel_id=1, source_target_pairs={{0,16},{16,0},{1,17},{17,1},{2,18},{18,2},{3,19},{19,3},{4,20},{20... | collective-permute-start | bytes 393224 | tf_op jit(solution)/shard_map/ppermute | solution.py:200
Sparse Core Ops, SparseCore 0:
  10.7 64.4 all-gather.2

commit v8 on v6

--- a/solution.py
+++ b/solution.py
@@ -30,6 +30,7 @@
 def call(kernel, place, args, in_specs, outs, flops, scratch=()):
     size = sum(math.prod(a.shape) * a.dtype.itemsize for a in args)
     size += sum(math.prod(o.shape) * o.dtype.itemsize for o in outs)
+    grant = 64 * MIB - (128 << 10) if kernel in (join_kernel, step_kernel) else 62 * MIB
     return pl.pallas_call(
         kernel,
         out_shape=outs,
@@ -40,7 +41,7 @@
             out_specs=[whole(o.shape) for o in outs],
             scratch_shapes=scratch,
         ),
-        compiler_params=pltpu.CompilerParams(vmem_limit_bytes=64 * MIB - (128 << 10)),
+        compiler_params=pltpu.CompilerParams(vmem_limit_bytes=grant),
         cost_estimate=pl.CostEstimate(flops=flops, bytes_accessed=size, transcendentals=0),
     )(*([] if place is None else [place]), *args)
 

time: 116 us -> 116 us (level)
  waiting for transfers between devices: 30.9 us -> 33.7 us
  other arithmetic: 3.96 us -> 1.43 us
  starting transfers between devices: 41.7 us -> 43.1 us
    convert_element_type x5, other arithmetic: 3.37 us -> 0.82 us  [add_pair(): return (part[0].astype(F32) + part[1].astype(F32)).astype(BF16)]
    all_gather x1, waiting for transfers between devices: 1.66 us -> 4.01 us  [body(): both = lax.all_gather(packed, 'y', axis=0, tiled=False)]
    ppermute x1, waiting for transfers between devices: 2.81 us -> 4.9 us  [body(): returned = lax.ppermute(to_return, 'zl', PAIR)]
    ppermute x4, waiting for transfers between devices: 23 us -> 21.3 us  [ring_step(): return add_pair((total, lax.ppermute(total, axis, ring_shift(4, k))))]
    ppermute x4, starting transfers between devices: 16.5 us -> 18 us  [ring_step(): return add_pair((total, lax.ppermute(total, axis, ring_shift(4, k))))]
  transfers between devices with their start and end apart: 11 -> 11, of which waited for: 7 -> 7; matrix products, arithmetic and copies ran while one was open for 4% -> 1% of each run, Pallas kernels for 15% -> 15%
where the time goes in v8:
time: 116 us; the launch traced here: 115 us
  starting transfers between devices  43.1 us (37%)
  waiting for transfers between devices  33.7 us (29%)
  Pallas kernels  22.7 us (20%)
  between operations  14.2 us (12%)
  other arithmetic  1.43 us (1%)
    pallas_call x7, Pallas kernels, call(): pl.pallas_call(kernel, out_shape=outs, grid_spec=pltpu.PrefetchScalarGrid...  22.7 us
    ppermute x4, waiting for transfers between devices, ring_step(): return add_pair((total, lax.ppermute(total, axis, ring_shift(4, k))))  21.3 us
    ppermute x4, starting transfers between devices, ring_step(): return add_pair((total, lax.ppermute(total, axis, ring_shift(4, k))))  18 us
    all_to_all x1, starting transfers between devices, body(): slab = lax.all_to_all(blocks, 'y', 0, 0, tiled=True)  7.78 us
    ppermute x1, waiting for transfers between devices, body(): returned = lax.ppermute(to_return, 'zl', PAIR)  4.9 us
    ppermute x1, starting transfers between devices, core_sum(): lax.ppermute(lax.dynamic_slice_in_dim(packed, (1 - core) * n, n), 'core',...  4.71 us
    all_gather x1, waiting for transfers between devices, body(): both = lax.all_gather(packed, 'y', axis=0, tiled=False)  4.01 us
    ppermute x1, starting transfers between devices, body(): returned = lax.ppermute(to_return, 'zl', PAIR)  4 us
  transfers between devices with their start and end apart: 11, of which 7 were waited for; matrix products, arithmetic and copies ran while one was open for 1% of the time, Pallas kernels for 15%

profile of v8, /device:TPU:1, one launch (start us, length us, event | category | flops | bytes accessed | tf_op | source)
XLA Modules:
  0.0 115.1 jit_solution(4706312903072636684)
XLA Ops:
  7.2 1.8 %shard_map.110 = bf16[384,512]{1,0:T(8,128)(2,1)} custom-call(f32[256,512]{1,0:T(8,128)} %bitcast.18, bf16[128,512]{1,0:T(8,128)(2,1)} %cot.5), custom_call_target="tpu_custom_call" | custom-call | bytes 1048576 | tf_op jit(solution)/shard_map/pallas_call | solution.py:34
  9.1 2.2 %shard_map.112 = bf16[8,128,512]{2,1,0:T(8,128)(2,1)} custom-call(bf16[128,4096]{1,0:T(8,128)(2,1)} %refs_3_.5, bf16[128,4096]{1,0:T(8,128)(2,1)} %refs_3_.5, bf16[128,4096]{1,0:T(8,128)(2,1)} %refs_3_.5, bf16[128,4096]{1,0:T(8,128)(2,1)} %refs_3_.5), custom_call_target="tpu_custom_call" | custom-call | bytes 5242880 | tf_op jit(solution)/shard_map/pallas_call | solution.py:34
  11.3 7.8 %all-to-all-start = ((bf16[8,128,512]{2,1,0:T(8,128)(2,1)}), bf16[8,128,512]{2,1,0:T(8,128)(2,1)S(1)}, u32[]{:S(2)}, u32[]{:S(2)}) async-start(bf16[8,128,512]{2,1,0:T(8,128)(2,1)} %shard_map.112), calls=%async_computation | async-start | bytes 2097152 | tf_op jit(solution)/shard_map/all_to_all | solution.py:181
  19.7 2.8 %shard_map.111 = bf16[128,2560]{1,0:T(8,128)(2,1)} custom-call(s32[3]{0:T(128)} %pad_add_fusion.place, bf16[128,512]{1,0:T(8,128)(2,1)} %cot.5, bf16[128,4096]{1,0:T(8,128)(2,1)} %refs_3_.5, bf16[128,4096]{1,0:T(8,128)(2,1)} %refs_3_.5, bf16[128,4096]{1,0:T(8,128)(2,1)} %refs_3_.5, bf16[128,4096]{1,0:T(8,128)(2,1)} %refs_3_.5), custom_call_target="tpu_custom_call" | custom-call | bytes 4980736 | tf_op jit(solution)/shard_map/pallas_call | solution.py:34
  22.5 4.7 %collective-permute-start = (bf16[128,512]{1,0:T(8,128)(2,1)S(1)}, bf16[128,512]{1,0:T(8,128)(2,1)S(1)}, u32[]{:S(2)}, u32[]{:S(2)}) collective-permute-start(bf16[128,512]{1,0:T(8,128)(2,1)S(1)} %constant_dynamic-slice_fusion), channel_id=1, source_target_pairs={{0,16},{16,0},{1,17},{17,1},{2,18},{18,2},{3,19},{19,3},{4,20},{20... | collective-permute-start | bytes 393224 | tf_op jit(solution)/shard_map/ppermute | solution.py:151
  27.3 1.0 collective-permute-done
  28.3 2.8 %collective-permute-start.1 = (bf16[128,512]{1,0:T(8,128)(2,1)S(1)}, bf16[128,512]{1,0:T(8,128)(2,1)S(1)}, u32[]{:S(2)}, u32[]{:S(2)}) collective-permute-start(bf16[128,512]{1,0:T(8,128)(2,1)S(1)} %add_convert_fusion.4), channel_id=1, source_target_pairs={{0,64},{32,96},{64,0},{96,32},{1,65},{33,97},{65,1},{97,33},{2,66}... | collective-permute-start | bytes 393224 | tf_op jit(solution)/shard_map/ppermute | solution.py:144
  31.1 5.3 %collective-permute-done.1 = bf16[128,512]{1,0:T(8,128)(2,1)S(1)} collective-permute-done((bf16[128,512]{1,0:T(8,128)(2,1)S(1)}, bf16[128,512]{1,0:T(8,128)(2,1)S(1)}, u32[]{:S(2)}, u32[]{:S(2)}) %collective-permute-start.1) | collective-permute-done | bytes 131104 | tf_op jit(solution)/shard_map/ppermute | solution.py:144
  36.4 1.9 %collective-permute-start.2 = (bf16[128,512]{1,0:T(8,128)(2,1)S(1)}, bf16[128,512]{1,0:T(8,128)(2,1)S(1)}, u32[]{:S(2)}, u32[]{:S(2)}) collective-permute-start(bf16[128,512]{1,0:T(8,128)(2,1)S(1)} %add_convert_fusion.3), channel_id=1, source_target_pairs={{0,32},{32,64},{64,96},{96,0},{1,33},{33,65},{65,97},{97,1},{2,34}... | collective-permute-start | bytes 393224 | tf_op jit(solution)/shard_map/ppermute | solution.py:144
  38.4 3.5 %collective-permute-start.6 = (bf16[128,2560]{1,0:T(8,128)(2,1)}, bf16[128,2560]{1,0:T(8,128)(2,1)S(1)}, u32[]{:S(2)}, u32[]{:S(2)}) collective-permute-start(bf16[128,2560]{1,0:T(8,128)(2,1)} %shard_map.111), channel_id=1, source_target_pairs={{0,1},{1,0},{2,3},{3,2},{4,5},{5,4},{6,7},{7,6},{8,9},{9,8},{10,11... | collective-permute-start | bytes 1966088 | tf_op jit(solution)/shard_map/ppermute | solution.py:178
  41.8 1.9 %collective-permute-done.2 = bf16[128,512]{1,0:T(8,128)(2,1)S(1)} collective-permute-done((bf16[128,512]{1,0:T(8,128)(2,1)S(1)}, bf16[128,512]{1,0:T(8,128)(2,1)S(1)}, u32[]{:S(2)}, u32[]{:S(2)}) %collective-permute-start.2) | collective-permute-done | bytes 131104 | tf_op jit(solution)/shard_map/ppermute | solution.py:144
  43.8 8.8 %collective-permute-start.3 = (bf16[128,512]{1,0:T(8,128)(2,1)S(1)}, bf16[128,512]{1,0:T(8,128)(2,1)S(1)}, u32[]{:S(2)}, u32[]{:S(2)}) collective-permute-start(bf16[128,512]{1,0:T(8,128)(2,1)S(1)} %add_convert_fusion.2), channel_id=1, source_target_pairs={{0,256},{128,384},{256,0},{384,128},{1,257},{129,385},{257,1},{385... | collective-permute-start | bytes 393224 | tf_op jit(solution)/shard_map/ppermute | solution.py:144
  52.6 14.1 %collective-permute-done.3 = bf16[128,512]{1,0:T(8,128)(2,1)S(1)} collective-permute-done((bf16[128,512]{1,0:T(8,128)(2,1)S(1)}, bf16[128,512]{1,0:T(8,128)(2,1)S(1)}, u32[]{:S(2)}, u32[]{:S(2)}) %collective-permute-start.3) | collective-permute-done | bytes 131104 | tf_op jit(solution)/shard_map/ppermute | solution.py:144
  66.7 4.5 %collective-permute-start.4 = (bf16[128,512]{1,0:T(8,128)(2,1)S(1)}, bf16[128,512]{1,0:T(8,128)(2,1)S(1)}, u32[]{:S(2)}, u32[]{:S(2)}) collective-permute-start(bf16[128,512]{1,0:T(8,128)(2,1)S(1)} %add_convert_fusion.1), channel_id=1, source_target_pairs={{0,128},{128,256},{256,384},{384,0},{1,129},{129,257},{257,385},{3... | collective-permute-start | bytes 393224 | tf_op jit(solution)/shard_map/ppermute | solution.py:144
  71.2 4.0 %all-gather.3.cloned.1.call-done = bf16[3072,512]{1,0:T(8,128)(2,1)} async-done(((bf16[384,512]{1,0:T(8,128)(2,1)}), bf16[3072,512]{1,0:T(8,128)(2,1)}) %all-gather.3.cloned.1.call-update) | async-done | bytes 3145744 | tf_op jit(solution)/shard_map/all_gather | solution.py:173
  75.3 5.1 %shard_map.114 = (bf16[128,2048]{1,0:T(8,128)(2,1)}, f32[128,512]{1,0:T(8,128)}, bf16[128,2560]{1,0:T(8,128)(2,1)}) custom-call(s32[3]{0:T(128)} %pad_add_fusion.place, bf16[128,512]{1,0:T(8,128)(2,1)} %cot.5, bf16[128,4096]{1,0:T(8,128)(2,1)} %refs_3_.5, bf16[128,4096]{1,0:T(8,128)(2,1)} %refs_3_.5, bf16[128,4096]{1,0:T(8,128)(2,1)} %refs_3_.5, ...), custom_call_target="tpu_custom_call" | custom-call | flops 1073741824 | bytes 21626880 | tf_op jit(solution)/shard_map/pallas_call | solution.py:34
  80.3 4.0 %collective-permute-start.7 = (bf16[128,2560]{1,0:T(8,128)(2,1)}, bf16[128,2560]{1,0:T(8,128)(2,1)}, u32[]{:S(2)}, u32[]{:S(2)}) collective-permute-start(bf16[128,2560]{1,0:T(8,128)(2,1)} %get-tuple-element.33), channel_id=1, source_target_pairs={{0,1},{1,0},{2,3},{3,2},{4,5},{5,4},{6,7},{7,6},{8,9},{9,8},{10,11... | collective-permute-start | bytes 1966088 | tf_op jit(solution)/shard_map/ppermute | solution.py:193
  85.0 3.7 %shard_map.113 = (f32[256,512]{1,0:T(8,128)}, bf16[256,512]{1,0:T(8,128)(2,1)}) custom-call(s32[3]{0:T(128)} %pad_add_fusion.place, bf16[8,128,512]{2,1,0:T(8,128)(2,1)} %copy-done, bf16[8,128,512]{2,1,0:T(8,128)(2,1)} %copy-done, bf16[8,128,512]{2,1,0:T(8,128)(2,1)} %copy-done, bf16[8,128,512]{2,1,0:T(8,128)(2,1)} %copy-done, ...), custom_call_target="tpu_custom_call" | custom-call | flops 536870912 | bytes 17563648 | tf_op jit(solution)/shard_map/pallas_call | solution.py:34
  88.8 1.9 %collective-permute-start.5 = (bf16[256,512]{1,0:T(8,128)(2,1)}, bf16[256,512]{1,0:T(8,128)(2,1)}, u32[]{:S(2)}, u32[]{:S(2)}) collective-permute-start(bf16[256,512]{1,0:T(8,128)(2,1)} %get-tuple-element.30), channel_id=1, source_target_pairs={{0,1},{1,0},{2,3},{3,2},{4,5},{5,4},{6,7},{7,6},{8,9},{9,8},{10,11... | collective-permute-start | bytes 786440 | tf_op jit(solution)/shard_map/ppermute | solution.py:199
  90.7 3.2 %collective-permute-start.8 = (bf16[128,512]{1,0:T(8,128)(2,1)}, bf16[128,512]{1,0:T(8,128)(2,1)}, u32[]{:S(2)}, u32[]{:S(2)}) collective-permute-start(bf16[128,512]{1,0:T(8,128)(2,1)} %add_convert_fusion.half_sum), channel_id=1, source_target_pairs={{0,16},{16,0},{1,17},{17,1},{2,18},{18,2},{3,19},{19,3},{4,20},{20... | collective-permute-start | bytes 393224 | tf_op jit(solution)/shard_map/ppermute | solution.py:200
  93.9 4.9 %collective-permute-done.7.returned = bf16[128,2560]{1,0:T(8,128)(2,1)} collective-permute-done((bf16[128,2560]{1,0:T(8,128)(2,1)}, bf16[128,2560]{1,0:T(8,128)(2,1)}, u32[]{:S(2)}, u32[]{:S(2)}) %collective-permute-start.7) | collective-permute-done | bytes 655392 | tf_op jit(solution)/shard_map/ppermute | solution.py:193
  98.8 3.1 %shard_map.115 = (bf16[128,512]{1,0:T(8,128)(2,1)}, bf16[128,4096]{1,0:T(8,128)(2,1)}) custom-call(s32[3]{0:T(128)} %pad_add_fusion.place, bf16[128,2048]{1,0:T(8,128)(2,1)} %get-tuple-element.31.own, f32[128,512]{1,0:T(8,128)} %get-tuple-element.32.ahead, bf16[128,2560]{1,0:T(8,128)(2,1)} %collective-permute-done.7.returned), custom_call_target="tpu_custom_call" | custom-call | bytes 2621440 | tf_op jit(solution)/shard_map/pallas_call | solution.py:34
  101.9 2.5 %collective-permute-done.5.sent = bf16[256,512]{1,0:T(8,128)(2,1)} collective-permute-done((bf16[256,512]{1,0:T(8,128)(2,1)}, bf16[256,512]{1,0:T(8,128)(2,1)}, u32[]{:S(2)}, u32[]{:S(2)}) %collective-permute-start.5) | collective-permute-done | bytes 262176 | tf_op jit(solution)/shard_map/ppermute | solution.py:199
  104.4 3.9 %shard_map.116 = (f32[256,512]{1,0:T(8,128)}, bf16[256,512]{1,0:T(8,128)(2,1)}, bf16[256,512]{1,0:T(8,128)(2,1)}) custom-call(s32[3]{0:T(128)} %pad_add_fusion.place, f32[256,512]{1,0:T(8,128)} %get-tuple-element.37.keep, bf16[256,512]{1,0:T(8,128)(2,1)} %collective-permute-done.5.sent, f32[256,512]{1,0:T(8,128)} %bitcast.19, bf16[256,512]{1,0:T(8,128)(2,1)} %bitcast.20, ...), custom_call_target="tpu_custom_call" | custom-call | flops 5242880 | bytes 3670016 | tf_op jit(solution)/shard_map/pallas_call | solution.py:34
  (19 shorter events, 1.5 us)
Async XLA Ops:
  7.2 68.1 %all-gather.3.cloned.1.call-start = ((), (), s32[]{:S(2)}) async-start(), calls=%async_computation.1 | async-start | bytes 3538944 | tf_op jit(solution)/shard_map/all_gather | solution.py:173
  11.3 11.2 %copy-start.2 = (bf16[384,512]{1,0:T(8,128)(2,1)S(1)}, bf16[384,512]{1,0:T(8,128)(2,1)}, u32[]{:S(2)}) copy-start(bf16[384,512]{1,0:T(8,128)(2,1)} %shard_map.110) | copy-start | bytes 1179652
  11.3 55.4 %all-to-all-start = ((bf16[8,128,512]{2,1,0:T(8,128)(2,1)}), bf16[8,128,512]{2,1,0:T(8,128)(2,1)S(1)}, u32[]{:S(2)}, u32[]{:S(2)}) async-start(bf16[8,128,512]{2,1,0:T(8,128)(2,1)} %shard_map.112), calls=%async_computation | async-start | bytes 2097152 | tf_op jit(solution)/shard_map/all_to_all | solution.py:181
  22.5 5.7 %collective-permute-start = (bf16[128,512]{1,0:T(8,128)(2,1)S(1)}, bf16[128,512]{1,0:T(8,128)(2,1)S(1)}, u32[]{:S(2)}, u32[]{:S(2)}) collective-permute-start(bf16[128,512]{1,0:T(8,128)(2,1)S(1)} %constant_dynamic-slice_fusion), channel_id=1, source_target_pairs={{0,16},{16,0},{1,17},{17,1},{2,18},{18,2},{3,19},{19,3},{4,20},{20... | collective-permute-start | bytes 393224 | tf_op jit(solution)/shard_map/ppermute | solution.py:151
  28.3 8.1 %collective-permute-start.1 = (bf16[128,512]{1,0:T(8,128)(2,1)S(1)}, bf16[128,512]{1,0:T(8,128)(2,1)S(1)}, u32[]{:S(2)}, u32[]{:S(2)}) collective-permute-start(bf16[128,512]{1,0:T(8,128)(2,1)S(1)} %add_convert_fusion.4), channel_id=1, source_target_pairs={{0,64},{32,96},{64,0},{96,32},{1,65},{33,97},{65,1},{97,33},{2,66}... | collective-permute-start | bytes 393224 | tf_op jit(solution)/shard_map/ppermute | solution.py:144
  36.4 7.3 %collective-permute-start.2 = (bf16[128,512]{1,0:T(8,128)(2,1)S(1)}, bf16[128,512]{1,0:T(8,128)(2,1)S(1)}, u32[]{:S(2)}, u32[]{:S(2)}) collective-permute-start(bf16[128,512]{1,0:T(8,128)(2,1)S(1)} %add_convert_fusion.3), channel_id=1, source_target_pairs={{0,32},{32,64},{64,96},{96,0},{1,33},{33,65},{65,97},{97,1},{2,34}... | collective-permute-start | bytes 393224 | tf_op jit(solution)/shard_map/ppermute | solution.py:144
  38.4 32.9 %collective-permute-start.6 = (bf16[128,2560]{1,0:T(8,128)(2,1)}, bf16[128,2560]{1,0:T(8,128)(2,1)S(1)}, u32[]{:S(2)}, u32[]{:S(2)}) collective-permute-start(bf16[128,2560]{1,0:T(8,128)(2,1)} %shard_map.111), channel_id=1, source_target_pairs={{0,1},{1,0},{2,3},{3,2},{4,5},{5,4},{6,7},{7,6},{8,9},{9,8},{10,11... | collective-permute-start | bytes 1966088 | tf_op jit(solution)/shard_map/ppermute | solution.py:178
  43.8 22.9 %collective-permute-start.3 = (bf16[128,512]{1,0:T(8,128)(2,1)S(1)}, bf16[128,512]{1,0:T(8,128)(2,1)S(1)}, u32[]{:S(2)}, u32[]{:S(2)}) collective-permute-start(bf16[128,512]{1,0:T(8,128)(2,1)S(1)} %add_convert_fusion.2), channel_id=1, source_target_pairs={{0,256},{128,384},{256,0},{384,128},{1,257},{129,385},{257,1},{385... | collective-permute-start | bytes 393224 | tf_op jit(solution)/shard_map/ppermute | solution.py:144
  66.7 13.6 %copy-start = (bf16[8,128,512]{2,1,0:T(8,128)(2,1)}, bf16[8,128,512]{2,1,0:T(8,128)(2,1)S(1)}, u32[]{:S(2)}) copy-start(bf16[8,128,512]{2,1,0:T(8,128)(2,1)S(1)} %all-to-all-done.refs_0_.refs_1_.refs_2_.refs_3_) | copy-start | bytes 3145732
  66.7 17.6 %collective-permute-start.4 = (bf16[128,512]{1,0:T(8,128)(2,1)S(1)}, bf16[128,512]{1,0:T(8,128)(2,1)S(1)}, u32[]{:S(2)}, u32[]{:S(2)}) collective-permute-start(bf16[128,512]{1,0:T(8,128)(2,1)S(1)} %add_convert_fusion.1), channel_id=1, source_target_pairs={{0,128},{128,256},{256,384},{384,0},{1,129},{129,257},{257,385},{3... | collective-permute-start | bytes 393224 | tf_op jit(solution)/shard_map/ppermute | solution.py:144
  71.2 4.0 %copy-start.1 = (bf16[128,2560]{1,0:T(8,128)(2,1)}, bf16[128,2560]{1,0:T(8,128)(2,1)S(1)}, u32[]{:S(2)}) copy-start(bf16[128,2560]{1,0:T(8,128)(2,1)S(1)} %collective-permute-done.6.refs_4_.refs_5_.refs_6_.refs_7_.refs_8_) | copy-start | bytes 1966084
  80.3 18.4 %collective-permute-start.7 = (bf16[128,2560]{1,0:T(8,128)(2,1)}, bf16[128,2560]{1,0:T(8,128)(2,1)}, u32[]{:S(2)}, u32[]{:S(2)}) collective-permute-start(bf16[128,2560]{1,0:T(8,128)(2,1)} %get-tuple-element.33), channel_id=1, source_target_pairs={{0,1},{1,0},{2,3},{3,2},{4,5},{5,4},{6,7},{7,6},{8,9},{9,8},{10,11... | collective-permute-start | bytes 1966088 | tf_op jit(solution)/shard_map/ppermute | solution.py:193
  88.8 15.6 %collective-permute-start.5 = (bf16[256,512]{1,0:T(8,128)(2,1)}, bf16[256,512]{1,0:T(8,128)(2,1)}, u32[]{:S(2)}, u32[]{:S(2)}) collective-permute-start(bf16[256,512]{1,0:T(8,128)(2,1)} %get-tuple-element.30), channel_id=1, source_target_pairs={{0,1},{1,0},{2,3},{3,2},{4,5},{5,4},{6,7},{7,6},{8,9},{9,8},{10,11... | collective-permute-start | bytes 786440 | tf_op jit(solution)/shard_map/ppermute | solution.py:199
  90.7 13.7 %collective-permute-start.8 = (bf16[128,512]{1,0:T(8,128)(2,1)}, bf16[128,512]{1,0:T(8,128)(2,1)}, u32[]{:S(2)}, u32[]{:S(2)}) collective-permute-start(bf16[128,512]{1,0:T(8,128)(2,1)} %add_convert_fusion.half_sum), channel_id=1, source_target_pairs={{0,16},{16,0},{1,17},{17,1},{2,18},{18,2},{3,19},{19,3},{4,20},{20... | collective-permute-start | bytes 393224 | tf_op jit(solution)/shard_map/ppermute | solution.py:200
Sparse Core Ops, SparseCore 0:
  10.7 64.5 all-gather.2
